TPU v7x, 32 devices: a whole 2x2x4 slice. The times are simulated.
32 devices in a mesh: roll: 16 (over z, y, core), trans: 2 (over x).
Axes of the slice: x: 2, y: 2, z: 4, core: 2. Of those that a mesh axis runs over, the one named last changes fastest.
Arguments:
- adjoint: float32 [4, 2, 32, 128, 256], P(None, None, None, 'roll', 'trans'), may hold values from -6 to 6
- source: float32 [4, 2, 32, 128, 256], P(None, None, None, 'roll', 'trans'), may hold values from -6 to 6
- pressure: float32 [2, 128, 256], P(None, 'roll', 'trans'), may hold values from -4 to 4
- film: float32 [128, 256], P('roll', 'trans'), may hold values from 0.6 to 1.4
- cavity: int32 [2, 128, 256], P(None, 'roll', 'trans'), may hold values 0 or 1
- temp_index: int32 [2], replicated, may hold values from 0 to 7
Outputs:
- adjoint_out: float32 [4, 2, 32, 128, 256], P(None, None, None, 'roll', 'trans')
- wall_step: float32 [128, 256], P('roll', 'trans')
All inputs are finite; a program needn't handle non-finite values. No bound on the sum of `cavity` on one device may be relied on, other than what follows from the above.
Results may differ from a plain program's by a relative error of at most 0.00002.
Values sent between devices are 32-bit elements; how exact they have to be, the bound alone decides.
No kernel may reach another device: no remote copies, remote signals or barrier semaphores. Data moves between devices by JAX's collectives and lax.ppermute only.
A program may use at most 64 MiB of HBM per device.

v0:
```python
import jax
import jax.numpy as jnp
from jax import lax
from jax.sharding import PartitionSpec as P

SECTIONS = 2


VISCOSITY_PRESS = 0.3
VISCOSITY_TEMP = 0.5
THETA_STEP = 0.2
SOUND = 0.5
KAPPA = 0.6
HEATING = 0.3
ROLL_SPEED = 1.0
COURANT = 0.8


def extended(array, sides, width):
    for axis, dim in sides:
        size, length = (lax.axis_size(axis), array.shape[dim])
        up = [(i, (i + 1) % size) for i in range(size - 1)]
        down = [(j, i) for i, j in up]
        last = lax.slice_in_dim(array, length - width, length, axis=dim)
        leading = lax.slice_in_dim(array, 0, width, axis=dim)
        before = lax.ppermute(last, axis, up)
        after = lax.ppermute(leading, axis, down)
        array = jnp.concatenate([before, array, after], axis=dim)
    return array


def coefficients(pressure, film, cavity, temp_index):
    implicit_weight = THETA_STEP * temp_index.astype(jnp.float32)
    fluid_viscosity = jnp.exp(
        VISCOSITY_PRESS * pressure - VISCOSITY_TEMP * implicit_weight[:, None, None]
    )
    film_coef = 4.0 * fluid_viscosity / (film * film)
    density = 1.0 - 0.6 * cavity.astype(jnp.float32)
    pseudo_step = COURANT / (32.0 / 3.0 * fluid_viscosity + 4.0 * film_coef + 2.0 * SOUND + 1.0)
    return jnp.stack([fluid_viscosity, film_coef, density, pseudo_step])


def time_section(padded, source, coeffs):
    depth = source.shape[-3]
    width_x = source.shape[-2]
    width_y = source.shape[-1]

    def along_x(offset):
        return padded[..., 2 + offset : 2 + offset + width_x, 2 : 2 + width_y]

    def along_y(offset):
        return padded[..., 2 : 2 + width_x, 2 + offset : 2 + offset + width_y]

    center = along_x(0)
    second_x = (
        -along_x(2) + 16.0 * along_x(1) - 30.0 * center + 16.0 * along_x(-1) - along_x(-2)
    ) / 12.0
    second_y = (
        -along_y(2) + 16.0 * along_y(1) - 30.0 * center + 16.0 * along_y(-1) - along_y(-2)
    ) / 12.0
    first_x = (-along_x(2) + 8.0 * along_x(1) - 8.0 * along_x(-1) + along_x(-2)) / 12.0
    first_y = (-along_y(2) + 8.0 * along_y(1) - 8.0 * along_y(-1) + along_y(-2)) / 12.0
    layered = jnp.pad(center, ((0, 0), (0, 0), (1, 1), (0, 0), (0, 0)))
    second_z = layered[:, :, 2:] - 2.0 * center + layered[:, :, :-2]
    fluid_viscosity = coeffs[0][:, None]
    film_coef = coeffs[1][:, None]
    density = coeffs[2][:, None]
    pseudo_step = coeffs[3][:, None]
    film_height = ((jnp.arange(depth).astype(jnp.float32) + 0.5) / depth)[:, None, None]
    diffused = fluid_viscosity * (second_x + second_y) + film_coef * second_z
    carried = density * ROLL_SPEED * film_height * first_x
    resid_density = 0.5 * diffused[0] + carried[0] + SOUND * (first_x[1] + first_y[2])
    resid_along = diffused[1] + carried[1] + SOUND * first_x[0]
    resid_across = diffused[2] + carried[2] + SOUND * first_y[0]
    resid_energy = KAPPA * diffused[3] + carried[3] + HEATING * fluid_viscosity * center[1]
    residual = jnp.stack([resid_density, resid_along, resid_across, resid_energy])
    return center + pseudo_step * (residual + source)


def wall_terms(padded_mean, momentum, coeffs, film):
    width_x = momentum.shape[-2]
    depth = momentum.shape[-3]
    slope = (
        -padded_mean[:, 4 : 4 + width_x]
        + 8.0 * padded_mean[:, 3 : 3 + width_x]
        - 8.0 * padded_mean[:, 1 : 1 + width_x]
        + padded_mean[:, 0:width_x]
    ) / 12.0
    layered = jnp.pad(momentum, ((0, 0), (1, 1), (0, 0), (0, 0)))
    bending = layered[:, 2:] - 2.0 * momentum + layered[:, :-2]
    curvature = jnp.sum(momentum * bending, axis=1) / depth
    flux = coeffs[2] * ROLL_SPEED * film / 2.0
    return flux * slope - 8.0 * coeffs[0] / (film * film * film) * curvature


def on_device(adjoint, source, pressure, film, cavity, temp_index):
    coeffs = coefficients(pressure, film, cavity, temp_index)
    depth = adjoint.shape[2]
    state = adjoint
    for section_index in range(SECTIONS):
        padded = extended(state, (("roll", 3), ("trans", 4)), 2)
        state = time_section(padded, source, coeffs)
    mean_density = jnp.sum(state[0], axis=1) / depth
    padded_mean = extended(mean_density, (("roll", 1),), 2)
    terms = wall_terms(padded_mean, state[1], coeffs, film)
    wall_grad = jnp.sum(terms, axis=0)
    total = lax.psum(jnp.sum(wall_grad * wall_grad), ("roll", "trans"))
    cell_count = (
        wall_grad.shape[0] * wall_grad.shape[1] * lax.axis_size("roll") * lax.axis_size("trans")
    )
    wall_step = wall_grad / jnp.sqrt(total / cell_count + 1e-06)
    return (state, wall_step)


def solution(mesh):
    placed = (
        P(None, None, None, "roll", "trans"),
        P(None, None, None, "roll", "trans"),
        P(None, "roll", "trans"),
        P("roll", "trans"),
        P(None, "roll", "trans"),
        P(),
    )
    return jax.shard_map(
        on_device,
        mesh=mesh,
        in_specs=placed,
        out_specs=(P(None, None, None, "roll", "trans"), P("roll", "trans")),
        check_vma=False,
    )
```

profile of v0, /device:TPU:0, one launch (start us, length us, event | category | flops | bytes accessed | tf_op | source)
XLA Modules:
  0.0 144.6 jit_solution(17224806247778329687)
XLA Ops:
  0.7 1.5 %copy.205 = f32[4,2,32,8,128]{4,2,3,1,0:T(8,128)S(1)} copy(f32[4,2,32,8,128]{4,3,2,1,0:T(8,128)} %param.6) | data formatting | bytes 2097152 | tf_op args[0]
  2.9 3.1 %collective-permute-start.1 = (f32[4,2,32,2,128]{4,2,3,1,0:T(8,128)S(1)}, f32[4,2,32,2,128]{4,2,3,1,0:T(8,128)}, u32[]{:S(2)}, u32[]{:S(2)}) collective-permute-start(f32[4,2,32,2,128]{4,2,3,1,0:T(8,128)S(1)} %get-tuple-element.33), channel_id=1, source_target_pairs={{0,2},{2,4},{4,6},{6,8},{8,10},{10,12},{12,14},{14,16},{16,18},{18... | collective-permute-start | bytes 786440 | tf_op jit(solution)/shard_map/ppermute | solution.py:26
  8.6 2.7 %copy.195 = f32[4,2,32,8,128]{2,3,4,1,0:T(8,128)} copy(f32[4,2,32,8,128]{4,3,2,1,0:T(8,128)S(1)} %copy-done.1) | data formatting | bytes 2097152 | tf_op args[0]
  12.1 1.4 copy.194
  14.9 3.7 %pad_maximum_fusion = f32[4,2,32,12,128]{2,3,4,1,0:T(8,128)S(1)} fusion(f32[4,2,32,2,128]{2,3,4,1,0:T(2,128)} %copy.196, f32[4,2,32,8,128]{2,3,4,1,0:T(8,128)} %copy.195, f32[4,2,32,2,128]{2,3,4,1,0:T(2,128)S(1)} %copy.194), kind=kLoop, calls=%fused_computation | loop fusion | flops 786432 | bytes 3145728 | tf_op jit(solution)/shard_map/concatenate | solution.py:28
  20.6 6.2 %collective-permute-start.3 = (f32[4,2,32,12,2]{2,3,4,1,0:T(8,128)S(1)}, f32[4,2,32,12,2]{2,3,4,1,0:T(8,128)}, u32[]{:S(2)}, u32[]{:S(2)}) collective-permute-start(f32[4,2,32,12,2]{2,3,4,1,0:T(8,128)S(1)} %get-tuple-element.16), channel_id=1, source_target_pairs={{0,1},{2,3},{4,5},{6,7},{8,9},{10,11},{12,13},{14,15},{16,17},{18,... | collective-permute-start | bytes 73736 | tf_op jit(solution)/shard_map/ppermute | solution.py:26
  31.2 6.1 %copy.197 = f32[4,2,32,12,128]{4,2,3,1,0:T(8,128)} copy(f32[4,2,32,12,128]{2,3,4,1,0:T(8,128)} %copy-done) | data formatting | bytes 3145728 | tf_op jit(solution)/shard_map/concatenate | solution.py:28
  37.3 2.7 %copy.198 = f32[4,2,32,12,2]{4,2,3,1,0:T(8,128)} copy(f32[4,2,32,12,2]{2,3,4,1,0:T(8,128)} %collective-permute-done.2) | data formatting | bytes 49152 | tf_op jit(solution)/shard_map/ppermute | solution.py:27
  40.0 2.7 %copy.199 = f32[4,2,32,12,2]{4,2,3,1,0:T(8,128)} copy(f32[4,2,32,12,2]{2,3,4,1,0:T(8,128)} %collective-permute-done.3) | data formatting | bytes 49152 | tf_op jit(solution)/shard_map/ppermute | solution.py:26
  42.7 5.9 %add_multiply_fusion.1 = f32[4,2,32,8,128]{4,2,3,1,0:T(8,128)S(1)} fusion(f32[4,2,32,12,2]{4,2,3,1,0:T(8,128)} %copy.198, f32[4,2,32,12,128]{4,2,3,1,0:T(8,128)} %copy.197, f32[4,2,32,12,2]{4,2,3,1,0:T(8,128)} %copy.199), kind=kLoop, calls=%fused_computation.44 | loop fusion | flops 2883584 | bytes 2670592 | tf_op jit(solution)/shard_map/div | solution.py:62
  48.7 3.5 %fusion.6 = f32[4,2,32,8,128]{4,2,3,1,0:T(8,128)S(1)} fusion(f32[4,2,32,8,128]{4,2,3,1,0:T(8,128)S(1)} %copy.205, f32[4,2,32,10,128]{4,2,3,1,0:T(8,128)S(1)} %copy-done.3, f32[4,2,32,10,128]{4,2,3,1,0:T(8,128)S(1)} %constant_dynamic-update-slice_fusion, f32[2,8,128]{2,1,0:T(8,128)S(1)} %copy-done.18, f32[2,8,128]{2,1,0:T(8,128)S(1)} %copy-done.17, ...), kind=kLoop, calls=%fused_computation.16 | loop fusion | flops 6815744 | bytes 7929856 | tf_op jit(solution)/shard_map/add | solution.py:70
  55.2 4.2 %collective-permute-start.5 = (f32[4,2,32,2,128]{4,2,3,1,0:T(8,128)S(1)}, f32[4,2,32,2,128]{4,2,3,1,0:T(8,128)S(1)}, u32[]{:S(2)}, u32[]{:S(2)}) collective-permute-start(f32[4,2,32,2,128]{4,2,3,1,0:T(8,128)S(1)} %get-tuple-element.31), channel_id=1, source_target_pairs={{0,2},{2,4},{4,6},{6,8},{8,10},{10,12},{12,14},{14,16},{16,18},{18... | collective-permute-start | bytes 786440 | tf_op jit(solution)/shard_map/ppermute | solution.py:26
  60.7 2.2 %fusion.42 = (f32[4,2,32,12,2]{4,2,3,1,0:T(8,128)}, f32[4,2,32,12,2]{4,2,3,1,0:T(8,128)}) fusion(f32[4,2,32,12,128]{4,2,3,1,0:T(8,128)S(1)} %pad_maximum_fusion.1), kind=kLoop, calls=%fused_computation.124 | loop fusion | bytes 98304 | tf_op jit(solution)/shard_map/slice | solution.py:24
  62.9 2.2 %copy.218 = f32[4,2,32,12,2]{2,3,4,1,0:T(8,128)S(1)} copy(f32[4,2,32,12,2]{4,2,3,1,0:T(8,128)} %get-tuple-element.27) | data formatting | bytes 49152
  66.4 2.2 %copy.219 = f32[4,2,32,12,2]{2,3,4,1,0:T(8,128)S(1)} copy(f32[4,2,32,12,2]{4,2,3,1,0:T(8,128)} %get-tuple-element.26) | data formatting | bytes 49152
  68.6 4.9 %collective-permute-start.7 = (f32[4,2,32,12,2]{2,3,4,1,0:T(8,128)S(1)}, f32[4,2,32,12,2]{2,3,4,1,0:T(8,128)S(1)}, u32[]{:S(2)}, u32[]{:S(2)}) collective-permute-start(f32[4,2,32,12,2]{2,3,4,1,0:T(8,128)S(1)} %copy.219), channel_id=1, source_target_pairs={{0,1},{2,3},{4,5},{6,7},{8,9},{10,11},{12,13},{14,15},{16,17},{18,... | collective-permute-start | bytes 73736 | tf_op jit(solution)/shard_map/ppermute | solution.py:26
  73.5 1.3 broadcast_multiply_fusion.3
  74.9 1.8 %copy.207 = f32[4,2,32,12,2]{4,2,3,1,0:T(8,128)} copy(f32[4,2,32,12,2]{2,3,4,1,0:T(8,128)S(1)} %collective-permute-done.6) | data formatting | bytes 49152 | tf_op jit(solution)/shard_map/ppermute | solution.py:27
  76.8 1.8 %copy.209 = f32[4,2,32,12,2]{4,2,3,1,0:T(8,128)} copy(f32[4,2,32,12,2]{2,3,4,1,0:T(8,128)S(1)} %collective-permute-done.7) | data formatting | bytes 49152 | tf_op jit(solution)/shard_map/ppermute | solution.py:26
  78.6 4.0 %fusion.10 = f32[4,2,32,8,128]{4,2,3,1,0:T(8,128)S(1)} fusion(f32[4,2,32,8,128]{4,2,3,1,0:T(8,128)S(1)} %fusion.12, f32[4,2,32,2,128]{4,2,3,1,0:T(8,128)S(1)} %collective-permute-done.4, f32[4,2,32,2,128]{4,2,3,1,0:T(8,128)S(1)} %collective-permute-done.5, f32[2,8,128]{2,1,0:T(8,128)S(1)} %copy-done.18, f32[2,8,128]{2,1,0:T(8,128)S(1)} %copy-done.17, ...), kind=kLoop, calls=%fused_computation.20 | loop fusion | flops 9961472 | bytes 2686976 | tf_op jit(solution)/shard_map/add | solution.py:70
  82.7 2.0 %add_multiply_fusion = f32[4,2,32,8,128]{4,2,3,1,0:T(8,128)S(1)} fusion(f32[4,2,32,12,2]{4,2,3,1,0:T(8,128)S(1)} %copy-done.5, f32[4,2,32,2,128]{4,2,3,1,0:T(8,128)S(1)} %collective-permute-done.4, f32[4,2,32,8,128]{4,2,3,1,0:T(8,128)S(1)} %fusion.12, f32[4,2,32,2,128]{4,2,3,1,0:T(8,128)S(1)} %collective-permute-done.5, f32[4,2,32,12,2]{4,2,3,1,0:T(8,128)S(1)} %copy-done.6), kind=kLoop, calls=%fused_computation.42 | loop fusion | flops 4980736 | bytes 2670592 | tf_op jit(solution)/shard_map/div | solution.py:62
  87.7 8.3 %collective-permute-start.9 = (f32[2,2,128]{2,1,0:T(2,128)S(1)}, f32[2,2,128]{2,1,0:T(2,128)S(1)}, u32[]{:S(2)}, u32[]{:S(2)}) collective-permute-start(f32[2,2,128]{2,1,0:T(2,128)S(1)} %get-tuple-element.43), channel_id=1, source_target_pairs={{0,2},{2,4},{4,6},{6,8},{8,10},{10,12},{12,14},{14,16},{16,18},{18... | collective-permute-start | bytes 6152 | tf_op jit(solution)/shard_map/ppermute | solution.py:26
  97.5 1.6 %copy.215 = f32[4,2,32,8,128]{4,3,2,1,0:T(8,128)} copy(f32[4,2,32,8,128]{4,2,3,1,0:T(8,128)S(1)} %fusion.14) | data formatting | bytes 2097152
  99.1 44.2 %psum.7 = f32[]{:T(128)} all-reduce(f32[]{:T(128)} %multiply_reduce_fusion), channel_id=1, replica_groups=mesh['roll'=16,'trans'=2] {'roll','trans'}, use_global_device_ids=true, to_apply=%region_4.5 | all-reduce | flops 1 | bytes 8 | tf_op jit(solution)/shard_map/psum | solution.py:107
  (101 shorter events, 22.6 us)
Async XLA Ops:
  0.6 8.0 %copy-start.1 = (f32[4,2,32,8,128]{4,3,2,1,0:T(8,128)S(1)}, f32[4,2,32,8,128]{4,3,2,1,0:T(8,128)}, u32[]{:S(2)}) copy-start(f32[4,2,32,8,128]{4,3,2,1,0:T(8,128)} %param.6) | copy-start | bytes 3145732
  0.6 6.7 %copy-start.23 = (f32[8,128]{1,0:T(8,128)S(1)}, f32[8,128]{1,0:T(8,128)}, u32[]{:S(2)}) copy-start(f32[8,128]{1,0:T(8,128)} %param.9) | copy-start | bytes 12292
  0.7 7.3 %copy-start.28 = (s32[2]{0:T(128)S(1)}, s32[2]{0:T(128)}, u32[]{:S(2)}) copy-start(s32[2]{0:T(128)} %param.11) | copy-start | bytes 28
  0.7 7.2 %copy-start.19 = (s32[2,8,128]{2,1,0:T(8,128)S(1)}, s32[2,8,128]{2,1,0:T(8,128)}, u32[]{:S(2)}) copy-start(s32[2,8,128]{2,1,0:T(8,128)} %param.10) | copy-start | bytes 24580
  0.7 7.3 %copy-start.21 = (f32[2,8,128]{2,1,0:T(8,128)S(1)}, f32[2,8,128]{2,1,0:T(8,128)}, u32[]{:S(2)}) copy-start(f32[2,8,128]{2,1,0:T(8,128)} %param.8) | copy-start | bytes 24580
  2.9 9.2 %collective-permute-start.1 = (f32[4,2,32,2,128]{4,2,3,1,0:T(8,128)S(1)}, f32[4,2,32,2,128]{4,2,3,1,0:T(8,128)}, u32[]{:S(2)}, u32[]{:S(2)}) collective-permute-start(f32[4,2,32,2,128]{4,2,3,1,0:T(8,128)S(1)} %get-tuple-element.33), channel_id=1, source_target_pairs={{0,2},{2,4},{4,6},{6,8},{8,10},{10,12},{12,14},{14,16},{16,18},{18... | collective-permute-start | bytes 786440 | tf_op jit(solution)/shard_map/ppermute | solution.py:26
  6.0 7.6 %collective-permute-start = (f32[4,2,32,2,128]{4,2,3,1,0:T(8,128)}, f32[4,2,32,2,128]{4,2,3,1,0:T(8,128)S(1)}, u32[]{:S(2)}, u32[]{:S(2)}) collective-permute-start(f32[4,2,32,2,128]{4,2,3,1,0:T(8,128)} %get-tuple-element.32), channel_id=1, source_target_pairs={{2,0},{4,2},{6,4},{8,6},{10,8},{12,10},{14,12},{16,14},{18,16},{20... | collective-permute-start | bytes 786440 | tf_op jit(solution)/shard_map/ppermute | solution.py:27
  18.6 11.4 %copy-start = (f32[4,2,32,12,128]{2,3,4,1,0:T(8,128)}, f32[4,2,32,12,128]{2,3,4,1,0:T(8,128)S(1)}, u32[]{:S(2)}) copy-start(f32[4,2,32,12,128]{2,3,4,1,0:T(8,128)S(1)} %pad_maximum_fusion) | copy-start | bytes 4718596
  19.4 17.9 %collective-permute-start.2 = (f32[4,2,32,12,2]{2,3,4,1,0:T(8,128)}, f32[4,2,32,12,2]{2,3,4,1,0:T(8,128)}, u32[]{:S(2)}, u32[]{:S(2)}) collective-permute-start(f32[4,2,32,12,2]{2,3,4,1,0:T(8,128)} %get-tuple-element.17), channel_id=1, source_target_pairs={{1,0},{3,2},{5,4},{7,6},{9,8},{11,10},{13,12},{15,14},{17,16},{19,... | collective-permute-start | bytes 73736 | tf_op jit(solution)/shard_map/ppermute | solution.py:27
  20.6 19.3 %collective-permute-start.3 = (f32[4,2,32,12,2]{2,3,4,1,0:T(8,128)S(1)}, f32[4,2,32,12,2]{2,3,4,1,0:T(8,128)}, u32[]{:S(2)}, u32[]{:S(2)}) collective-permute-start(f32[4,2,32,12,2]{2,3,4,1,0:T(8,128)S(1)} %get-tuple-element.16), channel_id=1, source_target_pairs={{0,1},{2,3},{4,5},{6,7},{8,9},{10,11},{12,13},{14,15},{16,17},{18,... | collective-permute-start | bytes 73736 | tf_op jit(solution)/shard_map/ppermute | solution.py:26
  42.7 5.9 %copy-start.17 = (f32[2,8,128]{2,1,0:T(8,128)S(1)}, f32[2,8,128]{2,1,0:T(8,128)}, u32[]{:S(2)}) copy-start(f32[2,8,128]{2,1,0:T(8,128)} %get-tuple-element.37) | copy-start | bytes 24580
  42.7 5.9 %copy-start.18 = (f32[2,8,128]{2,1,0:T(8,128)S(1)}, f32[2,8,128]{2,1,0:T(8,128)}, u32[]{:S(2)}) copy-start(f32[2,8,128]{2,1,0:T(8,128)} %get-tuple-element.38) | copy-start | bytes 24580
  53.9 5.5 %collective-permute-start.4 = (f32[4,2,32,2,128]{4,2,3,1,0:T(8,128)S(1)}, f32[4,2,32,2,128]{4,2,3,1,0:T(8,128)S(1)}, u32[]{:S(2)}, u32[]{:S(2)}) collective-permute-start(f32[4,2,32,2,128]{4,2,3,1,0:T(8,128)S(1)} %get-tuple-element.30), channel_id=1, source_target_pairs={{2,0},{4,2},{6,4},{8,6},{10,8},{12,10},{14,12},{16,14},{18,16},{20... | collective-permute-start | bytes 786440 | tf_op jit(solution)/shard_map/ppermute | solution.py:27
  55.2 5.3 %collective-permute-start.5 = (f32[4,2,32,2,128]{4,2,3,1,0:T(8,128)S(1)}, f32[4,2,32,2,128]{4,2,3,1,0:T(8,128)S(1)}, u32[]{:S(2)}, u32[]{:S(2)}) collective-permute-start(f32[4,2,32,2,128]{4,2,3,1,0:T(8,128)S(1)} %get-tuple-element.31), channel_id=1, source_target_pairs={{0,2},{2,4},{4,6},{6,8},{8,10},{10,12},{12,14},{14,16},{16,18},{18... | collective-permute-start | bytes 786440 | tf_op jit(solution)/shard_map/ppermute | solution.py:26
  65.1 9.9 %collective-permute-start.6 = (f32[4,2,32,12,2]{2,3,4,1,0:T(8,128)S(1)}, f32[4,2,32,12,2]{2,3,4,1,0:T(8,128)S(1)}, u32[]{:S(2)}, u32[]{:S(2)}) collective-permute-start(f32[4,2,32,12,2]{2,3,4,1,0:T(8,128)S(1)} %copy.218), channel_id=1, source_target_pairs={{1,0},{3,2},{5,4},{7,6},{9,8},{11,10},{13,12},{15,14},{17,16},{19,... | collective-permute-start | bytes 73736 | tf_op jit(solution)/shard_map/ppermute | solution.py:27
  68.6 6.2 %copy-start.13 = (f32[2,32,8,128]{3,1,2,0:T(8,128)S(1)}, f32[2,32,8,128]{3,1,2,0:T(8,128)}, u32[]{:S(2)}) copy-start(f32[2,32,8,128]{3,1,2,0:T(8,128)} %multiply_multiply_fusion) | copy-start | bytes 786436
  68.6 8.2 %collective-permute-start.7 = (f32[4,2,32,12,2]{2,3,4,1,0:T(8,128)S(1)}, f32[4,2,32,12,2]{2,3,4,1,0:T(8,128)S(1)}, u32[]{:S(2)}, u32[]{:S(2)}) collective-permute-start(f32[4,2,32,12,2]{2,3,4,1,0:T(8,128)S(1)} %copy.219), channel_id=1, source_target_pairs={{0,1},{2,3},{4,5},{6,7},{8,9},{10,11},{12,13},{14,15},{16,17},{18,... | collective-permute-start | bytes 73736 | tf_op jit(solution)/shard_map/ppermute | solution.py:26
  85.9 10.9 %copy-start.20 = (s32[2,8,128]{2,1,0:T(8,128)S(1)}, s32[2,8,128]{2,1,0:T(8,128)}, u32[]{:S(2)}) copy-start(s32[2,8,128]{2,1,0:T(8,128)} %param.10) | copy-start | bytes 24580
  85.9 10.9 %copy-start.22 = (f32[2,8,128]{2,1,0:T(8,128)S(1)}, f32[2,8,128]{2,1,0:T(8,128)}, u32[]{:S(2)}) copy-start(f32[2,8,128]{2,1,0:T(8,128)} %param.8) | copy-start | bytes 24580
  85.9 10.9 %copy-start.24 = (f32[8,128]{1,0:T(8,128)S(1)}, f32[8,128]{1,0:T(8,128)}, u32[]{:S(2)}) copy-start(f32[8,128]{1,0:T(8,128)} %param.9) | copy-start | bytes 12292
  85.9 10.9 %copy-start.25 = (f32[8,128]{1,0:T(8,128)S(1)}, f32[8,128]{1,0:T(8,128)}, u32[]{:S(2)}) copy-start(f32[8,128]{1,0:T(8,128)} %get-tuple-element.40) | copy-start | bytes 12292
  85.9 10.9 %copy-start.27 = (f32[2]{0:T(128)S(1)}, f32[2]{0:T(128)}, u32[]{:S(2)}) copy-start(f32[2]{0:T(128)} %copy-done.26) | copy-start | bytes 28
  86.4 9.7 %collective-permute-start.8 = (f32[2,2,128]{2,1,0:T(2,128)S(1)}, f32[2,2,128]{2,1,0:T(2,128)S(1)}, u32[]{:S(2)}, u32[]{:S(2)}) collective-permute-start(f32[2,2,128]{2,1,0:T(2,128)S(1)} %get-tuple-element.42), channel_id=1, source_target_pairs={{2,0},{4,2},{6,4},{8,6},{10,8},{12,10},{14,12},{16,14},{18,16},{20... | collective-permute-start | bytes 6152 | tf_op jit(solution)/shard_map/ppermute | solution.py:27
  87.7 9.1 %collective-permute-start.9 = (f32[2,2,128]{2,1,0:T(2,128)S(1)}, f32[2,2,128]{2,1,0:T(2,128)S(1)}, u32[]{:S(2)}, u32[]{:S(2)}) collective-permute-start(f32[2,2,128]{2,1,0:T(2,128)S(1)} %get-tuple-element.43), channel_id=1, source_target_pairs={{0,2},{2,4},{4,6},{6,8},{8,10},{10,12},{12,14},{14,16},{16,18},{18... | collective-permute-start | bytes 6152 | tf_op jit(solution)/shard_map/ppermute | solution.py:26
  (15 other events, 50.1 us)
where the time goes:
time: 145 us
  blocking collectives  44.2 us (30%)
  local copies, waits for them, and re-layouts  35.3 us (24%)
  starting transfers between devices  33 us (23%)
  other arithmetic  28.4 us (20%)
  between operations  1.84 us (1%)
  waiting for transfers between devices  1.83 us (1%)
    psum x1, blocking collectives, on_device(): total = lax.psum(jnp.sum(wall_grad * wall_grad), ('roll', 'trans'))  44.2 us
    ppermute x5, starting transfers between devices, extended(): before = lax.ppermute(last, axis, up)  26.6 us
    unnamed x65, local copies, waits for them, and re-layouts  13.8 us
    div x2, other arithmetic, time_section(): (-along_y(2) + 8.0 * along_y(1) - 8.0 * along_y(-1) + along_y(-2)) / 12.0  7.83 us
    add x2, other arithmetic, time_section(): diffused = fluid_viscosity * (second_x + second_y) + film_coef * second_z  7.57 us
    ppermute x5, starting transfers between devices, extended(): after = lax.ppermute(leading, axis, down)  6.44 us
    concatenate x2, local copies, waits for them, and re-layouts, extended(): array = jnp.concatenate([before, array, after], axis=dim)  6.07 us
    ppermute x3, local copies, waits for them, and re-layouts, extended(): before = lax.ppermute(last, axis, up)  5.96 us
  transfers between devices with their start and end apart: 10, of which 2 were waited for; matrix products, arithmetic and copies ran while one was open for 17% of the time, Pallas kernels for 0%

commit v1 on v0

v1 whole, which is shorter than its diff:
```python
import functools

import jax
import jax.numpy as jnp
from jax import lax
from jax.experimental import pallas as pl
from jax.experimental.pallas import tpu as pltpu
from jax.sharding import PartitionSpec as P

SECTIONS = 2


VISCOSITY_PRESS = 0.3
VISCOSITY_TEMP = 0.5
THETA_STEP = 0.2
SOUND = 0.5
KAPPA = 0.6
HEATING = 0.3
ROLL_SPEED = 1.0
COURANT = 0.8

VM = pl.BlockSpec(memory_space=pltpu.VMEM)
SM = pl.BlockSpec(memory_space=pltpu.SMEM)
WEIGHTS = (0.5, 1.0, 1.0, KAPPA)
N_COEF = 13


def lanes_of(shape):
    return lax.broadcasted_iota(jnp.int32, shape, 1)


def rows_of(shape):
    return lax.broadcasted_iota(jnp.int32, shape, 0)


def pack_rows(state_ref, up_ref, down_ref, planes):
    for row in range(2):
        for i in range(planes // 8):
            here = pl.ds(row * planes + 8 * i, 8)
            up_ref[here, :] = state_ref[pl.ds(64 * i + 6 + row, 8, stride=8), :]
            down_ref[here, :] = state_ref[pl.ds(64 * i + row, 8, stride=8), :]


def unpack_rows(halo_ref, below_ref, above_ref, planes):
    for row in range(2):
        for i in range(planes // 8):
            here = pl.ds(row * planes + 8 * i, 8)
            halo_ref[pl.ds(64 * i + 6 + row, 8, stride=8), :] = below_ref[here, :]
            halo_ref[pl.ds(64 * i + row, 8, stride=8), :] = above_ref[here, :]


def pack_columns(packed, plane, k, lane):
    return jnp.where(lane // 4 == k, pltpu.roll(plane, 4 * k + 2, 1), packed)


def pack_kernel(depth, cases, state_ref, up_ref, down_ref, cols_ref):
    planes = 4 * cases * depth
    pack_rows(state_ref, up_ref, down_ref, planes)
    lane = lanes_of((8, 128))
    for group in range(4 * cases):

        def step(k, packed):
            plane = state_ref[pl.ds(pl.multiple_of((group * depth + k) * 8, 8), 8), :]
            return pack_columns(packed, plane, k, lane)

        packed = lax.fori_loop(0, depth, step, jnp.zeros((8, 128), jnp.float32), unroll=8)
        cols_ref[pl.ds(group * 8, 8), :] = packed


def shifted(plane, halo, place, axis, size):
    def moved(edge, by):
        return pltpu.roll(jnp.where(edge, halo, plane), by, axis)

    before = moved(place == size - 1, 1), moved(place >= size - 2, 2)
    after = moved(place == 0, size - 1), moved(place < 2, size - 2)
    return before + after


def derivatives(plane, halo, cols, lane, row):
    ym1, ym2, yp1, yp2 = shifted(plane, cols, lane, 1, 128)
    xm1, xm2, xp1, xp2 = shifted(plane, halo, row, 0, 8)
    second = 16.0 * ((xm1 + xp1) + (ym1 + yp1)) - ((xm2 + xp2) + (ym2 + yp2))
    first_x = 8.0 * (xp1 - xm1) - (xp2 - xm2)
    first_y = 8.0 * (yp1 - ym1) - (yp2 - ym2)
    return second, first_x, first_y


def coefficient_planes(pressure, film, cavity, level):
    theta = THETA_STEP * level.astype(jnp.float32)
    viscosity = jnp.exp(VISCOSITY_PRESS * pressure - VISCOSITY_TEMP * theta)
    film_coef = 4.0 * viscosity / (film * film)
    density = 1.0 - 0.6 * cavity.astype(jnp.float32)
    step = COURANT / (32.0 / 3.0 * viscosity + 4.0 * film_coef + 2.0 * SOUND + 1.0)
    planes = []
    for weight in (0.5, 1.0, KAPPA):
        spread = (weight / 12.0) * step * viscosity
        across = weight * step * film_coef
        planes += [1.0 - 60.0 * spread - 2.0 * across, spread, across]
    planes += [(ROLL_SPEED / 12.0) * step * density, (SOUND / 12.0) * step, step, HEATING * step * viscosity]
    return planes, viscosity, density


def section_kernel(
    depth,
    cases,
    final,
    trans,
    level_ref,
    state_ref,
    source_ref,
    below_ref,
    above_ref,
    side_ref,
    pressure_ref,
    film_ref,
    cavity_ref,
    *rest,
):
    if final:
        out_ref, terms_ref, mean_up_ref, mean_down_ref, halo_ref, coef_ref = rest
    else:
        out_ref, up_ref, down_ref, cols_ref, halo_ref, coef_ref = rest
    planes = 4 * cases * depth
    lane, row = lanes_of((8, 128)), rows_of((8, 128))
    unpack_rows(halo_ref, below_ref, above_ref, planes)
    place = lax.axis_index(trans)
    from_left = jnp.where(place > 0, 1.0, 0.0)
    from_right = jnp.where(place < lax.axis_size(trans) - 1, 1.0, 0.0)
    side_mask = jnp.where(lane % 4 < 2, from_left, from_right)
    film = film_ref[...]
    wall = jnp.zeros((8, 128), jnp.float32)
    for case in range(cases):
        coefs, viscosity, density = coefficient_planes(
            pressure_ref[pl.ds(case * 8, 8), :], film, cavity_ref[pl.ds(case * 8, 8), :], level_ref[case]
        )
        for i, plane in enumerate(coefs):
            coef_ref[pl.ds(i * 8, 8), :] = plane
        sides = [side_ref[pl.ds((c * cases + case) * 8, 8), :] * side_mask for c in range(4)]

        def at(component, k):
            return pl.ds(pl.multiple_of(((component * cases + case) * depth + k) * 8, 8), 8)

        def coef(i):
            return coef_ref[pl.ds(i * 8, 8), :]

        def body(k, carry):
            before, now, extra = carry
            height = (k.astype(jnp.float32) + 0.5) / depth
            flag = jnp.where(k + 1 < depth, 1.0, 0.0)
            later = [state_ref[at(c, jnp.minimum(k + 1, depth - 1)), :] * flag for c in range(4)]
            parts = [
                derivatives(now[c], halo_ref[at(c, k), :], pltpu.roll(sides[c], 126 + 128 - 4 * k, 1), lane, row)
                for c in range(4)
            ]
            new = []
            density_step = coef(9) * height
            sound = coef(10)
            for c in range(4):
                which = (0, 1, 1, 2)[c]
                second, first_x, _ = parts[c]
                value = coef(3 * which) * now[c] + coef(3 * which + 1) * second
                value += coef(3 * which + 2) * (before[c] + later[c])
                value += density_step * first_x + coef(11) * source_ref[at(c, k), :]
                if c == 0:
                    value += sound * (parts[1][1] + parts[2][2])
                elif c == 1:
                    value += sound * parts[0][1]
                elif c == 2:
                    value += sound * parts[0][2]
                else:
                    value += coef(12) * now[1]
                out_ref[at(c, k), :] = value
                new.append(value)
            if final:
                total, bend, last = extra
                change = new[1] - last
                extra = (total + new[0], bend + change * change, new[1])
            else:
                extra = tuple(pack_columns(packed, value, k, lane) for packed, value in zip(extra, new, strict=True))
            return now, later, extra

        zero = jnp.zeros((8, 128), jnp.float32)
        start = [state_ref[at(c, 0), :] for c in range(4)]
        _, _, extra = lax.fori_loop(0, depth, body, ([zero] * 4, start, (zero,) * (3 if final else 4)), unroll=2)
        if final:
            total, bend, last = extra
            mean = total * (1.0 / depth)
            curvature = -(bend + last * last) * (1.0 / depth)
            wall = wall - 8.0 * viscosity / (film * film * film) * curvature
            terms_ref[pl.ds(case * 8, 8), :] = mean
            terms_ref[pl.ds((cases + case) * 8, 8), :] = (ROLL_SPEED / 24.0) * density * film
        else:
            for c in range(4):
                cols_ref[pl.ds((c * cases + case) * 8, 8), :] = extra[c]
    if final:
        terms_ref[pl.ds(2 * cases * 8, 8), :] = wall
        for case in range(cases):
            mean_up_ref[pl.ds(case * 8, 8), :] = terms_ref[pl.ds(case * 8, 8), :]
            mean_down_ref[pl.ds(case * 8, 8), :] = terms_ref[pl.ds(case * 8, 8), :]
    else:
        pack_rows(out_ref, up_ref, down_ref, planes)


def wall_kernel(cases, terms_ref, below_ref, above_ref, grad_ref, sums_ref):
    row = rows_of((8, 128))
    grad = terms_ref[pl.ds(2 * cases * 8, 8), :]
    for case in range(cases):
        mean = terms_ref[pl.ds(case * 8, 8), :]
        halo = jnp.where(row >= 4, below_ref[pl.ds(case * 8, 8), :], above_ref[pl.ds(case * 8, 8), :])
        xm1, xm2, xp1, xp2 = shifted(mean, halo, row, 0, 8)
        slope = 8.0 * (xp1 - xm1) - (xp2 - xm2)
        grad += terms_ref[pl.ds((cases + case) * 8, 8), :] * slope
    grad_ref[...] = grad
    part = jnp.sum(grad * grad, axis=0, keepdims=True)
    sums_ref[...] = jnp.broadcast_to(part[None], sums_ref.shape)


def scale_kernel(cells, grad_ref, sums_ref, out_ref):
    total = jnp.sum(sums_ref[...], axis=0)
    total = jnp.sum(total, axis=1, keepdims=True)
    out_ref[...] = grad_ref[...] / jnp.sqrt(total / cells + 1e-06)


def f32(*shape):
    return jax.ShapeDtypeStruct(shape, jnp.float32)


def neighbours(axis):
    size = lax.axis_size(axis)
    up = [(i, i + 1) for i in range(size - 1)]
    return up, [(j, i) for i, j in up]


def exchange_rows(up, down):
    ahead, back = neighbours("roll")
    return lax.ppermute(up, "roll", ahead), lax.ppermute(down, "roll", back)


def exchange_columns(cols):
    ahead, back = neighbours("trans")
    if lax.axis_size("trans") == 2:
        return lax.ppermute(cols, "trans", ahead + back)
    left, right = lax.ppermute(cols, "trans", ahead), lax.ppermute(cols, "trans", back)
    return jnp.where(lanes_of(cols.shape) % 4 < 2, left, right)


def on_device(adjoint, source, pressure, film, cavity, temp_index):
    components, cases, depth, width_x, width_y = adjoint.shape
    planes = components * cases * depth
    assert (components, width_x, width_y, 4 * depth) == (4, 8, 128, 128)
    state = adjoint.reshape(planes * 8, 128)
    forcing = source.reshape(planes * 8, 128)
    pressure = pressure.reshape(cases * 8, 128)
    cavity = cavity.reshape(cases * 8, 128)
    message = (f32(planes * 2, 128), f32(planes * 2, 128), f32(components * cases * 8, 128))
    params = pltpu.CompilerParams(vmem_limit_bytes=24 * 1024 * 1024)
    up, down, cols = pl.pallas_call(
        functools.partial(pack_kernel, depth, cases),
        out_shape=message,
        in_specs=[VM],
        out_specs=(VM,) * 3,
        compiler_params=params,
    )(state)
    for index in range(SECTIONS):
        final = index == SECTIONS - 1
        side = exchange_columns(cols)
        below, above = exchange_rows(up, down)
        if final:
            shapes = (f32(planes * 8, 128), f32((2 * cases + 1) * 8, 128), f32(cases * 8, 128), f32(cases * 8, 128))
        else:
            shapes = (f32(planes * 8, 128),) + message
        results = pl.pallas_call(
            functools.partial(section_kernel, depth, cases, final, "trans"),
            out_shape=shapes,
            in_specs=[SM] + [VM] * 8,
            out_specs=(VM,) * len(shapes),
            scratch_shapes=[pltpu.VMEM((planes * 8, 128), jnp.float32), pltpu.VMEM((N_COEF * 8, 128), jnp.float32)],
            compiler_params=params,
        )(temp_index, state, forcing, below, above, side, pressure, film, cavity)
        if final:
            state, terms, up, down = results
        else:
            state, up, down, cols = results
    below, above = exchange_rows(up, down)
    devices = lax.axis_size("roll") * lax.axis_size("trans")
    grad, sums = pl.pallas_call(
        functools.partial(wall_kernel, cases),
        out_shape=(f32(8, 128), f32(devices, 1, 128)),
        in_specs=[VM] * 3,
        out_specs=(VM,) * 2,
    )(terms, below, above)
    sums = lax.all_to_all(sums, ("roll", "trans"), 0, 0, tiled=True)
    wall_step = pl.pallas_call(
        functools.partial(scale_kernel, devices * width_x * width_y),
        out_shape=f32(8, 128),
        in_specs=[VM] * 2,
        out_specs=VM,
    )(grad, sums)
    return (state.reshape(adjoint.shape), wall_step)


def solution(mesh):
    placed = (
        P(None, None, None, "roll", "trans"),
        P(None, None, None, "roll", "trans"),
        P(None, "roll", "trans"),
        P("roll", "trans"),
        P(None, "roll", "trans"),
        P(),
    )
    return jax.shard_map(
        on_device,
        mesh=mesh,
        in_specs=placed,
        out_specs=(P(None, None, None, "roll", "trans"), P("roll", "trans")),
        check_vma=False,
    )
```

time: 145 us -> 70.7 us (0.49)
  local copies, waits for them, and re-layouts: 35.3 us -> 4.46 us
  blocking collectives: 44.2 us -> 15.6 us
  other arithmetic: 28.4 us -> 0 us
  Pallas kernels: 0 us -> 21.3 us
  starting transfers between devices: 33 us -> 21.7 us
  waiting for transfers between devices: 1.83 us -> 6.27 us
    psum x1 -> x0, blocking collectives: 44.2 us -> none  [on_device(): total = lax.psum(jnp.sum(wall_grad * wall_grad), ('roll', 'trans'))]
    pallas_call x0 -> x5, Pallas kernels: none -> 21.3 us  [the longest x2 15.9 us: on_device(): pl.pallas_call(functools.partial(section_kernel, depth, cases, final, 'tr...]
    all_to_all x0 -> x1, blocking collectives: none -> 15.6 us  [on_device(): sums = lax.all_to_all(sums, ('roll', 'trans'), 0, 0, tiled=True)]
    ppermute x6 -> x0, local copies, waits for them, and re-layouts: 11.7 us -> none  [the longest x3 5.96 us: extended(): before = lax.ppermute(last, axis, up)]
    div x8 -> x0, other arithmetic: 11.7 us -> none  [the longest x2 7.83 us: time_section(): (-along_y(2) + 8.0 * along_y(1) - 8.0 * along_y(-1) + along_y(-2)) / 12.0]
    ppermute x10 -> x8, starting transfers between devices: 33 us -> 21.7 us  [the longest x6 17.8 us: exchange_rows(): return (lax.ppermute(up, 'roll', ahead), lax.ppermute(down, 'roll', back))]
    unnamed x65 -> x20, local copies, waits for them, and re-layouts: 13.8 us -> 4.46 us
    add x6 -> x0, other arithmetic: 9.29 us -> none  [the longest x2 7.57 us: time_section(): diffused = fluid_viscosity * (second_x + second_y) + film_coef * second_z]
  transfers between devices with their start and end apart: 10 -> 8, of which waited for: 2 -> 3; matrix products, arithmetic and copies ran while one was open for 17% -> 0% of each run, Pallas kernels for 0% -> 0%
where the time goes in v1:
time: 70.7 us; the launch traced here: 70.1 us
  starting transfers between devices  21.7 us (31%)
  Pallas kernels  21.3 us (30%)
  blocking collectives  15.6 us (22%)
  waiting for transfers between devices  6.27 us (9%)
  local copies, waits for them, and re-layouts  4.46 us (6%)
  between operations  0.76 us (1%)
    ppermute x6, starting transfers between devices, exchange_rows(): return (lax.ppermute(up, 'roll', ahead), lax.ppermute(down, 'roll', back))  17.8 us
    pallas_call x2, Pallas kernels, on_device(): pl.pallas_call(functools.partial(section_kernel, depth, cases, final, 'tr...  15.9 us
    all_to_all x1, blocking collectives, on_device(): sums = lax.all_to_all(sums, ('roll', 'trans'), 0, 0, tiled=True)  15.6 us
    ppermute x2, waiting for transfers between devices, exchange_columns(): return lax.ppermute(cols, 'trans', ahead + back)  4.51 us
    unnamed x20, local copies, waits for them, and re-layouts  4.46 us
    ppermute x2, starting transfers between devices, exchange_columns(): return lax.ppermute(cols, 'trans', ahead + back)  3.94 us
    pallas_call x1, Pallas kernels, on_device(): pl.pallas_call(functools.partial(pack_kernel, depth, cases), out_shape=me...  2.57 us
    ppermute x6, waiting for transfers between devices, exchange_rows(): return (lax.ppermute(up, 'roll', ahead), lax.ppermute(down, 'roll', back))  1.76 us
  transfers between devices with their start and end apart: 8, of which 3 were waited for; matrix products, arithmetic and copies ran while one was open for 0% of the time, Pallas kernels for 0%

profile of v1, /device:TPU:0, one launch (start us, length us, event | category | flops | bytes accessed | tf_op | source)
XLA Modules:
  0.0 70.1 jit_solution(8309922800434921485)
XLA Ops:
  0.6 1.2 %copy-done = f32[4,2,32,8,128]{4,3,2,1,0:T(8,128)S(1)} copy-done((f32[4,2,32,8,128]{4,3,2,1,0:T(8,128)S(1)}, f32[4,2,32,8,128]{4,3,2,1,0:T(8,128)}, u32[]{:S(2)}) %copy-start) | copy-done | bytes 1048600
  1.9 2.6 %shard_map.77 = (f32[512,128]{1,0:T(8,128)S(1)}, f32[512,128]{1,0:T(8,128)S(1)}, f32[64,128]{1,0:T(8,128)S(1)}) custom-call(f32[2048,128]{1,0:T(8,128)S(1)} %bitcast.5), custom_call_target="tpu_custom_call" | custom-call | tf_op jit(solution)/shard_map/pallas_call | solution.py:257
  4.4 2.4 %collective-permute-start = (f32[512,128]{1,0:T(8,128)S(1)}, f32[512,128]{1,0:T(8,128)S(1)}, u32[]{:S(2)}, u32[]{:S(2)}) collective-permute-start(f32[512,128]{1,0:T(8,128)S(1)} %get-tuple-element.15), channel_id=1, source_target_pairs={{0,2},{2,4},{4,6},{6,8},{8,10},{10,12},{12,14},{14,16},{16,18},{18... | collective-permute-start | bytes 786440 | tf_op jit(solution)/shard_map/ppermute | solution.py:236
  6.8 1.3 %collective-permute-start.1 = (f32[512,128]{1,0:T(8,128)S(1)}, f32[512,128]{1,0:T(8,128)S(1)}, u32[]{:S(2)}, u32[]{:S(2)}) collective-permute-start(f32[512,128]{1,0:T(8,128)S(1)} %get-tuple-element.16), channel_id=1, source_target_pairs={{2,0},{4,2},{6,4},{8,6},{10,8},{12,10},{14,12},{16,14},{18,16},{20... | collective-permute-start | bytes 786440 | tf_op jit(solution)/shard_map/ppermute | solution.py:236
  8.1 2.4 %collective-permute-start.2 = (f32[64,128]{1,0:T(8,128)S(1)}, f32[64,128]{1,0:T(8,128)S(1)}, u32[]{:S(2)}, u32[]{:S(2)}) collective-permute-start(f32[64,128]{1,0:T(8,128)S(1)} %get-tuple-element.17), channel_id=1, source_target_pairs={{0,1},{1,0},{2,3},{3,2},{4,5},{5,4},{6,7},{7,6},{8,9},{9,8},{10,11... | collective-permute-start | bytes 98312 | tf_op jit(solution)/shard_map/ppermute | solution.py:242
  10.5 1.9 %collective-permute-done.2.side_ref = f32[64,128]{1,0:T(8,128)S(1)} collective-permute-done((f32[64,128]{1,0:T(8,128)S(1)}, f32[64,128]{1,0:T(8,128)S(1)}, u32[]{:S(2)}, u32[]{:S(2)}) %collective-permute-start.2) | collective-permute-done | bytes 32800 | tf_op jit(solution)/shard_map/ppermute | solution.py:242
  12.4 0.6 copy-done.7
  13.1 0.7 copy-done.3
  13.8 0.7 copy-done.5
  14.5 8.6 %shard_map.78 = (f32[2048,128]{1,0:T(8,128)S(1)}, f32[512,128]{1,0:T(8,128)S(1)}, f32[512,128]{1,0:T(8,128)S(1)}, f32[64,128]{1,0:T(8,128)S(1)}) custom-call(s32[2]{0:T(128)S(1)} %copy-done.7, f32[2048,128]{1,0:T(8,128)S(1)} %bitcast.6, f32[2048,128]{1,0:T(8,128)S(1)} %bitcast.7, f32[512,128]{1,0:T(8,128)S(1)} %collective-permute-done.below_ref, ...), custom_call_target="tpu_custom_call" | custom-call | tf_op jit(solution)/shard_map/pallas_call | solution.py:272
  23.1 0.0 copy-start.6
  23.1 6.6 %collective-permute-start.3 = (f32[512,128]{1,0:T(8,128)S(1)}, f32[512,128]{1,0:T(8,128)S(1)}, u32[]{:S(2)}, u32[]{:S(2)}) collective-permute-start(f32[512,128]{1,0:T(8,128)S(1)} %get-tuple-element.19), channel_id=1, source_target_pairs={{0,2},{2,4},{4,6},{6,8},{8,10},{10,12},{12,14},{14,16},{16,18},{18... | collective-permute-start | bytes 786440 | tf_op jit(solution)/shard_map/ppermute | solution.py:236
  29.7 1.3 %collective-permute-start.4 = (f32[512,128]{1,0:T(8,128)S(1)}, f32[512,128]{1,0:T(8,128)S(1)}, u32[]{:S(2)}, u32[]{:S(2)}) collective-permute-start(f32[512,128]{1,0:T(8,128)S(1)} %get-tuple-element.20), channel_id=1, source_target_pairs={{2,0},{4,2},{6,4},{8,6},{10,8},{12,10},{14,12},{16,14},{18,16},{20... | collective-permute-start | bytes 786440 | tf_op jit(solution)/shard_map/ppermute | solution.py:236
  31.0 1.6 %collective-permute-start.5 = (f32[64,128]{1,0:T(8,128)S(1)}, f32[64,128]{1,0:T(8,128)S(1)}, u32[]{:S(2)}, u32[]{:S(2)}) collective-permute-start(f32[64,128]{1,0:T(8,128)S(1)} %get-tuple-element.21), channel_id=1, source_target_pairs={{0,1},{1,0},{2,3},{3,2},{4,5},{5,4},{6,7},{7,6},{8,9},{9,8},{10,11... | collective-permute-start | bytes 98312 | tf_op jit(solution)/shard_map/ppermute | solution.py:242
  32.6 2.6 %collective-permute-done.5.side_ref = f32[64,128]{1,0:T(8,128)S(1)} collective-permute-done((f32[64,128]{1,0:T(8,128)S(1)}, f32[64,128]{1,0:T(8,128)S(1)}, u32[]{:S(2)}, u32[]{:S(2)}) %collective-permute-start.5) | collective-permute-done | bytes 32800 | tf_op jit(solution)/shard_map/ppermute | solution.py:242
  35.2 7.3 %shard_map.79 = (f32[2048,128]{1,0:T(8,128)}, f32[40,128]{1,0:T(8,128)S(1)}, f32[16,128]{1,0:T(8,128)S(1)}, f32[16,128]{1,0:T(8,128)S(1)}) custom-call(s32[2]{0:T(128)S(1)} %copy-done.7, f32[2048,128]{1,0:T(8,128)S(1)} %get-tuple-element.18.state_ref, f32[2048,128]{1,0:T(8,128)S(1)} %bitcast.8, f32[512,128]{1,0:T(8,128)S(1)} %collective-permute-done.3.below_ref, ...), custom_call_target="tpu_custom_call" | custom-call | tf_op jit(solution)/shard_map/pallas_call | solution.py:272
  42.5 0.6 copy-done.4
  43.1 4.9 %collective-permute-start.6 = (f32[16,128]{1,0:T(8,128)S(1)}, f32[16,128]{1,0:T(8,128)S(1)}, u32[]{:S(2)}, u32[]{:S(2)}) collective-permute-start(f32[16,128]{1,0:T(8,128)S(1)} %get-tuple-element.24), channel_id=1, source_target_pairs={{0,2},{2,4},{4,6},{6,8},{8,10},{10,12},{12,14},{14,16},{16,18},{18... | collective-permute-start | bytes 24584 | tf_op jit(solution)/shard_map/ppermute | solution.py:236
  48.0 1.3 %collective-permute-start.7 = (f32[16,128]{1,0:T(8,128)S(1)}, f32[16,128]{1,0:T(8,128)S(1)}, u32[]{:S(2)}, u32[]{:S(2)}) collective-permute-start(f32[16,128]{1,0:T(8,128)S(1)} %get-tuple-element.25), channel_id=1, source_target_pairs={{2,0},{4,2},{6,4},{8,6},{10,8},{12,10},{14,12},{16,14},{18,16},{20... | collective-permute-start | bytes 24584 | tf_op jit(solution)/shard_map/ppermute | solution.py:236
  49.4 1.7 %collective-permute-done.7.above_ref = f32[16,128]{1,0:T(8,128)S(1)} collective-permute-done((f32[16,128]{1,0:T(8,128)S(1)}, f32[16,128]{1,0:T(8,128)S(1)}, u32[]{:S(2)}, u32[]{:S(2)}) %collective-permute-start.7) | collective-permute-done | bytes 8224 | tf_op jit(solution)/shard_map/ppermute | solution.py:236
  51.1 0.6 copy-done.9
  51.7 1.4 %shard_map.80 = (f32[8,128]{1,0:T(8,128)}, f32[32,1,128]{2,1,0:T(1,128)}) custom-call(f32[40,128]{1,0:T(8,128)} %copy-done.4, f32[16,128]{1,0:T(8,128)} %copy-done.8, f32[16,128]{1,0:T(8,128)} %copy-done.9), custom_call_target="tpu_custom_call" | custom-call | tf_op jit(solution)/shard_map/pallas_call | solution.py:286
  53.1 15.6 %all_to_all.5.sums_ref = f32[32,1,128]{2,1,0:T(1,128)} all-to-all(f32[32,1,128]{2,1,0:T(1,128)} %get-tuple-element.27), channel_id=1, replica_groups=mesh['roll'=16,'trans'=2] {'roll','trans'}, dimensions={0} | all-to-all | bytes 32768 | tf_op jit(solution)/shard_map/all_to_all | solution.py:292
  68.7 1.4 %shard_map.81 = f32[8,128]{1,0:T(8,128)} custom-call(f32[8,128]{1,0:T(8,128)} %get-tuple-element.26.grad_ref, f32[32,1,128]{2,1,0:T(1,128)} %all_to_all.5.sums_ref), custom_call_target="tpu_custom_call" | custom-call | tf_op jit(solution)/shard_map/pallas_call | solution.py:293
  (18 shorter events, 0.0 us)
Async XLA Ops:
  0.6 1.2 %copy-start = (f32[4,2,32,8,128]{4,3,2,1,0:T(8,128)S(1)}, f32[4,2,32,8,128]{4,3,2,1,0:T(8,128)}, u32[]{:S(2)}) copy-start(f32[4,2,32,8,128]{4,3,2,1,0:T(8,128)} %param.6) | copy-start | bytes 3145732
  1.9 10.6 %copy-start.1 = (f32[4,2,32,8,128]{4,3,2,1,0:T(8,128)S(1)}, f32[4,2,32,8,128]{4,3,2,1,0:T(8,128)}, u32[]{:S(2)}) copy-start(f32[4,2,32,8,128]{4,3,2,1,0:T(8,128)} %param.7) | copy-start | bytes 3145732
  4.4 8.0 %copy-start.2 = (f32[2,8,128]{2,1,0:T(8,128)S(1)}, f32[2,8,128]{2,1,0:T(8,128)}, u32[]{:S(2)}) copy-start(f32[2,8,128]{2,1,0:T(8,128)} %param.8) | copy-start | bytes 24580
  4.4 8.0 %collective-permute-start = (f32[512,128]{1,0:T(8,128)S(1)}, f32[512,128]{1,0:T(8,128)S(1)}, u32[]{:S(2)}, u32[]{:S(2)}) collective-permute-start(f32[512,128]{1,0:T(8,128)S(1)} %get-tuple-element.15), channel_id=1, source_target_pairs={{0,2},{2,4},{4,6},{6,8},{8,10},{10,12},{12,14},{14,16},{16,18},{18... | collective-permute-start | bytes 786440 | tf_op jit(solution)/shard_map/ppermute | solution.py:236
  6.8 5.6 %collective-permute-start.1 = (f32[512,128]{1,0:T(8,128)S(1)}, f32[512,128]{1,0:T(8,128)S(1)}, u32[]{:S(2)}, u32[]{:S(2)}) collective-permute-start(f32[512,128]{1,0:T(8,128)S(1)} %get-tuple-element.16), channel_id=1, source_target_pairs={{2,0},{4,2},{6,4},{8,6},{10,8},{12,10},{14,12},{16,14},{18,16},{20... | collective-permute-start | bytes 786440 | tf_op jit(solution)/shard_map/ppermute | solution.py:236
  8.1 4.3 %collective-permute-start.2 = (f32[64,128]{1,0:T(8,128)S(1)}, f32[64,128]{1,0:T(8,128)S(1)}, u32[]{:S(2)}, u32[]{:S(2)}) collective-permute-start(f32[64,128]{1,0:T(8,128)S(1)} %get-tuple-element.17), channel_id=1, source_target_pairs={{0,1},{1,0},{2,3},{3,2},{4,5},{5,4},{6,7},{7,6},{8,9},{9,8},{10,11... | collective-permute-start | bytes 98312 | tf_op jit(solution)/shard_map/ppermute | solution.py:242
  12.4 0.7 copy-start.7
  13.1 0.7 copy-start.3
  13.8 0.7 copy-start.5
  23.1 12.1 %copy-start.6 = (f32[8,128]{1,0:T(8,128)S(1)}, f32[8,128]{1,0:T(8,128)}, u32[]{:S(2)}) copy-start(f32[8,128]{1,0:T(8,128)} %film_ref.3) | copy-start | bytes 12292
  23.1 12.1 %collective-permute-start.3 = (f32[512,128]{1,0:T(8,128)S(1)}, f32[512,128]{1,0:T(8,128)S(1)}, u32[]{:S(2)}, u32[]{:S(2)}) collective-permute-start(f32[512,128]{1,0:T(8,128)S(1)} %get-tuple-element.19), channel_id=1, source_target_pairs={{0,2},{2,4},{4,6},{6,8},{8,10},{10,12},{12,14},{14,16},{16,18},{18... | collective-permute-start | bytes 786440 | tf_op jit(solution)/shard_map/ppermute | solution.py:236
  29.7 5.5 %collective-permute-start.4 = (f32[512,128]{1,0:T(8,128)S(1)}, f32[512,128]{1,0:T(8,128)S(1)}, u32[]{:S(2)}, u32[]{:S(2)}) collective-permute-start(f32[512,128]{1,0:T(8,128)S(1)} %get-tuple-element.20), channel_id=1, source_target_pairs={{2,0},{4,2},{6,4},{8,6},{10,8},{12,10},{14,12},{16,14},{18,16},{20... | collective-permute-start | bytes 786440 | tf_op jit(solution)/shard_map/ppermute | solution.py:236
  31.0 4.2 %collective-permute-start.5 = (f32[64,128]{1,0:T(8,128)S(1)}, f32[64,128]{1,0:T(8,128)S(1)}, u32[]{:S(2)}, u32[]{:S(2)}) collective-permute-start(f32[64,128]{1,0:T(8,128)S(1)} %get-tuple-element.21), channel_id=1, source_target_pairs={{0,1},{1,0},{2,3},{3,2},{4,5},{5,4},{6,7},{7,6},{8,9},{9,8},{10,11... | collective-permute-start | bytes 98312 | tf_op jit(solution)/shard_map/ppermute | solution.py:242
  42.5 0.6 copy-start.4
  43.1 6.2 %collective-permute-start.6 = (f32[16,128]{1,0:T(8,128)S(1)}, f32[16,128]{1,0:T(8,128)S(1)}, u32[]{:S(2)}, u32[]{:S(2)}) collective-permute-start(f32[16,128]{1,0:T(8,128)S(1)} %get-tuple-element.24), channel_id=1, source_target_pairs={{0,2},{2,4},{4,6},{6,8},{8,10},{10,12},{12,14},{14,16},{16,18},{18... | collective-permute-start | bytes 24584 | tf_op jit(solution)/shard_map/ppermute | solution.py:236
  48.0 3.1 %collective-permute-start.7 = (f32[16,128]{1,0:T(8,128)S(1)}, f32[16,128]{1,0:T(8,128)S(1)}, u32[]{:S(2)}, u32[]{:S(2)}) collective-permute-start(f32[16,128]{1,0:T(8,128)S(1)} %get-tuple-element.25), channel_id=1, source_target_pairs={{2,0},{4,2},{6,4},{8,6},{10,8},{12,10},{14,12},{16,14},{18,16},{20... | collective-permute-start | bytes 24584 | tf_op jit(solution)/shard_map/ppermute | solution.py:236
  49.3 1.8 %copy-start.8 = (f32[16,128]{1,0:T(8,128)}, f32[16,128]{1,0:T(8,128)S(1)}, u32[]{:S(2)}) copy-start(f32[16,128]{1,0:T(8,128)S(1)} %collective-permute-done.6.below_ref) | copy-start | bytes 24580
  51.1 0.6 copy-start.9

commit v2 on v0

v2 whole, which is shorter than its diff:
```python
import functools

import jax
import jax.numpy as jnp
from jax import lax
from jax.experimental import pallas as pl
from jax.experimental.pallas import tpu as pltpu
from jax.sharding import PartitionSpec as P

SECTIONS = 2


VISCOSITY_PRESS = 0.3
VISCOSITY_TEMP = 0.5
THETA_STEP = 0.2
SOUND = 0.5
KAPPA = 0.6
HEATING = 0.3
ROLL_SPEED = 1.0
COURANT = 0.8

VM = pl.BlockSpec(memory_space=pltpu.VMEM)
SM = pl.BlockSpec(memory_space=pltpu.SMEM)
PARAMS = pltpu.CompilerParams(vmem_limit_bytes=16 * 1024 * 1024)

PAD = 8
CENTER, SPREAD, ACROSS = (0, 3, 6)
CARRY, SOUND_STEP, STEP, HEAT, FLUX, BEND = range(9, 15)
N_COEF = 15
N_PACKED = 5
WEIGHT = (0, 1, 1, 2)


def lanes_of(shape):
    return lax.broadcasted_iota(jnp.int32, shape, 1)


def rows_of(shape):
    return lax.broadcasted_iota(jnp.int32, shape, 0)


def rows(start, count=8):
    return pl.ds(start, count)


def strided(start):
    return pl.ds(start, 8, stride=8)


def coefficient_kernel(depth, cases, level_ref, place_ref, pressure_ref, film_ref, cavity_ref, coef_ref, packed_ref, mask_ref):
    lane, row = lanes_of((8, 128)), rows_of((8, 128))
    film = film_ref[...]
    height = ((depth - 1 - lane // 4).astype(jnp.float32) + 0.5) / depth
    for case in range(cases):
        theta = THETA_STEP * level_ref[case].astype(jnp.float32)
        viscosity = jnp.exp(VISCOSITY_PRESS * pressure_ref[rows(case * 8), :] - VISCOSITY_TEMP * theta)
        film_coef = 4.0 * viscosity / (film * film)
        density = 1.0 - 0.6 * cavity_ref[rows(case * 8), :].astype(jnp.float32)
        step = COURANT / (32.0 / 3.0 * viscosity + 4.0 * film_coef + 2.0 * SOUND + 1.0)
        planes = [None] * N_COEF
        for i, weight in enumerate((0.5, 1.0, KAPPA)):
            planes[SPREAD + i] = (weight / 12.0) * step * viscosity
            planes[ACROSS + i] = weight * step * film_coef
            planes[CENTER + i] = 1.0 - 60.0 * planes[SPREAD + i] - 2.0 * planes[ACROSS + i]
        planes[CARRY] = (ROLL_SPEED / 12.0) * step * density
        planes[SOUND_STEP] = (SOUND / 12.0) * step
        planes[STEP] = step
        planes[HEAT] = HEATING * step * viscosity
        planes[FLUX] = (ROLL_SPEED / (24.0 * depth)) * density * film
        planes[BEND] = (8.0 / depth) * viscosity / (film * film * film)
        for i, plane in enumerate(planes):
            coef_ref[rows((case * N_COEF + i) * 8), :] = plane
        wanted = jnp.concatenate(planes[SPREAD : SPREAD + 3] + [planes[CARRY], planes[SOUND_STEP]], axis=0)
        packed = exact_dot(wanted, edge_columns())
        for i in range(N_PACKED):
            plane = packed[i * 8 : i * 8 + 8]
            packed_ref[rows((case * N_PACKED + i) * 8), :] = plane * height if i == 3 else plane
    from_left = jnp.where(place_ref[0] > 0, 1.0, 0.0)
    from_right = jnp.where(place_ref[0] < place_ref[1] - 1, 1.0, 0.0)
    mask_ref[...] = jnp.where(lane % 4 < 2, from_left, from_right)


def edge_columns():
    source = lanes_of((128, 128)) % 4
    source = jnp.where(source < 2, 126 + source, source - 2)
    return jnp.where(rows_of((128, 128)) == source, 1.0, 0.0).astype(jnp.bfloat16)


def in_parts(value):
    high = value.astype(jnp.bfloat16)
    rest = value - high.astype(jnp.float32)
    middle = rest.astype(jnp.bfloat16)
    return jnp.concatenate([high, middle], axis=1), (rest - middle.astype(jnp.float32)).astype(jnp.bfloat16)


def exact_dot(value, weights):
    upper, low = in_parts(value)
    part = jnp.dot(upper, jnp.concatenate([weights, weights], axis=0), preferred_element_type=jnp.float32)
    return part + jnp.dot(low, weights, preferred_element_type=jnp.float32)


def send_edges(cols_ref, up_ref, down_ref, planes):
    for row in range(2):
        up_ref[rows(2 * planes + 8 * row), :] = cols_ref[strided(6 + row), :]
        down_ref[rows(2 * planes + 8 * row), :] = cols_ref[strided(row), :]


def pack_kernel(depth, cases, state_ref, tiles_ref, up_ref, down_ref, cols_ref):
    planes = 4 * cases * depth
    lane = lanes_of((8, 128))

    def one(pair, _):
        held = jnp.zeros((8, 128), jnp.float32)
        for layer in range(depth):
            group = depth - 1 - layer
            plane = state_ref[rows(pl.multiple_of((pair * depth + layer) * 8, 8)), :]
            held = jnp.where(lane // 4 == group, pltpu.roll(plane, (4 * group + 2) % 128, 1), held)
        cols_ref[rows(pl.multiple_of(pair * 8, 8)), :] = held
        for row in (0, 1, 6, 7, 2, 3, 4, 5):
            for block in range(depth // 8):
                first = pl.multiple_of(pair * depth + 8 * block, 8)
                tile = state_ref[strided(first * 8 + row), :]
                tiles_ref[rows(PAD + row * planes + first), :] = tile
                if row < 2:
                    down_ref[rows(row * planes + first), :] = tile
                if row > 5:
                    up_ref[rows((row - 6) * planes + first), :] = tile
        return 0

    lax.fori_loop(0, 4 * cases, one, 0)
    send_edges(cols_ref, up_ref, down_ref, planes)


def inner_kernel(depth, cases, tiles_ref, source_ref, coef_ref, *rest):
    out_ref, *cols_ref, deriv_ref = rest
    planes = 4 * cases * depth
    lane, layer = lanes_of((8, 128)), rows_of((8, 128))
    gap = rows_of((128, 256)) - lanes_of((128, 256)) % 128
    second = jnp.where(jnp.abs(gap) == 1, 16.0, jnp.where(jnp.abs(gap) == 2, -1.0, 0.0))
    first = jnp.where(gap == 1, 8.0, jnp.where(gap == -1, -8.0, jnp.where(gap == 2, -1.0, jnp.where(gap == -2, 1.0, 0.0))))
    weights = jnp.where(lanes_of((128, 256)) < 128, second, first).astype(jnp.bfloat16)
    for row in range(8):
        value = tiles_ref[rows(PAD + row * planes, planes), :]
        deriv_ref[rows(row * planes, planes), :] = exact_dot(value, weights)

    def one(index, _):
        case, block = index // (depth // 8), index % (depth // 8)
        k = layer + 8 * block
        height = (k.astype(jnp.float32) + 0.5) / depth
        offsets = [pl.multiple_of((c * cases + case) * depth + 8 * block, 8) for c in range(4)]
        tiles = [[tiles_ref[rows(PAD + row * planes + offsets[c]), :] for row in range(8)] for c in range(4)]

        for row in range(8):

            def coef(i):
                return coef_ref[pl.ds((case * N_COEF + i) * 8 + row, 1), :]

            along = []
            for c in range(4):
                near = [tiles[c][row + by] if 0 <= row + by < 8 else None for by in (-2, -1, 1, 2)]
                along.append(near)

            def first_x(c):
                m2, m1, p1, p2 = along[c]
                ones = 8.0 * (p1 - m1) if m1 is not None and p1 is not None else 8.0 * p1 if m1 is None else -8.0 * m1
                if m2 is not None and p2 is not None:
                    return ones - (p2 - m2)
                return ones - p2 if m2 is None else ones + m2

            def second_x(c):
                m2, m1, p1, p2 = along[c]
                ones = 16.0 * (p1 + m1) if m1 is not None and p1 is not None else 16.0 * (p1 if m1 is None else m1)
                if m2 is not None and p2 is not None:
                    return ones - (p2 + m2)
                return ones - (p2 if m2 is None else m2)

            carry = coef(CARRY) * height
            sound = coef(SOUND_STEP)
            step = coef(STEP)
            slopes = [first_x(c) for c in range(4)]
            for c in range(4):
                here = row * planes + offsets[c]
                behind = jnp.where(k > 0, tiles_ref[rows(PAD - 1 + here), :], 0.0)
                beyond = jnp.where(k < depth - 1, tiles_ref[rows(PAD + 1 + here), :], 0.0)
                source = source_ref[strided(offsets[c] * 8 + row), :]
                w = WEIGHT[c]
                value = coef(CENTER + w) * tiles[c][row] + coef(SPREAD + w) * (second_x(c) + deriv_ref[rows(here), 0:128])
                value += coef(ACROSS + w) * (behind + beyond) + step * source + carry * slopes[c]
                if c == 0:
                    other = row * planes + offsets[2]
                    value += sound * (slopes[1] + deriv_ref[rows(other), 128:256])
                elif c == 1:
                    value += sound * slopes[0]
                elif c == 2:
                    other = row * planes + offsets[0]
                    value += sound * deriv_ref[rows(other), 128:256]
                else:
                    value += coef(HEAT) * tiles[1][row]
                out_ref[rows(here), :] = value
        return 0

    lax.fori_loop(0, cases * (depth // 8), one, 0)

    if cols_ref:
        columns = edge_columns()
        group = (depth - 1) - rows_of((depth, 128))
        for row in range(8):
            edges = exact_dot(out_ref[rows(row * planes, planes), :], columns)
            for pair in range(4 * cases):
                kept = jnp.where(lanes_of((depth, 128)) // 4 == group, edges[pair * depth : (pair + 1) * depth], 0.0)
                cols_ref[0][pl.ds(pair * 8 + row, 1), :] = jnp.sum(kept, axis=0, keepdims=True)


def packed_coef(packed_ref, case):
    return [packed_ref[rows((case * N_PACKED + i) * 8), :] for i in range(N_PACKED)]


def columns_beyond(cases, side_ref, mask_ref, packed_ref, corr_ref):
    slot = lanes_of((8, 128)) % 4
    for case in range(cases):
        coefs = packed_coef(packed_ref, case)
        second, first = [], []
        for c in range(4):
            side = side_ref[rows((c * cases + case) * 8), :] * mask_ref[...]
            p1 = jnp.where(slot == 1, pltpu.roll(side, 127, 1), 0.0)
            p2 = jnp.where(slot < 2, pltpu.roll(side, 126, 1), 0.0)
            m1 = jnp.where(slot == 2, pltpu.roll(side, 1, 1), 0.0)
            m2 = jnp.where(slot >= 2, pltpu.roll(side, 2, 1), 0.0)
            second.append(16.0 * (p1 + m1) - (p2 + m2))
            first.append(8.0 * (p1 - m1) - (p2 - m2))
        for c in range(4):
            value = coefs[WEIGHT[c]] * second[c]
            if c == 0:
                value += coefs[4] * first[2]
            elif c == 2:
                value += coefs[4] * first[0]
            corr_ref[rows((c * cases + case) * 8), :] = value


def packed_edges(cases, planes, edge_ref, corr_ref, below_ref, above_ref, packed_ref, cols_ref, halo_ref):
    row = rows_of((8, 128))
    for i in range(2):
        halo_ref[strided(6 + i), :] = below_ref[rows(2 * planes + 8 * i), :]
        halo_ref[strided(i), :] = above_ref[rows(2 * planes + 8 * i), :]
    for case in range(cases):
        coefs = packed_coef(packed_ref, case)
        second, first = [], []
        for c in range(4):
            halo = halo_ref[rows((c * cases + case) * 8), :]
            m1 = pltpu.roll(jnp.where(row == 7, halo, 0.0), 1, 0)
            m2 = pltpu.roll(jnp.where(row >= 6, halo, 0.0), 2, 0)
            p1 = pltpu.roll(jnp.where(row == 0, halo, 0.0), 7, 0)
            p2 = pltpu.roll(jnp.where(row < 2, halo, 0.0), 6, 0)
            second.append(16.0 * (p1 + m1) - (p2 + m2))
            first.append(8.0 * (p1 - m1) - (p2 - m2))
        for c in range(4):
            here = rows((c * cases + case) * 8)
            value = edge_ref[here, :] + corr_ref[here, :] + coefs[WEIGHT[c]] * second[c] + coefs[3] * first[c]
            if c < 2:
                value += coefs[4] * first[1 - c]
            cols_ref[here, :] = value


def whole_rows(depth, cases, planes, inner_ref, below_ref, above_ref, coef_ref, corr_ref, lane, layer, store):
    edge = (lane < 2) | (lane >= 126)

    def one(case, _):
        for block in range(depth // 8):
            tile_rows(case, block)
        return 0

    def tile_rows(case, block):
        height = ((layer + 8 * block).astype(jnp.float32) + 0.5) / depth
        offsets = [pl.multiple_of((c * cases + case) * depth + 8 * block, 8) for c in range(4)]
        arrived = [
            [ref[rows(i * planes + offsets[c]), :] for ref in (below_ref, above_ref) for i in range(2)] for c in range(4)
        ]
        for row in (0, 1, 6, 7, 2, 3, 4, 5):

            def coef(i):
                return coef_ref[pl.ds((case * N_COEF + i) * 8 + row, 1), :]

            second, first = [], []
            for c in range(4):
                m2, m1, p1, p2 = arrived[c]
                if row == 0:
                    second.append(16.0 * m1 - m2)
                    first.append(m2 - 8.0 * m1)
                elif row == 1:
                    second.append(-m1)
                    first.append(m1)
                elif row == 6:
                    second.append(-p1)
                    first.append(-p1)
                elif row == 7:
                    second.append(16.0 * p1 - p2)
                    first.append(8.0 * p1 - p2)
            for c in range(4):
                value = inner_ref[rows(row * planes + offsets[c]), :]
                if second:
                    value += coef(SPREAD + WEIGHT[c]) * second[c] + coef(CARRY) * height * first[c]
                    if c < 2:
                        value += coef(SOUND_STEP) * first[1 - c]
                line = corr_ref[pl.ds((c * cases + case) * 8 + row, 1), :]
                moved = pltpu.roll(jnp.broadcast_to(line, (8, 128)), 2 + 32 * block, 1, stride=4, stride_axis=0)
                store(c, case, block, row, offsets[c], value + jnp.where(edge, moved, 0.0))

    lax.fori_loop(0, cases, one, 0)


def joined_kernel(
    depth,
    cases,
    inner_ref,
    edge_ref,
    below_ref,
    above_ref,
    side_ref,
    mask_ref,
    coef_ref,
    packed_ref,
    tiles_ref,
    up_ref,
    down_ref,
    cols_ref,
    corr_ref,
    halo_ref,
):
    planes = 4 * cases * depth
    lane, layer = lanes_of((8, 128)), rows_of((8, 128))
    columns_beyond(cases, side_ref, mask_ref, packed_ref, corr_ref)
    packed_edges(cases, planes, edge_ref, corr_ref, below_ref, above_ref, packed_ref, cols_ref, halo_ref)
    send_edges(cols_ref, up_ref, down_ref, planes)

    def store(c, case, block, row, offset, value):
        tiles_ref[rows(PAD + row * planes + offset), :] = value
        if row < 2:
            down_ref[rows(row * planes + offset), :] = value
        if row > 5:
            up_ref[rows((row - 6) * planes + offset), :] = value

    whole_rows(depth, cases, planes, inner_ref, below_ref, above_ref, coef_ref, corr_ref, lane, layer, store)


def final_kernel(
    depth,
    cases,
    inner_ref,
    below_ref,
    above_ref,
    side_ref,
    mask_ref,
    coef_ref,
    packed_ref,
    out_ref,
    mean_ref,
    wall_ref,
    corr_ref,
    density_ref,
    momentum_ref,
    bend_ref,
):
    planes = 4 * cases * depth
    lane, layer = lanes_of((8, 128)), rows_of((8, 128))
    columns_beyond(cases, side_ref, mask_ref, packed_ref, corr_ref)
    span = depth + 16

    def store(c, case, block, row, offset, value):
        out_ref[strided(offset * 8 + row), :] = value
        if c == 0:
            density_ref[rows(pl.multiple_of((case * 8 + row) * depth + 8 * block, 8)), :] = value
        if c == 1:
            momentum_ref[rows(pl.multiple_of((case * 8 + row) * span + 8 + 8 * block, 8)), :] = value

    whole_rows(depth, cases, planes, inner_ref, below_ref, above_ref, coef_ref, corr_ref, lane, layer, store)
    zero = jnp.zeros((8, 128), jnp.float32)
    for line in range(cases * 8):
        total, bend = zero, zero
        momentum_ref[rows(line * span), :] = zero
        momentum_ref[rows(line * span + 8 + depth), :] = zero
        for block in range(depth // 8):
            total += density_ref[rows(line * depth + 8 * block), :]
        for block in range(depth // 8 + 1):
            at = line * span + 8 + 8 * block
            change = momentum_ref[rows(at), :] - momentum_ref[rows(at - 1), :]
            bend += change * change
        mean_ref[pl.ds(line, 1), :] = jnp.sum(total, axis=0, keepdims=True)
        bend_ref[pl.ds(line, 1), :] = jnp.sum(bend, axis=0, keepdims=True)
    wall = zero
    for case in range(cases):
        wall += coef_ref[rows((case * N_COEF + BEND) * 8), :] * bend_ref[rows(case * 8), :]
    wall_ref[...] = wall


def wall_kernel(cases, wall_ref, mean_ref, below_ref, above_ref, coef_ref, grad_ref, sums_ref):
    row = rows_of((8, 128))
    grad = wall_ref[...]
    for case in range(cases):
        mean = mean_ref[rows(case * 8), :]
        halo = jnp.where(row >= 4, below_ref[rows(case * 8), :], above_ref[rows(case * 8), :])
        m1 = pltpu.roll(jnp.where(row == 7, halo, mean), 1, 0)
        m2 = pltpu.roll(jnp.where(row >= 6, halo, mean), 2, 0)
        p1 = pltpu.roll(jnp.where(row == 0, halo, mean), 7, 0)
        p2 = pltpu.roll(jnp.where(row < 2, halo, mean), 6, 0)
        grad += coef_ref[rows((case * N_COEF + FLUX) * 8), :] * (8.0 * (p1 - m1) - (p2 - m2))
    grad_ref[...] = grad
    part = jnp.sum(grad * grad, axis=0, keepdims=True)
    sums_ref[...] = jnp.broadcast_to(part[None], sums_ref.shape)


def scale_kernel(cells, grad_ref, sums_ref, out_ref):
    total = jnp.sum(sums_ref[...], axis=0)
    total = jnp.sum(total, axis=1, keepdims=True)
    out_ref[...] = grad_ref[...] / jnp.sqrt(total / cells + 1e-06)


def f32(*shape):
    return jax.ShapeDtypeStruct(shape, jnp.float32)


def call(kernel, *args, outs, scratch=(), smem=0):
    return pl.pallas_call(
        kernel,
        out_shape=outs,
        in_specs=[SM] * smem + [VM] * (len(args) - smem),
        out_specs=tuple([VM] * len(outs)),
        scratch_shapes=[pltpu.VMEM(shape, jnp.float32) for shape in scratch],
        compiler_params=PARAMS,
    )(*args)


def neighbours(axis):
    size = lax.axis_size(axis)
    up = [(i, i + 1) for i in range(size - 1)]
    return up, [(j, i) for i, j in up]


def exchange_rows(up, down):
    ahead, back = neighbours("roll")
    return lax.ppermute(up, "roll", ahead), lax.ppermute(down, "roll", back)


def exchange_columns(cols):
    ahead, back = neighbours("trans")
    if lax.axis_size("trans") == 2:
        return lax.ppermute(cols, "trans", ahead + back)
    left, right = lax.ppermute(cols, "trans", ahead), lax.ppermute(cols, "trans", back)
    return jnp.where(lanes_of(cols.shape) % 4 < 2, left, right)


def on_device(adjoint, source, pressure, film, cavity, temp_index):
    components, cases, depth, width_x, width_y = adjoint.shape
    planes = components * cases * depth
    assert (components, width_x, width_y, 4 * depth) == (4, 8, 128, 128)
    state = adjoint.reshape(planes * 8, 128)
    forcing = source.reshape(planes * 8, 128)
    place = jnp.stack([lax.axis_index("trans"), lax.axis_size("trans")]).astype(jnp.int32)
    whole, inner = f32(planes * 8 + 2 * PAD, 128), f32(planes * 8, 128)
    message, cols_shape = f32(planes * 2 + 16, 128), f32(components * cases * 8, 128)
    coef, packed, mask = call(
        functools.partial(coefficient_kernel, depth, cases),
        temp_index,
        place,
        pressure.reshape(cases * 8, 128),
        film,
        cavity.reshape(cases * 8, 128),
        outs=(f32(cases * N_COEF * 8, 128), f32(cases * N_PACKED * 8, 128), f32(8, 128)),
        smem=2,
    )
    tiles, up, down, cols = call(
        functools.partial(pack_kernel, depth, cases), state, outs=(whole, message, message, cols_shape)
    )
    for index in range(SECTIONS):
        below, above = exchange_rows(up, down)
        side = exchange_columns(cols)
        more = index < SECTIONS - 1
        part, *edges = call(
            functools.partial(inner_kernel, depth, cases),
            tiles,
            forcing,
            coef,
            outs=(inner, cols_shape) if more else (inner,),
            scratch=[(planes * 8, 256)],
        )
        arrived = (part, *edges, below, above, side, mask, coef, packed)
        if more:
            tiles, up, down, cols = call(
                functools.partial(joined_kernel, depth, cases),
                *arrived,
                outs=(whole, message, message, cols_shape),
                scratch=[cols_shape.shape] * 2,
            )
        else:
            state, mean, wall = call(
                functools.partial(final_kernel, depth, cases),
                *arrived,
                outs=(inner, f32(cases * 8, 128), f32(8, 128)),
                scratch=[
                    cols_shape.shape,
                    (cases * 8 * depth, 128),
                    (cases * 8 * (depth + 16), 128),
                    (cases * 8, 128),
                ],
            )
    below, above = exchange_rows(mean, mean)
    devices = lax.axis_size("roll") * lax.axis_size("trans")
    grad, sums = call(
        functools.partial(wall_kernel, cases), wall, mean, below, above, coef, outs=(f32(8, 128), f32(devices, 1, 128))
    )
    sums = lax.all_to_all(sums, ("roll", "trans"), 0, 0, tiled=True)
    (wall_step,) = call(functools.partial(scale_kernel, devices * width_x * width_y), grad, sums, outs=(f32(8, 128),))
    return (state.reshape(adjoint.shape), wall_step)


def solution(mesh):
    placed = (
        P(None, None, None, "roll", "trans"),
        P(None, None, None, "roll", "trans"),
        P(None, "roll", "trans"),
        P("roll", "trans"),
        P(None, "roll", "trans"),
        P(),
    )
    return jax.shard_map(
        on_device,
        mesh=mesh,
        in_specs=placed,
        out_specs=(P(None, None, None, "roll", "trans"), P("roll", "trans")),
        check_vma=False,
    )
```

time: 145 us -> 51.1 us (0.35)
  local copies, waits for them, and re-layouts: 35.3 us -> 1.32 us
  other arithmetic: 28.4 us -> 0.07 us
  blocking collectives: 44.2 us -> 17.1 us
  starting transfers between devices: 33 us -> 21.3 us
  Pallas kernels: 0 us -> 8.86 us
    psum x1 -> x0, blocking collectives: 44.2 us -> none  [on_device(): total = lax.psum(jnp.sum(wall_grad * wall_grad), ('roll', 'trans'))]
    all_to_all x0 -> x1, blocking collectives: none -> 17.1 us  [on_device(): sums = lax.all_to_all(sums, ('roll', 'trans'), 0, 0, tiled=True)]
    unnamed x65 -> x12, local copies, waits for them, and re-layouts: 13.8 us -> 1.32 us
    ppermute x10 -> x8, starting transfers between devices: 33 us -> 21.3 us  [the longest x6 17.3 us: exchange_rows(): return (lax.ppermute(up, 'roll', ahead), lax.ppermute(down, 'roll', back))]
    ppermute x6 -> x0, local copies, waits for them, and re-layouts: 11.7 us -> none  [the longest x3 5.96 us: extended(): before = lax.ppermute(last, axis, up)]
    div x8 -> x0, other arithmetic: 11.7 us -> none  [the longest x2 7.83 us: time_section(): (-along_y(2) + 8.0 * along_y(1) - 8.0 * along_y(-1) + along_y(-2)) / 12.0]
    add x6 -> x0, other arithmetic: 9.29 us -> none  [the longest x2 7.57 us: time_section(): diffused = fluid_viscosity * (second_x + second_y) + film_coef * second_z]
    pallas_call x0 -> x8, Pallas kernels: none -> 8.86 us  [call(): pl.pallas_call(kernel, out_shape=outs, in_specs=[SM] * smem + [VM] * (len...]
  transfers between devices with their start and end apart: 10 -> 8, of which waited for: 2 -> 2; matrix products, arithmetic and copies ran while one was open for 17% -> 0% of each run, Pallas kernels for 0% -> 10%
where the time goes in v2:
time: 51.1 us; the launch traced here: 50.8 us
  starting transfers between devices  21.3 us (42%)
  blocking collectives  17.1 us (33%)
  Pallas kernels  8.86 us (17%)
  waiting for transfers between devices  1.42 us (3%)
  local copies, waits for them, and re-layouts  1.32 us (3%)
  between operations  0.78 us (2%)
    ppermute x6, starting transfers between devices, exchange_rows(): return (lax.ppermute(up, 'roll', ahead), lax.ppermute(down, 'roll', back))  17.3 us
    all_to_all x1, blocking collectives, on_device(): sums = lax.all_to_all(sums, ('roll', 'trans'), 0, 0, tiled=True)  17.1 us
    pallas_call x8, Pallas kernels, call(): pl.pallas_call(kernel, out_shape=outs, in_specs=[SM] * smem + [VM] * (len...  8.86 us
    ppermute x2, starting transfers between devices, exchange_columns(): return lax.ppermute(cols, 'trans', ahead + back)  3.94 us
    unnamed x12, local copies, waits for them, and re-layouts  1.32 us
  transfers between devices with their start and end apart: 8, of which 2 were waited for; matrix products, arithmetic and copies ran while one was open for 0% of the time, Pallas kernels for 10%

profile of v2, /device:TPU:0, one launch (start us, length us, event | category | flops | bytes accessed | tf_op | source)
XLA Modules:
  0.0 50.8 jit_solution(11309719955433100862)
XLA Ops:
  0.7 1.3 %copy-done.1 = f32[4,2,32,8,128]{4,3,2,1,0:T(8,128)S(1)} copy-done((f32[4,2,32,8,128]{4,3,2,1,0:T(8,128)S(1)}, f32[4,2,32,8,128]{4,3,2,1,0:T(8,128)}, u32[]{:S(2)}) %copy-start.1) | copy-done | bytes 1048600
  2.0 1.0 %shard_map.77 = (f32[2064,128]{1,0:T(8,128)S(1)}, f32[528,128]{1,0:T(8,128)S(1)}, f32[528,128]{1,0:T(8,128)S(1)}, f32[64,128]{1,0:T(8,128)S(1)}) custom-call(f32[2048,128]{1,0:T(8,128)S(1)} %bitcast.8), custom_call_target="tpu_custom_call" | custom-call | tf_op jit(solution)/shard_map/pallas_call | solution.py:422
  3.0 2.4 %collective-permute-start = (f32[528,128]{1,0:T(8,128)S(1)}, f32[528,128]{1,0:T(8,128)S(1)}, u32[]{:S(2)}, u32[]{:S(2)}) collective-permute-start(f32[528,128]{1,0:T(8,128)S(1)} %get-tuple-element.24), channel_id=1, source_target_pairs={{0,2},{2,4},{4,6},{6,8},{8,10},{10,12},{12,14},{14,16},{16,18},{18... | collective-permute-start | bytes 811016 | tf_op jit(solution)/shard_map/ppermute | solution.py:440
  5.4 1.3 %collective-permute-start.1 = (f32[528,128]{1,0:T(8,128)S(1)}, f32[528,128]{1,0:T(8,128)S(1)}, u32[]{:S(2)}, u32[]{:S(2)}) collective-permute-start(f32[528,128]{1,0:T(8,128)S(1)} %get-tuple-element.25), channel_id=1, source_target_pairs={{2,0},{4,2},{6,4},{8,6},{10,8},{12,10},{14,12},{16,14},{18,16},{20... | collective-permute-start | bytes 811016 | tf_op jit(solution)/shard_map/ppermute | solution.py:440
  6.7 2.4 %collective-permute-start.2 = (f32[64,128]{1,0:T(8,128)S(1)}, f32[64,128]{1,0:T(8,128)S(1)}, u32[]{:S(2)}, u32[]{:S(2)}) collective-permute-start(f32[64,128]{1,0:T(8,128)S(1)} %get-tuple-element.26), channel_id=1, source_target_pairs={{0,1},{1,0},{2,3},{3,2},{4,5},{5,4},{6,7},{7,6},{8,9},{9,8},{10,11... | collective-permute-start | bytes 98312 | tf_op jit(solution)/shard_map/ppermute | solution.py:446
  9.0 0.1 pad_add_fusion.place_ref
  9.1 0.7 %shard_map.78 = (f32[240,128]{1,0:T(8,128)S(1)}, f32[80,128]{1,0:T(8,128)S(1)}, f32[8,128]{1,0:T(8,128)S(1)}) custom-call(s32[2]{0:T(128)S(1)} %copy-done.5, s32[2]{0:T(128)S(1)} %pad_add_fusion.place_ref, f32[16,128]{1,0:T(8,128)S(1)} %bitcast.9, f32[8,128]{1,0:T(8,128)S(1)} %copy-done.4, s32[16,128]{1,0:T(8,128)S(1)} %bitcast.10), custom_call_target="tpu_custom_call" | custom-call | tf_op jit(solution)/shard_map/pallas_call | solution.py:422
  9.9 2.5 %shard_map.79 = (f32[2048,128]{1,0:T(8,128)S(1)}, f32[64,128]{1,0:T(8,128)S(1)}) custom-call(f32[2064,128]{1,0:T(8,128)S(1)} %get-tuple-element.20.tiles_ref, f32[2048,128]{1,0:T(8,128)S(1)} %bitcast.6, f32[240,128]{1,0:T(8,128)S(1)} %get-tuple-element.21.coef_ref), custom_call_target="tpu_custom_call" | custom-call | tf_op jit(solution)/shard_map/pallas_call | solution.py:422
  12.3 0.0 collective-permute-done.2.side_ref
  12.4 0.0 collective-permute-done.below_ref
  12.4 0.5 %shard_map.80 = (f32[2064,128]{1,0:T(8,128)S(1)}, f32[528,128]{1,0:T(8,128)S(1)}, f32[528,128]{1,0:T(8,128)S(1)}, f32[64,128]{1,0:T(8,128)S(1)}) custom-call(f32[2048,128]{1,0:T(8,128)S(1)} %get-tuple-element.22.inner_ref, f32[64,128]{1,0:T(8,128)S(1)} %get-tuple-element.23.edge_ref, f32[528,128]{1,0:T(8,128)S(1)} %collective-permute-done.below_ref, ...), custom_call_target="tpu_custom_call" | custom-call | tf_op jit(solution)/shard_map/pallas_call | solution.py:422
  12.9 5.3 %collective-permute-start.3 = (f32[528,128]{1,0:T(8,128)S(1)}, f32[528,128]{1,0:T(8,128)S(1)}, u32[]{:S(2)}, u32[]{:S(2)}) collective-permute-start(f32[528,128]{1,0:T(8,128)S(1)} %get-tuple-element.30), channel_id=1, source_target_pairs={{0,2},{2,4},{4,6},{6,8},{8,10},{10,12},{12,14},{14,16},{16,18},{18... | collective-permute-start | bytes 811016 | tf_op jit(solution)/shard_map/ppermute | solution.py:440
  18.2 1.3 %collective-permute-start.4 = (f32[528,128]{1,0:T(8,128)S(1)}, f32[528,128]{1,0:T(8,128)S(1)}, u32[]{:S(2)}, u32[]{:S(2)}) collective-permute-start(f32[528,128]{1,0:T(8,128)S(1)} %get-tuple-element.31), channel_id=1, source_target_pairs={{2,0},{4,2},{6,4},{8,6},{10,8},{12,10},{14,12},{16,14},{18,16},{20... | collective-permute-start | bytes 811016 | tf_op jit(solution)/shard_map/ppermute | solution.py:440
  19.5 1.6 %collective-permute-start.5 = (f32[64,128]{1,0:T(8,128)S(1)}, f32[64,128]{1,0:T(8,128)S(1)}, u32[]{:S(2)}, u32[]{:S(2)}) collective-permute-start(f32[64,128]{1,0:T(8,128)S(1)} %get-tuple-element.32), channel_id=1, source_target_pairs={{0,1},{1,0},{2,3},{3,2},{4,5},{5,4},{6,7},{7,6},{8,9},{9,8},{10,11... | collective-permute-start | bytes 98312 | tf_op jit(solution)/shard_map/ppermute | solution.py:446
  21.1 1.8 %shard_map.81.inner_ref = f32[2048,128]{1,0:T(8,128)S(1)} custom-call(f32[2064,128]{1,0:T(8,128)S(1)} %get-tuple-element.29.tiles_ref, f32[2048,128]{1,0:T(8,128)S(1)} %bitcast.7, f32[240,128]{1,0:T(8,128)S(1)} %get-tuple-element.21.coef_ref), custom_call_target="tpu_custom_call" | custom-call | tf_op jit(solution)/shard_map/pallas_call | solution.py:422
  22.9 0.6 %collective-permute-done.5.side_ref = f32[64,128]{1,0:T(8,128)S(1)} collective-permute-done((f32[64,128]{1,0:T(8,128)S(1)}, f32[64,128]{1,0:T(8,128)S(1)}, u32[]{:S(2)}, u32[]{:S(2)}) %collective-permute-start.5) | collective-permute-done | bytes 32800 | tf_op jit(solution)/shard_map/ppermute | solution.py:446
  23.5 0.0 collective-permute-done.3.below_ref
  23.5 0.0 collective-permute-done.4.above_ref
  23.5 1.6 %shard_map.82 = (f32[2048,128]{1,0:T(8,128)}, f32[16,128]{1,0:T(8,128)S(1)}, f32[8,128]{1,0:T(8,128)S(1)}) custom-call(f32[2048,128]{1,0:T(8,128)S(1)} %shard_map.81.inner_ref, f32[528,128]{1,0:T(8,128)S(1)} %collective-permute-done.3.below_ref, f32[528,128]{1,0:T(8,128)S(1)} %collective-permute-done.4.above_ref, ...), custom_call_target="tpu_custom_call" | custom-call | tf_op jit(solution)/shard_map/pallas_call | solution.py:422
  25.1 1.3 %collective-permute-start.7 = (f32[16,128]{1,0:T(8,128)S(1)}, f32[16,128]{1,0:T(8,128)S(1)}, u32[]{:S(2)}, u32[]{:S(2)}) collective-permute-start(f32[16,128]{1,0:T(8,128)S(1)} %get-tuple-element.35.mean_ref), channel_id=1, source_target_pairs={{2,0},{4,2},{6,4},{8,6},{10,8},{12,10},{14,12},{16,14},{18,16},{20... | collective-permute-start | bytes 24584 | tf_op jit(solution)/shard_map/ppermute | solution.py:440
  26.4 5.8 %collective-permute-start.6 = (f32[16,128]{1,0:T(8,128)S(1)}, f32[16,128]{1,0:T(8,128)S(1)}, u32[]{:S(2)}, u32[]{:S(2)}) collective-permute-start(f32[16,128]{1,0:T(8,128)S(1)} %get-tuple-element.35.mean_ref), channel_id=1, source_target_pairs={{0,2},{2,4},{4,6},{6,8},{8,10},{10,12},{12,14},{14,16},{16,18},{18... | collective-permute-start | bytes 24584 | tf_op jit(solution)/shard_map/ppermute | solution.py:440
  32.2 0.8 %collective-permute-done.6.below_ref = f32[16,128]{1,0:T(8,128)S(1)} collective-permute-done((f32[16,128]{1,0:T(8,128)S(1)}, f32[16,128]{1,0:T(8,128)S(1)}, u32[]{:S(2)}, u32[]{:S(2)}) %collective-permute-start.6) | collective-permute-done | bytes 8224 | tf_op jit(solution)/shard_map/ppermute | solution.py:440
  33.0 17.1 %all_to_all.5.sums_ref = f32[32,1,128]{2,1,0:T(1,128)S(1)} all-to-all(f32[32,1,128]{2,1,0:T(1,128)S(1)} %get-tuple-element.37), channel_id=1, replica_groups=mesh['roll'=16,'trans'=2] {'roll','trans'}, dimensions={0} | all-to-all | bytes 32768 | tf_op jit(solution)/shard_map/all_to_all | solution.py:510
  50.1 0.7 %shard_map.84 = f32[8,128]{1,0:T(8,128)} custom-call(f32[8,128]{1,0:T(8,128)S(1)} %get-tuple-element.36.grad_ref, f32[32,1,128]{2,1,0:T(1,128)S(1)} %all_to_all.5.sums_ref), custom_call_target="tpu_custom_call" | custom-call | tf_op jit(solution)/shard_map/pallas_call | solution.py:422
  (14 shorter events, 0.1 us)
Async XLA Ops:
  0.6 9.2 %copy-start = (f32[4,2,32,8,128]{4,3,2,1,0:T(8,128)S(1)}, f32[4,2,32,8,128]{4,3,2,1,0:T(8,128)}, u32[]{:S(2)}) copy-start(f32[4,2,32,8,128]{4,3,2,1,0:T(8,128)} %param.7) | copy-start | bytes 3145732
  0.6 1.3 %copy-start.1 = (f32[4,2,32,8,128]{4,3,2,1,0:T(8,128)S(1)}, f32[4,2,32,8,128]{4,3,2,1,0:T(8,128)}, u32[]{:S(2)}) copy-start(f32[4,2,32,8,128]{4,3,2,1,0:T(8,128)} %param.6) | copy-start | bytes 3145732
  2.0 7.2 %copy-start.2 = (f32[2,8,128]{2,1,0:T(8,128)S(1)}, f32[2,8,128]{2,1,0:T(8,128)}, u32[]{:S(2)}) copy-start(f32[2,8,128]{2,1,0:T(8,128)} %param.8) | copy-start | bytes 24580
  2.0 7.2 %copy-start.3 = (s32[2,8,128]{2,1,0:T(8,128)S(1)}, s32[2,8,128]{2,1,0:T(8,128)}, u32[]{:S(2)}) copy-start(s32[2,8,128]{2,1,0:T(8,128)} %param.10) | copy-start | bytes 24580
  2.0 7.2 %copy-start.4 = (f32[8,128]{1,0:T(8,128)S(1)}, f32[8,128]{1,0:T(8,128)}, u32[]{:S(2)}) copy-start(f32[8,128]{1,0:T(8,128)} %film_ref.1) | copy-start | bytes 12292
  2.0 7.2 %copy-start.5 = (s32[2]{0:T(128)S(1)}, s32[2]{0:T(128)}, u32[]{:S(2)}) copy-start(s32[2]{0:T(128)} %level_ref.1) | copy-start | bytes 28
  3.0 9.4 %collective-permute-start = (f32[528,128]{1,0:T(8,128)S(1)}, f32[528,128]{1,0:T(8,128)S(1)}, u32[]{:S(2)}, u32[]{:S(2)}) collective-permute-start(f32[528,128]{1,0:T(8,128)S(1)} %get-tuple-element.24), channel_id=1, source_target_pairs={{0,2},{2,4},{4,6},{6,8},{8,10},{10,12},{12,14},{14,16},{16,18},{18... | collective-permute-start | bytes 811016 | tf_op jit(solution)/shard_map/ppermute | solution.py:440
  5.4 7.0 %collective-permute-start.1 = (f32[528,128]{1,0:T(8,128)S(1)}, f32[528,128]{1,0:T(8,128)S(1)}, u32[]{:S(2)}, u32[]{:S(2)}) collective-permute-start(f32[528,128]{1,0:T(8,128)S(1)} %get-tuple-element.25), channel_id=1, source_target_pairs={{2,0},{4,2},{6,4},{8,6},{10,8},{12,10},{14,12},{16,14},{18,16},{20... | collective-permute-start | bytes 811016 | tf_op jit(solution)/shard_map/ppermute | solution.py:440
  6.7 5.7 %collective-permute-start.2 = (f32[64,128]{1,0:T(8,128)S(1)}, f32[64,128]{1,0:T(8,128)S(1)}, u32[]{:S(2)}, u32[]{:S(2)}) collective-permute-start(f32[64,128]{1,0:T(8,128)S(1)} %get-tuple-element.26), channel_id=1, source_target_pairs={{0,1},{1,0},{2,3},{3,2},{4,5},{5,4},{6,7},{7,6},{8,9},{9,8},{10,11... | collective-permute-start | bytes 98312 | tf_op jit(solution)/shard_map/ppermute | solution.py:446
  12.9 10.6 %collective-permute-start.3 = (f32[528,128]{1,0:T(8,128)S(1)}, f32[528,128]{1,0:T(8,128)S(1)}, u32[]{:S(2)}, u32[]{:S(2)}) collective-permute-start(f32[528,128]{1,0:T(8,128)S(1)} %get-tuple-element.30), channel_id=1, source_target_pairs={{0,2},{2,4},{4,6},{6,8},{8,10},{10,12},{12,14},{14,16},{16,18},{18... | collective-permute-start | bytes 811016 | tf_op jit(solution)/shard_map/ppermute | solution.py:440
  18.2 5.3 %collective-permute-start.4 = (f32[528,128]{1,0:T(8,128)S(1)}, f32[528,128]{1,0:T(8,128)S(1)}, u32[]{:S(2)}, u32[]{:S(2)}) collective-permute-start(f32[528,128]{1,0:T(8,128)S(1)} %get-tuple-element.31), channel_id=1, source_target_pairs={{2,0},{4,2},{6,4},{8,6},{10,8},{12,10},{14,12},{16,14},{18,16},{20... | collective-permute-start | bytes 811016 | tf_op jit(solution)/shard_map/ppermute | solution.py:440
  19.5 4.0 %collective-permute-start.5 = (f32[64,128]{1,0:T(8,128)S(1)}, f32[64,128]{1,0:T(8,128)S(1)}, u32[]{:S(2)}, u32[]{:S(2)}) collective-permute-start(f32[64,128]{1,0:T(8,128)S(1)} %get-tuple-element.32), channel_id=1, source_target_pairs={{0,1},{1,0},{2,3},{3,2},{4,5},{5,4},{6,7},{7,6},{8,9},{9,8},{10,11... | collective-permute-start | bytes 98312 | tf_op jit(solution)/shard_map/ppermute | solution.py:446
  25.1 7.1 %collective-permute-start.7 = (f32[16,128]{1,0:T(8,128)S(1)}, f32[16,128]{1,0:T(8,128)S(1)}, u32[]{:S(2)}, u32[]{:S(2)}) collective-permute-start(f32[16,128]{1,0:T(8,128)S(1)} %get-tuple-element.35.mean_ref), channel_id=1, source_target_pairs={{2,0},{4,2},{6,4},{8,6},{10,8},{12,10},{14,12},{16,14},{18,16},{20... | collective-permute-start | bytes 24584 | tf_op jit(solution)/shard_map/ppermute | solution.py:440
  26.4 6.6 %collective-permute-start.6 = (f32[16,128]{1,0:T(8,128)S(1)}, f32[16,128]{1,0:T(8,128)S(1)}, u32[]{:S(2)}, u32[]{:S(2)}) collective-permute-start(f32[16,128]{1,0:T(8,128)S(1)} %get-tuple-element.35.mean_ref), channel_id=1, source_target_pairs={{0,2},{2,4},{4,6},{6,8},{8,10},{10,12},{12,14},{14,16},{16,18},{18... | collective-permute-start | bytes 24584 | tf_op jit(solution)/shard_map/ppermute | solution.py:440

commit v3 on v2

--- a/solution.py
+++ b/solution.py
@@ -28,6 +28,8 @@
 CARRY, SOUND_STEP, STEP, HEAT, FLUX, BEND = range(9, 15)
 N_COEF = 15
 N_PACKED = 5
+TAIL = 24
+TRANS, TRANS_SIZE, ODD, DEVICE = range(4)
 WEIGHT = (0, 1, 1, 2)
 
 
@@ -75,8 +77,8 @@
         for i in range(N_PACKED):
             plane = packed[i * 8 : i * 8 + 8]
             packed_ref[rows((case * N_PACKED + i) * 8), :] = plane * height if i == 3 else plane
-    from_left = jnp.where(place_ref[0] > 0, 1.0, 0.0)
-    from_right = jnp.where(place_ref[0] < place_ref[1] - 1, 1.0, 0.0)
+    from_left = jnp.where(place_ref[TRANS] > 0, 1.0, 0.0)
+    from_right = jnp.where(place_ref[TRANS] < place_ref[TRANS_SIZE] - 1, 1.0, 0.0)
     mask_ref[...] = jnp.where(lane % 4 < 2, from_left, from_right)
 
 
@@ -99,15 +101,33 @@
     return part + jnp.dot(low, weights, preferred_element_type=jnp.float32)
 
 
-def send_edges(cols_ref, up_ref, down_ref, planes):
-    for row in range(2):
-        up_ref[rows(2 * planes + 8 * row), :] = cols_ref[strided(6 + row), :]
-        down_ref[rows(2 * planes + 8 * row), :] = cols_ref[strided(row), :]
-
-
-def pack_kernel(depth, cases, state_ref, tiles_ref, up_ref, down_ref, cols_ref):
+class Post:
+    def __init__(self, place_ref, first_ref, second_ref):
+        self.odd = place_ref[ODD] == 1
+        self.refs = first_ref, second_ref
+
+    def put(self, where, up, down):
+        first, second = self.refs
+        first[where, :] = jnp.where(self.odd, down, up)
+        second[where, :] = jnp.where(self.odd, up, down)
+
+    def get(self, where):
+        first, second = (ref[where, :] for ref in self.refs)
+        return jnp.where(self.odd, first, second), jnp.where(self.odd, second, first)
+
+    def put_tiles(self, planes, first, tiles):
+        for i in range(2):
+            self.put(rows(i * planes + first), tiles[6 + i], tiles[i])
+
+    def put_edges(self, planes, cols_ref):
+        for i in range(2):
+            self.put(rows(2 * planes + 8 * i), cols_ref[strided(6 + i), :], cols_ref[strided(i), :])
+
+
+def pack_kernel(depth, cases, place_ref, state_ref, tiles_ref, first_ref, second_ref, cols_ref):
     planes = 4 * cases * depth
     lane = lanes_of((8, 128))
+    post = Post(place_ref, first_ref, second_ref)
 
     def one(pair, _):
         held = jnp.zeros((8, 128), jnp.float32)
@@ -116,23 +136,20 @@
             plane = state_ref[rows(pl.multiple_of((pair * depth + layer) * 8, 8)), :]
             held = jnp.where(lane // 4 == group, pltpu.roll(plane, (4 * group + 2) % 128, 1), held)
         cols_ref[rows(pl.multiple_of(pair * 8, 8)), :] = held
-        for row in (0, 1, 6, 7, 2, 3, 4, 5):
-            for block in range(depth // 8):
-                first = pl.multiple_of(pair * depth + 8 * block, 8)
-                tile = state_ref[strided(first * 8 + row), :]
-                tiles_ref[rows(PAD + row * planes + first), :] = tile
-                if row < 2:
-                    down_ref[rows(row * planes + first), :] = tile
-                if row > 5:
-                    up_ref[rows((row - 6) * planes + first), :] = tile
+        for block in range(depth // 8):
+            first = pl.multiple_of(pair * depth + 8 * block, 8)
+            tiles = [state_ref[strided(first * 8 + row), :] for row in range(8)]
+            for row in range(8):
+                tiles_ref[rows(PAD + row * planes + first), :] = tiles[row]
+            post.put_tiles(planes, first, tiles)
         return 0
 
     lax.fori_loop(0, 4 * cases, one, 0)
-    send_edges(cols_ref, up_ref, down_ref, planes)
+    post.put_edges(planes, cols_ref)
 
 
 def inner_kernel(depth, cases, tiles_ref, source_ref, coef_ref, *rest):
-    out_ref, *cols_ref, deriv_ref = rest
+    out_ref, *more_refs, deriv_ref = rest
     planes = 4 * cases * depth
     lane, layer = lanes_of((8, 128)), rows_of((8, 128))
     gap = rows_of((128, 256)) - lanes_of((128, 256)) % 128
@@ -201,14 +218,21 @@
 
     lax.fori_loop(0, cases * (depth // 8), one, 0)
 
-    if cols_ref:
+    if more_refs:
+        cols_ref, total_ref = more_refs
+        for case in range(cases):
+            for row in range(8):
+                total = jnp.zeros((8, 128), jnp.float32)
+                for block in range(depth // 8):
+                    total += source_ref[strided((case * depth + 8 * block) * 8 + row), :]
+                total_ref[pl.ds(case * 8 + row, 1), :] = jnp.sum(total, axis=0, keepdims=True)
         columns = edge_columns()
         group = (depth - 1) - rows_of((depth, 128))
         for row in range(8):
             edges = exact_dot(out_ref[rows(row * planes, planes), :], columns)
             for pair in range(4 * cases):
                 kept = jnp.where(lanes_of((depth, 128)) // 4 == group, edges[pair * depth : (pair + 1) * depth], 0.0)
-                cols_ref[0][pl.ds(pair * 8 + row, 1), :] = jnp.sum(kept, axis=0, keepdims=True)
+                cols_ref[pl.ds(pair * 8 + row, 1), :] = jnp.sum(kept, axis=0, keepdims=True)
 
 
 def packed_coef(packed_ref, case):
@@ -237,11 +261,12 @@
             corr_ref[rows((c * cases + case) * 8), :] = value
 
 
-def packed_edges(cases, planes, edge_ref, corr_ref, below_ref, above_ref, packed_ref, cols_ref, halo_ref):
+def packed_edges(cases, planes, edge_ref, corr_ref, post, packed_ref, cols_ref, halo_ref):
     row = rows_of((8, 128))
     for i in range(2):
-        halo_ref[strided(6 + i), :] = below_ref[rows(2 * planes + 8 * i), :]
-        halo_ref[strided(i), :] = above_ref[rows(2 * planes + 8 * i), :]
+        below, above = post.get(rows(2 * planes + 8 * i))
+        halo_ref[strided(6 + i), :] = below
+        halo_ref[strided(i), :] = above
     for case in range(cases):
         coefs = packed_coef(packed_ref, case)
         second, first = [], []
@@ -261,7 +286,7 @@
             cols_ref[here, :] = value
 
 
-def whole_rows(depth, cases, planes, inner_ref, below_ref, above_ref, coef_ref, corr_ref, lane, layer, store):
+def whole_rows(depth, cases, planes, inner_ref, post, coef_ref, corr_ref, lane, layer, store):
     edge = (lane < 2) | (lane >= 126)
 
     def one(case, _):
@@ -272,9 +297,11 @@
     def tile_rows(case, block):
         height = ((layer + 8 * block).astype(jnp.float32) + 0.5) / depth
         offsets = [pl.multiple_of((c * cases + case) * depth + 8 * block, 8) for c in range(4)]
-        arrived = [
-            [ref[rows(i * planes + offsets[c]), :] for ref in (below_ref, above_ref) for i in range(2)] for c in range(4)
-        ]
+        arrived = []
+        for c in range(4):
+            pairs = [post.get(rows(i * planes + offsets[c])) for i in range(2)]
+            arrived.append([pairs[0][0], pairs[1][0], pairs[0][1], pairs[1][1]])
+        whole = [[None] * 8 for _ in range(4)]
         for row in (0, 1, 6, 7, 2, 3, 4, 5):
 
             def coef(i):
@@ -303,115 +330,220 @@
                         value += coef(SOUND_STEP) * first[1 - c]
                 line = corr_ref[pl.ds((c * cases + case) * 8 + row, 1), :]
                 moved = pltpu.roll(jnp.broadcast_to(line, (8, 128)), 2 + 32 * block, 1, stride=4, stride_axis=0)
-                store(c, case, block, row, offsets[c], value + jnp.where(edge, moved, 0.0))
+                whole[c][row] = value + jnp.where(edge, moved, 0.0)
+        for c in range(4):
+            store(c, case, block, offsets[c], whole[c])
 
     lax.fori_loop(0, cases, one, 0)
+
+
+def depth_sum(tiles):
+    total = tiles[0]
+    for tile in tiles[1:]:
+        total = total + tile
+    return jnp.sum(total, axis=0, keepdims=True)
+
+
+def edge_rows(post, planes, place, plane):
+    post.put(pl.ds(2 * planes + place, 2), plane[6:8], plane[0:2])
 
 
 def joined_kernel(
     depth,
     cases,
+    place_ref,
     inner_ref,
     edge_ref,
-    below_ref,
-    above_ref,
+    source_total_ref,
+    first_in_ref,
+    second_in_ref,
     side_ref,
     mask_ref,
     coef_ref,
     packed_ref,
     tiles_ref,
-    up_ref,
-    down_ref,
+    first_ref,
+    second_ref,
     cols_ref,
+    moment_ref,
     corr_ref,
     halo_ref,
 ):
     planes = 4 * cases * depth
     lane, layer = lanes_of((8, 128)), rows_of((8, 128))
+    post, arrived = Post(place_ref, first_ref, second_ref), Post(place_ref, first_in_ref, second_in_ref)
     columns_beyond(cases, side_ref, mask_ref, packed_ref, corr_ref)
-    packed_edges(cases, planes, edge_ref, corr_ref, below_ref, above_ref, packed_ref, cols_ref, halo_ref)
-    send_edges(cols_ref, up_ref, down_ref, planes)
-
-    def store(c, case, block, row, offset, value):
-        tiles_ref[rows(PAD + row * planes + offset), :] = value
-        if row < 2:
-            down_ref[rows(row * planes + offset), :] = value
-        if row > 5:
-            up_ref[rows((row - 6) * planes + offset), :] = value
-
-    whole_rows(depth, cases, planes, inner_ref, below_ref, above_ref, coef_ref, corr_ref, lane, layer, store)
+    packed_edges(cases, planes, edge_ref, corr_ref, arrived, packed_ref, cols_ref, halo_ref)
+
+    def store(c, case, block, offset, tiles):
+        for row in range(8):
+            tiles_ref[rows(PAD + row * planes + offset), :] = tiles[row]
+        post.put_tiles(planes, offset, tiles)
+
+    whole_rows(depth, cases, planes, inner_ref, arrived, coef_ref, corr_ref, lane, layer, store)
+
+    blocks = depth // 8
+    for case in range(cases):
+        for row in range(8):
+
+            def tiles_of(c):
+                start = PAD + row * planes + (c * cases + case) * depth
+                return [tiles_ref[rows(start + 8 * block), :] for block in range(blocks)]
+
+            density, heights = tiles_of(0), [(layer + (8 * block + 0.5)).astype(jnp.float32) / depth for block in range(blocks)]
+            lines = (
+                depth_sum(density),
+                depth_sum([tile * height for tile, height in zip(density, heights, strict=True)]),
+                depth_sum(tiles_of(1)),
+                depth_sum(tiles_of(2)),
+                density[0][0:1] + density[-1][7:8],
+            )
+            for i, line in enumerate(lines):
+                moment_ref[pl.ds((case * 5 + i) * 8 + row, 1), :] = line
+    for case in range(cases):
+
+        def coef(i):
+            return coef_ref[rows((case * N_COEF + i) * 8), :]
+
+        total, lifted, along, across, walls = (moment_ref[rows((case * 5 + i) * 8), :] for i in range(5))
+
+        def x_parts(plane):
+            m1, m2 = jnp.where(layer >= 1, pltpu.roll(plane, 1, 0), 0.0), jnp.where(layer >= 2, pltpu.roll(plane, 2, 0), 0.0)
+            p1, p2 = jnp.where(layer < 7, pltpu.roll(plane, 7, 0), 0.0), jnp.where(layer < 6, pltpu.roll(plane, 6, 0), 0.0)
+            return 16.0 * (p1 + m1) - (p2 + m2), 8.0 * (p1 - m1) - (p2 - m2)
+
+        def y_parts(plane):
+            m1, m2 = jnp.where(lane >= 1, pltpu.roll(plane, 1, 1), 0.0), jnp.where(lane >= 2, pltpu.roll(plane, 2, 1), 0.0)
+            p1, p2 = jnp.where(lane < 127, pltpu.roll(plane, 127, 1), 0.0), jnp.where(lane < 126, pltpu.roll(plane, 126, 1), 0.0)
+            return 16.0 * (p1 + m1) - (p2 + m2), 8.0 * (p1 - m1) - (p2 - m2)
+
+        value = coef(CENTER) * total + coef(SPREAD) * (x_parts(total)[0] + y_parts(total)[0])
+        value += coef(ACROSS) * (2.0 * total - walls) + coef(CARRY) * x_parts(lifted)[1]
+        value += coef(SOUND_STEP) * (x_parts(along)[1] + y_parts(across)[1]) + coef(STEP) * source_total_ref[rows(case * 8), :]
+        sent = (value, coef(SPREAD), coef(CARRY), coef(SOUND_STEP), coef(FLUX))
+        for i, plane in enumerate(sent):
+            edge_rows(post, planes, (case * 5 + i) * 2, plane)
+
+
+def edge_sums(tile):
+    for by in (4, 8, 16, 32, 64):
+        tile = tile + pltpu.roll(tile, by, 1)
+    return pltpu.roll(tile, 2, 1)
 
 
 def final_kernel(
     depth,
     cases,
+    place_ref,
     inner_ref,
-    below_ref,
-    above_ref,
+    first_in_ref,
+    second_in_ref,
     side_ref,
     mask_ref,
     coef_ref,
     packed_ref,
+    moment_ref,
     out_ref,
-    mean_ref,
-    wall_ref,
+    grad_ref,
+    sums_ref,
     corr_ref,
     density_ref,
     momentum_ref,
+    mean_ref,
     bend_ref,
 ):
     planes = 4 * cases * depth
     lane, layer = lanes_of((8, 128)), rows_of((8, 128))
+    arrived = Post(place_ref, first_in_ref, second_in_ref)
     columns_beyond(cases, side_ref, mask_ref, packed_ref, corr_ref)
     span = depth + 16
 
-    def store(c, case, block, row, offset, value):
-        out_ref[strided(offset * 8 + row), :] = value
-        if c == 0:
-            density_ref[rows(pl.multiple_of((case * 8 + row) * depth + 8 * block, 8)), :] = value
-        if c == 1:
-            momentum_ref[rows(pl.multiple_of((case * 8 + row) * span + 8 + 8 * block, 8)), :] = value
-
-    whole_rows(depth, cases, planes, inner_ref, below_ref, above_ref, coef_ref, corr_ref, lane, layer, store)
+    def store(c, case, block, offset, tiles):
+        for row in range(8):
+            out_ref[strided(offset * 8 + row), :] = tiles[row]
+            if c == 0:
+                density_ref[rows(pl.multiple_of((case * 8 + row) * depth + 8 * block, 8)), :] = tiles[row]
+            if c == 1:
+                momentum_ref[rows(pl.multiple_of((case * 8 + row) * span + 8 + 8 * block, 8)), :] = tiles[row]
+
+    whole_rows(depth, cases, planes, inner_ref, arrived, coef_ref, corr_ref, lane, layer, store)
     zero = jnp.zeros((8, 128), jnp.float32)
     for line in range(cases * 8):
-        total, bend = zero, zero
+        bend = zero
         momentum_ref[rows(line * span), :] = zero
         momentum_ref[rows(line * span + 8 + depth), :] = zero
-        for block in range(depth // 8):
-            total += density_ref[rows(line * depth + 8 * block), :]
         for block in range(depth // 8 + 1):
             at = line * span + 8 + 8 * block
             change = momentum_ref[rows(at), :] - momentum_ref[rows(at - 1), :]
             bend += change * change
-        mean_ref[pl.ds(line, 1), :] = jnp.sum(total, axis=0, keepdims=True)
+        mean_ref[pl.ds(line, 1), :] = depth_sum([density_ref[rows(line * depth + 8 * block), :] for block in range(depth // 8)])
         bend_ref[pl.ds(line, 1), :] = jnp.sum(bend, axis=0, keepdims=True)
-    wall = zero
+
+    grad, missing = zero, zero
     for case in range(cases):
-        wall += coef_ref[rows((case * N_COEF + BEND) * 8), :] * bend_ref[rows(case * 8), :]
-    wall_ref[...] = wall
-
-
-def wall_kernel(cases, wall_ref, mean_ref, below_ref, above_ref, coef_ref, grad_ref, sums_ref):
-    row = rows_of((8, 128))
-    grad = wall_ref[...]
-    for case in range(cases):
+
+        def coef(i):
+            return coef_ref[rows((case * N_COEF + i) * 8), :]
+
+        pairs = [arrived.get(pl.ds(2 * planes + (case * 5 + i) * 2, 2)) for i in range(5)]
+        below, above = [pair[0] for pair in pairs], [pair[1] for pair in pairs]
+        total, lifted, along = (moment_ref[rows((case * 5 + i) * 8), :] for i in range(3))
+
+        def beyond(plane):
+            first, second, last, before = plane[0:1], plane[1:2], plane[7:8], plane[6:7]
+            none = jnp.zeros((1, 128), jnp.float32)
+            down = (jnp.concatenate([-first, 16.0 * first - second], 0), jnp.concatenate([-first, 8.0 * first - second], 0))
+            up = (jnp.concatenate([16.0 * last - before, -last], 0), jnp.concatenate([before - 8.0 * last, last], 0))
+            return down, up, none
+
+        down, up, _ = zip(beyond(total), beyond(lifted), beyond(along), strict=True)
+        mean_below = below[0] + below[1] * down[0][0] + below[2] * down[1][1] + below[3] * down[2][1]
+        mean_above = above[0] + above[1] * up[0][0] + above[2] * up[1][1] + above[3] * up[2][1]
         mean = mean_ref[rows(case * 8), :]
-        halo = jnp.where(row >= 4, below_ref[rows(case * 8), :], above_ref[rows(case * 8), :])
-        m1 = pltpu.roll(jnp.where(row == 7, halo, mean), 1, 0)
-        m2 = pltpu.roll(jnp.where(row >= 6, halo, mean), 2, 0)
-        p1 = pltpu.roll(jnp.where(row == 0, halo, mean), 7, 0)
-        p2 = pltpu.roll(jnp.where(row < 2, halo, mean), 6, 0)
-        grad += coef_ref[rows((case * N_COEF + FLUX) * 8), :] * (8.0 * (p1 - m1) - (p2 - m2))
+        halo = jnp.concatenate([mean_above, zero[0:4], mean_below], axis=0)
+        m1 = pltpu.roll(jnp.where(layer == 7, halo, mean), 1, 0)
+        m2 = pltpu.roll(jnp.where(layer >= 6, halo, mean), 2, 0)
+        p1 = pltpu.roll(jnp.where(layer == 0, halo, mean), 7, 0)
+        p2 = pltpu.roll(jnp.where(layer < 2, halo, mean), 6, 0)
+        grad += coef(FLUX) * (8.0 * (p1 - m1) - (p2 - m2)) + coef(BEND) * bend_ref[rows(case * 8), :]
+        change = edge_sums(corr_ref[rows(case * 8), :])
+        down_rows = jnp.concatenate([change[6:7] - 8.0 * change[7:8], change[7:8]], axis=0)
+        up_rows = jnp.concatenate([-change[0:1], 8.0 * change[0:1] - change[1:2]], axis=0)
+        missing += jnp.concatenate([above[4] * down_rows, zero[0:4], below[4] * up_rows], axis=0)
+    corner = ((lane < 2) | (lane >= 126)) & ((layer < 2) | (layer >= 6))
     grad_ref[...] = grad
-    part = jnp.sum(grad * grad, axis=0, keepdims=True)
-    sums_ref[...] = jnp.broadcast_to(part[None], sums_ref.shape)
-
-
-def scale_kernel(cells, grad_ref, sums_ref, out_ref):
-    total = jnp.sum(sums_ref[...], axis=0)
-    total = jnp.sum(total, axis=1, keepdims=True)
-    out_ref[...] = grad_ref[...] / jnp.sqrt(total / cells + 1e-06)
+    inside = jnp.where(corner, 0.0, grad)
+    rest = jnp.sum(inside * inside, axis=0, keepdims=True)
+    corners = pltpu.roll(jnp.where(corner, grad, 0.0), 2, 1, stride=4, stride_axis=0)
+    shares = pltpu.roll(jnp.where(corner, missing, 0.0), 34, 1, stride=4, stride_axis=0)
+    line = jnp.sum(corners + shares, axis=0, keepdims=True)
+    line = jnp.where(lanes_of((1, 128)) < 64, line, rest + pltpu.roll(rest, 64, 1))
+    sums_ref[...] = jnp.broadcast_to(line[None], sums_ref.shape)
+
+
+def scale_kernel(cells, devices, trans, place_ref, grad_ref, sums_ref, out_ref, lines_ref, shares_ref):
+    pad = -(-trans // 8) * 8
+    lane, row = lanes_of((8, 128)), rows_of((8, 128))
+    zero = jnp.zeros((pad, 128), jnp.float32)
+    lines_ref[rows(0, pad), :] = zero
+    lines_ref[rows(pad + devices, pad), :] = zero
+    for device in range(devices):
+        lines_ref[pl.ds(pad + device, 1), :] = sums_ref[device]
+    total = jnp.zeros((8, 128), jnp.float32)
+    for block in range(devices // 8):
+        here = lines_ref[rows(pad + 8 * block), :]
+        below, above = lines_ref[rows(pad - trans + 8 * block), :], lines_ref[rows(pad + trans + 8 * block), :]
+        share = pltpu.roll(jnp.where(lane < 48, below, above), 96, 1)
+        shares_ref[rows(8 * block), :] = share
+        corner = here + share
+        total += jnp.where(lane < 32, corner * corner, jnp.where(lane >= 64, here, 0.0))
+    total = jnp.sum(jnp.sum(total, axis=0, keepdims=True), axis=1, keepdims=True)
+    own = jnp.broadcast_to(shares_ref[pl.ds(place_ref[DEVICE], 1), :], (8, 128))
+    grad = grad_ref[...]
+    edge = (lane < 2) | (lane >= 126)
+    for i in (0, 1, 6, 7):
+        grad += jnp.where((row == i) & edge, pltpu.roll(own, (126 - 4 * i) % 128, 1), 0.0)
+    out_ref[...] = grad / jnp.sqrt(total / cells + 1e-06)
 
 
 def f32(*shape):
@@ -435,9 +567,11 @@
     return up, [(j, i) for i, j in up]
 
 
-def exchange_rows(up, down):
-    ahead, back = neighbours("roll")
-    return lax.ppermute(up, "roll", ahead), lax.ppermute(down, "roll", back)
+def exchange_rows(first, second):
+    size = lax.axis_size("roll")
+    inner = [(i, i ^ 1) for i in range(size) if i ^ 1 < size]
+    outer = [pair for i in range(1, size - 1, 2) for pair in ((i, i + 1), (i + 1, i))]
+    return lax.ppermute(first, "roll", inner), lax.ppermute(second, "roll", outer)
 
 
 def exchange_columns(cols):
@@ -454,9 +588,11 @@
     assert (components, width_x, width_y, 4 * depth) == (4, 8, 128, 128)
     state = adjoint.reshape(planes * 8, 128)
     forcing = source.reshape(planes * 8, 128)
-    place = jnp.stack([lax.axis_index("trans"), lax.axis_size("trans")]).astype(jnp.int32)
+    roll, trans, trans_size = lax.axis_index("roll"), lax.axis_index("trans"), lax.axis_size("trans")
+    place = jnp.stack([trans, trans_size, roll % 2, roll * trans_size + trans]).astype(jnp.int32)
+    devices = lax.axis_size("roll") * trans_size
     whole, inner = f32(planes * 8 + 2 * PAD, 128), f32(planes * 8, 128)
-    message, cols_shape = f32(planes * 2 + 16, 128), f32(components * cases * 8, 128)
+    message, cols_shape = f32(planes * 2 + TAIL, 128), f32(components * cases * 8, 128)
     coef, packed, mask = call(
         functools.partial(coefficient_kernel, depth, cases),
         temp_index,
@@ -467,11 +603,11 @@
         outs=(f32(cases * N_COEF * 8, 128), f32(cases * N_PACKED * 8, 128), f32(8, 128)),
         smem=2,
     )
-    tiles, up, down, cols = call(
-        functools.partial(pack_kernel, depth, cases), state, outs=(whole, message, message, cols_shape)
+    tiles, first, second, cols = call(
+        functools.partial(pack_kernel, depth, cases), place, state, outs=(whole, message, message, cols_shape), smem=1
     )
     for index in range(SECTIONS):
-        below, above = exchange_rows(up, down)
+        first, second = exchange_rows(first, second)
         side = exchange_columns(cols)
         more = index < SECTIONS - 1
         part, *edges = call(
@@ -479,36 +615,44 @@
             tiles,
             forcing,
             coef,
-            outs=(inner, cols_shape) if more else (inner,),
+            outs=(inner, cols_shape, f32(cases * 8, 128)) if more else (inner,),
             scratch=[(planes * 8, 256)],
         )
-        arrived = (part, *edges, below, above, side, mask, coef, packed)
+        arrived = (place, part, *edges, first, second, side, mask, coef, packed)
         if more:
-            tiles, up, down, cols = call(
+            tiles, first, second, cols, moments = call(
                 functools.partial(joined_kernel, depth, cases),
                 *arrived,
-                outs=(whole, message, message, cols_shape),
+                outs=(whole, message, message, cols_shape, f32(cases * 5 * 8, 128)),
                 scratch=[cols_shape.shape] * 2,
+                smem=1,
             )
         else:
-            state, mean, wall = call(
+            state, grad, sums = call(
                 functools.partial(final_kernel, depth, cases),
                 *arrived,
-                outs=(inner, f32(cases * 8, 128), f32(8, 128)),
+                moments,
+                outs=(inner, f32(8, 128), f32(devices, 1, 128)),
                 scratch=[
                     cols_shape.shape,
                     (cases * 8 * depth, 128),
                     (cases * 8 * (depth + 16), 128),
                     (cases * 8, 128),
+                    (cases * 8, 128),
                 ],
+                smem=1,
             )
-    below, above = exchange_rows(mean, mean)
-    devices = lax.axis_size("roll") * lax.axis_size("trans")
-    grad, sums = call(
-        functools.partial(wall_kernel, cases), wall, mean, below, above, coef, outs=(f32(8, 128), f32(devices, 1, 128))
+    sums = lax.all_to_all(sums, ("roll", "trans"), 0, 0, tiled=True)
+    pad = -(-trans_size // 8) * 8
+    (wall_step,) = call(
+        functools.partial(scale_kernel, devices * width_x * width_y, devices, trans_size),
+        place,
+        grad,
+        sums,
+        outs=(f32(8, 128),),
+        scratch=[(devices + 2 * pad, 128), (devices, 128)],
+        smem=1,
     )
-    sums = lax.all_to_all(sums, ("roll", "trans"), 0, 0, tiled=True)
-    (wall_step,) = call(functools.partial(scale_kernel, devices * width_x * width_y), grad, sums, outs=(f32(8, 128),))
     return (state.reshape(adjoint.shape), wall_step)
 
 

time: 51.1 us -> 43.9 us (0.86)
  starting transfers between devices: 21.3 us -> 10.4 us
  Pallas kernels: 8.86 us -> 11.6 us
  blocking collectives: 17.1 us -> 18.9 us
  waiting for transfers between devices: 1.42 us -> 0.62 us
    ppermute x6 -> x4, starting transfers between devices: 17.3 us -> 6.31 us  [the longest x2 4.98 us: exchange_rows(): lax.ppermute(first, 'roll', inner)]
    pallas_call x8 -> x7, Pallas kernels: 8.86 us -> 11.6 us  [call(): pl.pallas_call(kernel, out_shape=outs, in_specs=[SM] * smem + [VM] * (len...]
    all_to_all x1, blocking collectives: 17.1 us -> 18.9 us  [on_device(): sums = lax.all_to_all(sums, ('roll', 'trans'), 0, 0, tiled=True)]
    ppermute x6 -> x4, waiting for transfers between devices: 0.81 us -> 0.01 us  [the longest x2 0.01 us: exchange_rows(): lax.ppermute(first, 'roll', inner)]
  transfers between devices with their start and end apart: 8 -> 6, of which waited for: 2 -> 1; matrix products, arithmetic and copies ran while one was open for 0% -> 0% of each run, Pallas kernels for 10% -> 11%
where the time goes in v3:
time: 43.9 us; the launch traced here: 43.7 us
  blocking collectives  18.9 us (43%)
  Pallas kernels  11.6 us (26%)
  starting transfers between devices  10.4 us (24%)
  local copies, waits for them, and re-layouts  1.31 us (3%)
  between operations  0.74 us (2%)
  waiting for transfers between devices  0.62 us (1%)
    all_to_all x1, blocking collectives, on_device(): sums = lax.all_to_all(sums, ('roll', 'trans'), 0, 0, tiled=True)  18.9 us
    pallas_call x7, Pallas kernels, call(): pl.pallas_call(kernel, out_shape=outs, in_specs=[SM] * smem + [VM] * (len...  11.6 us
    ppermute x2, starting transfers between devices, exchange_rows(): lax.ppermute(first, 'roll', inner)  4.98 us
    ppermute x2, starting transfers between devices, exchange_columns(): return lax.ppermute(cols, 'trans', ahead + back)  4.13 us
    ppermute x2, starting transfers between devices, exchange_rows(): lax.ppermute(second, 'roll', outer)  1.33 us
    unnamed x12, local copies, waits for them, and re-layouts  1.31 us
  transfers between devices with their start and end apart: 6, of which 1 were waited for; matrix products, arithmetic and copies ran while one was open for 0% of the time, Pallas kernels for 11%

profile of v3, /device:TPU:0, one launch (start us, length us, event | category | flops | bytes accessed | tf_op | source)
XLA Modules:
  0.0 43.7 jit_solution(1374104610811278991)
XLA Ops:
  0.6 0.0 copy-start
  0.7 0.1 pad_add_fusion.place_ref
  0.7 1.3 %copy-done.1 = f32[4,2,32,8,128]{4,3,2,1,0:T(8,128)S(1)} copy-done((f32[4,2,32,8,128]{4,3,2,1,0:T(8,128)S(1)}, f32[4,2,32,8,128]{4,3,2,1,0:T(8,128)}, u32[]{:S(2)}) %copy-start.1) | copy-done | bytes 1048600
  2.0 1.5 %shard_map.77 = (f32[2064,128]{1,0:T(8,128)S(1)}, f32[536,128]{1,0:T(8,128)S(1)}, f32[536,128]{1,0:T(8,128)S(1)}, f32[64,128]{1,0:T(8,128)S(1)}) custom-call(s32[4]{0:T(128)S(1)} %pad_add_fusion.place_ref, f32[2048,128]{1,0:T(8,128)S(1)} %bitcast.10), custom_call_target="tpu_custom_call" | custom-call | tf_op jit(solution)/shard_map/pallas_call | solution.py:554
  3.6 0.5 %collective-permute-start = (f32[536,128]{1,0:T(8,128)S(1)}, f32[536,128]{1,0:T(8,128)S(1)}, u32[]{:S(2)}, u32[]{:S(2)}) collective-permute-start(f32[536,128]{1,0:T(8,128)S(1)} %get-tuple-element.25), channel_id=1, source_target_pairs={{0,2},{2,0},{4,6},{6,4},{8,10},{10,8},{12,14},{14,12},{16,18},{18,... | collective-permute-start | bytes 823304 | tf_op jit(solution)/shard_map/ppermute | solution.py:574
  4.1 0.7 %collective-permute-start.1 = (f32[536,128]{1,0:T(8,128)S(1)}, f32[536,128]{1,0:T(8,128)S(1)}, u32[]{:S(2)}, u32[]{:S(2)}) collective-permute-start(f32[536,128]{1,0:T(8,128)S(1)} %get-tuple-element.26), channel_id=1, source_target_pairs={{2,4},{4,2},{6,8},{8,6},{10,12},{12,10},{14,16},{16,14},{18,20},{2... | collective-permute-start | bytes 823304 | tf_op jit(solution)/shard_map/ppermute | solution.py:574
  4.8 2.6 %collective-permute-start.2 = (f32[64,128]{1,0:T(8,128)S(1)}, f32[64,128]{1,0:T(8,128)S(1)}, u32[]{:S(2)}, u32[]{:S(2)}) collective-permute-start(f32[64,128]{1,0:T(8,128)S(1)} %get-tuple-element.27), channel_id=1, source_target_pairs={{0,1},{1,0},{2,3},{3,2},{4,5},{5,4},{6,7},{7,6},{8,9},{9,8},{10,11... | collective-permute-start | bytes 98312 | tf_op jit(solution)/shard_map/ppermute | solution.py:580
  7.3 0.0 copy-done.5
  7.4 0.7 %shard_map.78 = (f32[240,128]{1,0:T(8,128)S(1)}, f32[80,128]{1,0:T(8,128)S(1)}, f32[8,128]{1,0:T(8,128)S(1)}) custom-call(s32[2]{0:T(128)S(1)} %copy-done.5, s32[4]{0:T(128)S(1)} %pad_add_fusion.place_ref, f32[16,128]{1,0:T(8,128)S(1)} %bitcast.11, f32[8,128]{1,0:T(8,128)S(1)} %copy-done.4, s32[16,128]{1,0:T(8,128)S(1)} %bitcast.12), custom_call_target="tpu_custom_call" | custom-call | tf_op jit(solution)/shard_map/pallas_call | solution.py:554
  8.1 2.5 %shard_map.79 = (f32[2048,128]{1,0:T(8,128)S(1)}, f32[64,128]{1,0:T(8,128)S(1)}, f32[16,128]{1,0:T(8,128)S(1)}) custom-call(f32[2064,128]{1,0:T(8,128)S(1)} %get-tuple-element.20.tiles_ref, f32[2048,128]{1,0:T(8,128)S(1)} %bitcast.8, f32[240,128]{1,0:T(8,128)S(1)} %get-tuple-element.21.coef_ref), custom_call_target="tpu_custom_call" | custom-call | tf_op jit(solution)/shard_map/pallas_call | solution.py:554
  10.6 0.0 collective-permute-done.2.side_ref
  10.6 0.0 collective-permute-done.first_in_ref
  10.6 0.0 collective-permute-done.1.second_in_ref
  10.6 1.2 %shard_map.80 = (f32[2064,128]{1,0:T(8,128)S(1)}, f32[536,128]{1,0:T(8,128)S(1)}, f32[536,128]{1,0:T(8,128)S(1)}, f32[64,128]{1,0:T(8,128)S(1)}, f32[80,128]{1,0:T(8,128)S(1)}) custom-call(s32[4]{0:T(128)S(1)} %pad_add_fusion.place_ref, f32[2048,128]{1,0:T(8,128)S(1)} %get-tuple-element.22.inner_ref, f32[64,128]{1,0:T(8,128)S(1)} %get-tuple-element.23.edge_ref, ...), custom_call_target="tpu_custom_call" | custom-call | tf_op jit(solution)/shard_map/pallas_call | solution.py:554
  11.8 4.5 %collective-permute-start.3 = (f32[536,128]{1,0:T(8,128)S(1)}, f32[536,128]{1,0:T(8,128)S(1)}, u32[]{:S(2)}, u32[]{:S(2)}) collective-permute-start(f32[536,128]{1,0:T(8,128)S(1)} %get-tuple-element.31), channel_id=1, source_target_pairs={{0,2},{2,0},{4,6},{6,4},{8,10},{10,8},{12,14},{14,12},{16,18},{18,... | collective-permute-start | bytes 823304 | tf_op jit(solution)/shard_map/ppermute | solution.py:574
  16.3 0.7 %collective-permute-start.4 = (f32[536,128]{1,0:T(8,128)S(1)}, f32[536,128]{1,0:T(8,128)S(1)}, u32[]{:S(2)}, u32[]{:S(2)}) collective-permute-start(f32[536,128]{1,0:T(8,128)S(1)} %get-tuple-element.32), channel_id=1, source_target_pairs={{2,4},{4,2},{6,8},{8,6},{10,12},{12,10},{14,16},{16,14},{18,20},{2... | collective-permute-start | bytes 823304 | tf_op jit(solution)/shard_map/ppermute | solution.py:574
  17.0 1.6 %collective-permute-start.5 = (f32[64,128]{1,0:T(8,128)S(1)}, f32[64,128]{1,0:T(8,128)S(1)}, u32[]{:S(2)}, u32[]{:S(2)}) collective-permute-start(f32[64,128]{1,0:T(8,128)S(1)} %get-tuple-element.33), channel_id=1, source_target_pairs={{0,1},{1,0},{2,3},{3,2},{4,5},{5,4},{6,7},{7,6},{8,9},{9,8},{10,11... | collective-permute-start | bytes 98312 | tf_op jit(solution)/shard_map/ppermute | solution.py:580
  18.5 1.8 %shard_map.81.inner_ref = f32[2048,128]{1,0:T(8,128)S(1)} custom-call(f32[2064,128]{1,0:T(8,128)S(1)} %get-tuple-element.30.tiles_ref, f32[2048,128]{1,0:T(8,128)S(1)} %bitcast.9, f32[240,128]{1,0:T(8,128)S(1)} %get-tuple-element.21.coef_ref), custom_call_target="tpu_custom_call" | custom-call | tf_op jit(solution)/shard_map/pallas_call | solution.py:554
  20.3 0.6 %collective-permute-done.5.side_ref = f32[64,128]{1,0:T(8,128)S(1)} collective-permute-done((f32[64,128]{1,0:T(8,128)S(1)}, f32[64,128]{1,0:T(8,128)S(1)}, u32[]{:S(2)}, u32[]{:S(2)}) %collective-permute-start.5) | collective-permute-done | bytes 32800 | tf_op jit(solution)/shard_map/ppermute | solution.py:580
  21.0 0.0 collective-permute-done.3.first_in_ref
  21.0 0.0 collective-permute-done.4.second_in_ref
  21.0 2.5 %shard_map.82 = (f32[2048,128]{1,0:T(8,128)}, f32[8,128]{1,0:T(8,128)S(1)}, f32[32,1,128]{2,1,0:T(1,128)S(1)}) custom-call(s32[4]{0:T(128)S(1)} %pad_add_fusion.place_ref, f32[2048,128]{1,0:T(8,128)S(1)} %shard_map.81.inner_ref, f32[536,128]{1,0:T(8,128)S(1)} %collective-permute-done.3.first_in_ref, f32[536,128]{1,0:T(8,128)S(1)} %collective-permute-done.4.second_in_ref, ...), custom_call_target="tpu_custom_call" | custom-call | tf_op jit(solution)/shard_map/pallas_call | solution.py:554
  23.5 18.9 %all_to_all.5.sums_ref = f32[32,1,128]{2,1,0:T(1,128)S(1)} all-to-all(f32[32,1,128]{2,1,0:T(1,128)S(1)} %get-tuple-element.37), channel_id=1, replica_groups=mesh['roll'=16,'trans'=2] {'roll','trans'}, dimensions={0} | all-to-all | bytes 32768 | tf_op jit(solution)/shard_map/all_to_all | solution.py:645
  42.4 1.3 %shard_map.83 = f32[8,128]{1,0:T(8,128)} custom-call(s32[4]{0:T(128)S(1)} %pad_add_fusion.place_ref, f32[8,128]{1,0:T(8,128)S(1)} %get-tuple-element.36.grad_ref, f32[32,1,128]{2,1,0:T(1,128)S(1)} %all_to_all.5.sums_ref), custom_call_target="tpu_custom_call" | custom-call | tf_op jit(solution)/shard_map/pallas_call | solution.py:554
  (9 shorter events, 0.0 us)
Async XLA Ops:
  0.6 7.5 %copy-start = (f32[4,2,32,8,128]{4,3,2,1,0:T(8,128)S(1)}, f32[4,2,32,8,128]{4,3,2,1,0:T(8,128)}, u32[]{:S(2)}) copy-start(f32[4,2,32,8,128]{4,3,2,1,0:T(8,128)} %param.7) | copy-start | bytes 3145732
  0.7 1.3 %copy-start.1 = (f32[4,2,32,8,128]{4,3,2,1,0:T(8,128)S(1)}, f32[4,2,32,8,128]{4,3,2,1,0:T(8,128)}, u32[]{:S(2)}) copy-start(f32[4,2,32,8,128]{4,3,2,1,0:T(8,128)} %param.6) | copy-start | bytes 3145732
  2.0 5.3 %copy-start.2 = (f32[2,8,128]{2,1,0:T(8,128)S(1)}, f32[2,8,128]{2,1,0:T(8,128)}, u32[]{:S(2)}) copy-start(f32[2,8,128]{2,1,0:T(8,128)} %param.8) | copy-start | bytes 24580
  2.0 5.3 %copy-start.3 = (s32[2,8,128]{2,1,0:T(8,128)S(1)}, s32[2,8,128]{2,1,0:T(8,128)}, u32[]{:S(2)}) copy-start(s32[2,8,128]{2,1,0:T(8,128)} %param.10) | copy-start | bytes 24580
  2.0 5.3 %copy-start.4 = (f32[8,128]{1,0:T(8,128)S(1)}, f32[8,128]{1,0:T(8,128)}, u32[]{:S(2)}) copy-start(f32[8,128]{1,0:T(8,128)} %film_ref.1) | copy-start | bytes 12292
  2.0 5.3 %copy-start.5 = (s32[2]{0:T(128)S(1)}, s32[2]{0:T(128)}, u32[]{:S(2)}) copy-start(s32[2]{0:T(128)} %level_ref.1) | copy-start | bytes 28
  3.6 7.0 %collective-permute-start = (f32[536,128]{1,0:T(8,128)S(1)}, f32[536,128]{1,0:T(8,128)S(1)}, u32[]{:S(2)}, u32[]{:S(2)}) collective-permute-start(f32[536,128]{1,0:T(8,128)S(1)} %get-tuple-element.25), channel_id=1, source_target_pairs={{0,2},{2,0},{4,6},{6,4},{8,10},{10,8},{12,14},{14,12},{16,18},{18,... | collective-permute-start | bytes 823304 | tf_op jit(solution)/shard_map/ppermute | solution.py:574
  4.1 6.5 %collective-permute-start.1 = (f32[536,128]{1,0:T(8,128)S(1)}, f32[536,128]{1,0:T(8,128)S(1)}, u32[]{:S(2)}, u32[]{:S(2)}) collective-permute-start(f32[536,128]{1,0:T(8,128)S(1)} %get-tuple-element.26), channel_id=1, source_target_pairs={{2,4},{4,2},{6,8},{8,6},{10,12},{12,10},{14,16},{16,14},{18,20},{2... | collective-permute-start | bytes 823304 | tf_op jit(solution)/shard_map/ppermute | solution.py:574
  4.8 5.8 %collective-permute-start.2 = (f32[64,128]{1,0:T(8,128)S(1)}, f32[64,128]{1,0:T(8,128)S(1)}, u32[]{:S(2)}, u32[]{:S(2)}) collective-permute-start(f32[64,128]{1,0:T(8,128)S(1)} %get-tuple-element.27), channel_id=1, source_target_pairs={{0,1},{1,0},{2,3},{3,2},{4,5},{5,4},{6,7},{7,6},{8,9},{9,8},{10,11... | collective-permute-start | bytes 98312 | tf_op jit(solution)/shard_map/ppermute | solution.py:580
  11.8 9.1 %collective-permute-start.3 = (f32[536,128]{1,0:T(8,128)S(1)}, f32[536,128]{1,0:T(8,128)S(1)}, u32[]{:S(2)}, u32[]{:S(2)}) collective-permute-start(f32[536,128]{1,0:T(8,128)S(1)} %get-tuple-element.31), channel_id=1, source_target_pairs={{0,2},{2,0},{4,6},{6,4},{8,10},{10,8},{12,14},{14,12},{16,18},{18,... | collective-permute-start | bytes 823304 | tf_op jit(solution)/shard_map/ppermute | solution.py:574
  16.3 4.7 %collective-permute-start.4 = (f32[536,128]{1,0:T(8,128)S(1)}, f32[536,128]{1,0:T(8,128)S(1)}, u32[]{:S(2)}, u32[]{:S(2)}) collective-permute-start(f32[536,128]{1,0:T(8,128)S(1)} %get-tuple-element.32), channel_id=1, source_target_pairs={{2,4},{4,2},{6,8},{8,6},{10,12},{12,10},{14,16},{16,14},{18,20},{2... | collective-permute-start | bytes 823304 | tf_op jit(solution)/shard_map/ppermute | solution.py:574
  17.0 4.0 %collective-permute-start.5 = (f32[64,128]{1,0:T(8,128)S(1)}, f32[64,128]{1,0:T(8,128)S(1)}, u32[]{:S(2)}, u32[]{:S(2)}) collective-permute-start(f32[64,128]{1,0:T(8,128)S(1)} %get-tuple-element.33), channel_id=1, source_target_pairs={{0,1},{1,0},{2,3},{3,2},{4,5},{5,4},{6,7},{7,6},{8,9},{9,8},{10,11... | collective-permute-start | bytes 98312 | tf_op jit(solution)/shard_map/ppermute | solution.py:580

commit v4 on v3

v4 whole, which is shorter than its diff:
```python
import functools

import jax
import jax.numpy as jnp
from jax import lax
from jax.experimental import pallas as pl
from jax.experimental.pallas import tpu as pltpu
from jax.sharding import PartitionSpec as P

SECTIONS = 2


VISCOSITY_PRESS = 0.3
VISCOSITY_TEMP = 0.5
THETA_STEP = 0.2
SOUND = 0.5
KAPPA = 0.6
HEATING = 0.3
ROLL_SPEED = 1.0
COURANT = 0.8

VM = pl.BlockSpec(memory_space=pltpu.VMEM)
SM = pl.BlockSpec(memory_space=pltpu.SMEM)
HB = pl.BlockSpec(memory_space=pltpu.HBM)
PARAMS = pltpu.CompilerParams(vmem_limit_bytes=16 * 1024 * 1024)

PAD = 8
CENTER, SPREAD, ACROSS = (0, 3, 6)
CARRY, SOUND_STEP, STEP, HEAT, FLUX, BEND = range(9, 15)
N_COEF = 15
N_PACKED = 4
PIECES = 4
TAIL = 24
MIDDLE, OUTER = (2, 3, 4, 5), (0, 1, 6, 7)
TRANS, TRANS_SIZE, ODD, DEVICE = range(4)
WEIGHT = (0, 1, 1, 2)


def lanes_of(shape):
    return lax.broadcasted_iota(jnp.int32, shape, 1)


def rows_of(shape):
    return lax.broadcasted_iota(jnp.int32, shape, 0)


def rows(start, count=8):
    return pl.ds(start, count)


def strided(start):
    return pl.ds(start, 8, stride=8)


def coefficient_kernel(depth, cases, level_ref, place_ref, pressure_ref, film_ref, cavity_ref, coef_ref, packed_ref, mask_ref):
    lane, row = lanes_of((8, 128)), rows_of((8, 128))
    film = film_ref[...]
    for case in range(cases):
        theta = THETA_STEP * level_ref[case].astype(jnp.float32)
        viscosity = jnp.exp(VISCOSITY_PRESS * pressure_ref[rows(case * 8), :] - VISCOSITY_TEMP * theta)
        film_coef = 4.0 * viscosity / (film * film)
        density = 1.0 - 0.6 * cavity_ref[rows(case * 8), :].astype(jnp.float32)
        step = COURANT / (32.0 / 3.0 * viscosity + 4.0 * film_coef + 2.0 * SOUND + 1.0)
        planes = [None] * N_COEF
        for i, weight in enumerate((0.5, 1.0, KAPPA)):
            planes[SPREAD + i] = (weight / 12.0) * step * viscosity
            planes[ACROSS + i] = weight * step * film_coef
            planes[CENTER + i] = 1.0 - 60.0 * planes[SPREAD + i] - 2.0 * planes[ACROSS + i]
        planes[CARRY] = (ROLL_SPEED / 12.0) * step * density
        planes[SOUND_STEP] = (SOUND / 12.0) * step
        planes[STEP] = step
        planes[HEAT] = HEATING * step * viscosity
        planes[FLUX] = (ROLL_SPEED / (24.0 * depth)) * density * film
        planes[BEND] = (8.0 / depth) * viscosity / (film * film * film)
        for i, plane in enumerate(planes):
            coef_ref[rows((case * N_COEF + i) * 8), :] = plane
        wanted = jnp.concatenate(planes[SPREAD : SPREAD + 3] + [planes[SOUND_STEP]], axis=0)
        packed = exact_dot(wanted, edge_columns())
        for i in range(N_PACKED):
            packed_ref[rows((case * N_PACKED + i) * 8), :] = packed[i * 8 : i * 8 + 8]
    from_left = jnp.where(place_ref[TRANS] > 0, 1.0, 0.0)
    from_right = jnp.where(place_ref[TRANS] < place_ref[TRANS_SIZE] - 1, 1.0, 0.0)
    mask_ref[...] = jnp.where(lane % 4 < 2, from_left, from_right)


def edge_columns():
    source = lanes_of((128, 128)) % 4
    source = jnp.where(source < 2, 126 + source, source - 2)
    return jnp.where(rows_of((128, 128)) == source, 1.0, 0.0).astype(jnp.bfloat16)


def in_parts(value):
    high = value.astype(jnp.bfloat16)
    rest = value - high.astype(jnp.float32)
    middle = rest.astype(jnp.bfloat16)
    return jnp.concatenate([high, middle], axis=1), (rest - middle.astype(jnp.float32)).astype(jnp.bfloat16)


def exact_dot(value, weights):
    upper, low = in_parts(value)
    part = jnp.dot(upper, jnp.concatenate([weights, weights], axis=0), preferred_element_type=jnp.float32)
    return part + jnp.dot(low, weights, preferred_element_type=jnp.float32)


class Post:
    def __init__(self, place_ref, first_ref, second_ref):
        self.odd = place_ref[ODD] == 1
        self.refs = first_ref, second_ref

    def put(self, where, up, down):
        first, second = self.refs
        first[where, :] = jnp.where(self.odd, down, up)
        second[where, :] = jnp.where(self.odd, up, down)

    def get(self, where):
        first, second = (ref[where, :] for ref in self.refs)
        return jnp.where(self.odd, first, second), jnp.where(self.odd, second, first)

    def put_tiles(self, planes, first, tiles):
        for i in range(2):
            self.put(rows(i * planes + first), tiles[6 + i], tiles[i])


def row_place(refs, row, planes):
    if row in MIDDLE:
        return refs[0], PAD + MIDDLE.index(row) * planes
    return refs[1], PAD + OUTER.index(row) * planes


def send_kernel(depth, cases, place_ref, state_ref, copy_ref, first_ref, second_ref, sems):
    planes = 4 * cases * depth
    post = Post(place_ref, first_ref, second_ref)

    def piece(i):
        here = rows(i * (planes * 8 // PIECES), planes * 8 // PIECES)
        return pltpu.make_async_copy(state_ref.at[here, :], copy_ref.at[here, :], sems.at[i])

    for i in range(PIECES):
        piece(i).start()
    for i in range(PIECES):
        piece(i).wait()
        for first in range(i * planes // PIECES, (i + 1) * planes // PIECES, 8):
            post.put_tiles(planes, first, {row: copy_ref[strided(first * 8 + row), :] for row in (0, 1, 6, 7)})


def pack_kernel(depth, cases, state_ref, source_ref, middle_ref, outer_ref, cols_ref, copy_ref, sem):
    planes = 4 * cases * depth
    lane = lanes_of((8, 128))
    copy = pltpu.make_async_copy(source_ref, copy_ref, sem)
    copy.start()

    def one(pair, _):
        held = jnp.zeros((8, 128), jnp.float32)
        for layer in range(depth):
            group = depth - 1 - layer
            plane = state_ref[rows(pl.multiple_of((pair * depth + layer) * 8, 8)), :]
            held = jnp.where(lane // 4 == group, pltpu.roll(plane, (4 * group + 2) % 128, 1), held)
        cols_ref[rows(pl.multiple_of(pair * 8, 8)), :] = held
        for row in range(8):
            for block in range(depth // 8):
                first = pl.multiple_of(pair * depth + 8 * block, 8)
                ref, place = row_place((middle_ref, outer_ref), row, planes)
                ref[rows(place + first), :] = state_ref[strided(first * 8 + row), :]
        return 0

    lax.fori_loop(0, 4 * cases, one, 0)
    copy.wait()


def columns_kernel(depth, cases, middle_ref, outer_ref, cols_ref):
    planes = 4 * cases * depth
    columns = edge_columns()
    mine = lanes_of((depth, 128)) // 4 == (depth - 1) - rows_of((depth, 128))
    for row in range(8):
        ref, place = row_place((middle_ref, outer_ref), row, planes)
        edges = exact_dot(ref[rows(place, planes), :], columns)
        for pair in range(4 * cases):
            kept = jnp.where(mine, edges[pair * depth : (pair + 1) * depth], 0.0)
            cols_ref[pl.ds(pair * 8 + row, 1), :] = jnp.sum(kept, axis=0, keepdims=True)


def inner_kernel(depth, cases, middle_ref, outer_ref, source_ref, coef_ref, *rest):
    out_ref, *more_refs, deriv_ref = rest
    planes = 4 * cases * depth
    lane, layer = lanes_of((8, 128)), rows_of((8, 128))
    gap = rows_of((128, 256)) - lanes_of((128, 256)) % 128
    second = jnp.where(jnp.abs(gap) == 1, 16.0, jnp.where(jnp.abs(gap) == 2, -1.0, 0.0))
    first = jnp.where(gap == 1, 8.0, jnp.where(gap == -1, -8.0, jnp.where(gap == 2, -1.0, jnp.where(gap == -2, 1.0, 0.0))))
    weights = jnp.where(lanes_of((128, 256)) < 128, second, first).astype(jnp.bfloat16)
    for row in range(8):
        ref, place = row_place((middle_ref, outer_ref), row, planes)
        value = ref[rows(place, planes), :]
        deriv_ref[rows(row * planes, planes), :] = exact_dot(value, weights)

    def one(index, _):
        case, block = index // (depth // 8), index % (depth // 8)
        k = layer + 8 * block
        height = (k.astype(jnp.float32) + 0.5) / depth
        offsets = [pl.multiple_of((c * cases + case) * depth + 8 * block, 8) for c in range(4)]
        places = [row_place((middle_ref, outer_ref), row, planes) for row in range(8)]
        tiles = [[ref[rows(place + offsets[c]), :] for ref, place in places] for c in range(4)]

        for row in range(8):

            def coef(i):
                return coef_ref[pl.ds((case * N_COEF + i) * 8 + row, 1), :]

            along = []
            for c in range(4):
                near = [tiles[c][row + by] if 0 <= row + by < 8 else None for by in (-2, -1, 1, 2)]
                along.append(near)

            def first_x(c):
                m2, m1, p1, p2 = along[c]
                ones = 8.0 * (p1 - m1) if m1 is not None and p1 is not None else 8.0 * p1 if m1 is None else -8.0 * m1
                if m2 is not None and p2 is not None:
                    return ones - (p2 - m2)
                return ones - p2 if m2 is None else ones + m2

            def second_x(c):
                m2, m1, p1, p2 = along[c]
                ones = 16.0 * (p1 + m1) if m1 is not None and p1 is not None else 16.0 * (p1 if m1 is None else m1)
                if m2 is not None and p2 is not None:
                    return ones - (p2 + m2)
                return ones - (p2 if m2 is None else m2)

            carry = coef(CARRY) * height
            sound = coef(SOUND_STEP)
            step = coef(STEP)
            slopes = [first_x(c) for c in range(4)]
            for c in range(4):
                here = row * planes + offsets[c]
                ref, place = places[row]
                behind = jnp.where(k > 0, ref[rows(place + offsets[c] - 1), :], 0.0)
                beyond = jnp.where(k < depth - 1, ref[rows(place + offsets[c] + 1), :], 0.0)
                source = source_ref[strided(offsets[c] * 8 + row), :]
                w = WEIGHT[c]
                value = coef(CENTER + w) * tiles[c][row] + coef(SPREAD + w) * (second_x(c) + deriv_ref[rows(here), 0:128])
                value += coef(ACROSS + w) * (behind + beyond) + step * source + carry * slopes[c]
                if c == 0:
                    other = row * planes + offsets[2]
                    value += sound * (slopes[1] + deriv_ref[rows(other), 128:256])
                elif c == 1:
                    value += sound * slopes[0]
                elif c == 2:
                    other = row * planes + offsets[0]
                    value += sound * deriv_ref[rows(other), 128:256]
                else:
                    value += coef(HEAT) * tiles[1][row]
                out_ref[rows(here), :] = value
        return 0

    lax.fori_loop(0, cases * (depth // 8), one, 0)

    if more_refs:
        (total_ref,) = more_refs
        for case in range(cases):
            for row in range(8):
                total = jnp.zeros((8, 128), jnp.float32)
                for block in range(depth // 8):
                    total += source_ref[strided((case * depth + 8 * block) * 8 + row), :]
                total_ref[pl.ds(case * 8 + row, 1), :] = jnp.sum(total, axis=0, keepdims=True)


def columns_beyond(cases, side_ref, mask_ref, packed_ref, corr_ref):
    slot = lanes_of((8, 128)) % 4
    for case in range(cases):
        coefs = [packed_ref[rows((case * N_PACKED + i) * 8), :] for i in range(N_PACKED)]
        second, first = [], []
        for c in range(4):
            side = side_ref[rows((c * cases + case) * 8), :] * mask_ref[...]
            p1 = jnp.where(slot == 1, pltpu.roll(side, 127, 1), 0.0)
            p2 = jnp.where(slot < 2, pltpu.roll(side, 126, 1), 0.0)
            m1 = jnp.where(slot == 2, pltpu.roll(side, 1, 1), 0.0)
            m2 = jnp.where(slot >= 2, pltpu.roll(side, 2, 1), 0.0)
            second.append(16.0 * (p1 + m1) - (p2 + m2))
            first.append(8.0 * (p1 - m1) - (p2 - m2))
        for c in range(4):
            value = coefs[WEIGHT[c]] * second[c]
            if c == 0:
                value += coefs[3] * first[2]
            elif c == 2:
                value += coefs[3] * first[0]
            corr_ref[rows((c * cases + case) * 8), :] = value


def depth_sum(tiles):
    total = tiles[0]
    for tile in tiles[1:]:
        total = total + tile
    return jnp.sum(total, axis=0, keepdims=True)


def next_moments(depth, tiles_of, layer):
    density = tiles_of(0)
    heights = [(layer + (8 * block + 0.5)).astype(jnp.float32) / depth for block in range(depth // 8)]
    return (
        depth_sum(density),
        depth_sum([tile * height for tile, height in zip(density, heights, strict=True)]),
        depth_sum(tiles_of(1)),
        depth_sum(tiles_of(2)),
        density[0][0:1] + density[-1][7:8],
    )


def wall_sums(depth, tiles_of, layer):
    momentum, before = tiles_of(1), tiles_of(1, -1)
    changes = [momentum[0] - jnp.where(layer > 0, before[0], 0.0)]
    changes += [here - there for here, there in zip(momentum[1:], before[1:], strict=True)]
    squares = [change * change for change in changes] + [jnp.where(layer == 7, momentum[-1] * momentum[-1], 0.0)]
    return depth_sum(tiles_of(0)), depth_sum(squares)


def line_sums(depth, cases, planes, sums, ref, which, out_ref, layer):
    for case in range(cases):
        for i, row in enumerate(which):

            def tiles_of(c, by=0):
                start = PAD + i * planes + (c * cases + case) * depth
                return [ref[rows(start + by + 8 * block), :] for block in range(depth // 8)]

            lines = sums(depth, tiles_of, layer)
            for n, line in enumerate(lines):
                out_ref[pl.ds((case * len(lines) + n) * 8 + row, 1), :] = line


def joined_sums(middle_ref, outer_ref, index, layer):
    return jnp.where((layer >= 2) & (layer < 6), middle_ref[rows(index * 8), :], outer_ref[rows(index * 8), :])


def sides_kernel(depth, cases, sums, inner_ref, side_ref, mask_ref, packed_ref, middle_ref, loose_ref, sums_ref, corr_ref):
    planes = 4 * cases * depth
    lane, layer = lanes_of((8, 128)), rows_of((8, 128))
    edge = (lane < 2) | (lane >= 126)
    columns_beyond(cases, side_ref, mask_ref, packed_ref, corr_ref)

    def one(case, _):
        for row in range(8):
            for c in range(4):
                line = jnp.broadcast_to(corr_ref[pl.ds((c * cases + case) * 8 + row, 1), :], (8, 128))
                for block in range(depth // 8):
                    offset = pl.multiple_of((c * cases + case) * depth + 8 * block, 8)
                    moved = pltpu.roll(line, 2 + 32 * block, 1, stride=4, stride_axis=0)
                    value = inner_ref[rows(row * planes + offset), :] + jnp.where(edge, moved, 0.0)
                    ref, place = row_place((middle_ref, loose_ref), row, planes)
                    ref[rows(place + offset), :] = value
        return 0

    lax.fori_loop(0, cases, one, 0)
    line_sums(depth, cases, planes, sums, middle_ref, MIDDLE, sums_ref, layer)


def outer_rows(depth, cases, planes, parts, loose_ref, post, coef_ref, store):
    layer = rows_of((8, 128))

    def one(case, _):
        for block in range(depth // 8):
            height = ((layer + 8 * block).astype(jnp.float32) + 0.5) / depth
            offsets = [pl.multiple_of((c * cases + case) * depth + 8 * block, 8) for c in range(4)]
            near = {c: [post.get(rows(i * planes + offsets[c])) for i in range(2)] for c in {*parts, *range(2)}}
            whole = {c: {} for c in parts}
            for i, row in enumerate(OUTER):

                def coef(n):
                    return coef_ref[pl.ds((case * N_COEF + n) * 8 + row, 1), :]

                second, first = {}, {}
                for c, ((m2, p1), (m1, p2)) in near.items():
                    if row == 0:
                        second[c], first[c] = 16.0 * m1 - m2, m2 - 8.0 * m1
                    elif row == 1:
                        second[c], first[c] = -m1, m1
                    elif row == 6:
                        second[c], first[c] = -p1, -p1
                    else:
                        second[c], first[c] = 16.0 * p1 - p2, 8.0 * p1 - p2
                for c in parts:
                    value = loose_ref[rows(PAD + i * planes + offsets[c]), :]
                    value += coef(SPREAD + WEIGHT[c]) * second[c] + coef(CARRY) * height * first[c]
                    if c < 2:
                        value += coef(SOUND_STEP) * first[1 - c]
                    whole[c][row] = value
            for c in parts:
                store(c, case, block, offsets[c], whole[c])
        return 0

    lax.fori_loop(0, cases, one, 0)


def joined_kernel(
    depth,
    cases,
    place_ref,
    loose_ref,
    middle_sums_ref,
    source_total_ref,
    first_in_ref,
    second_in_ref,
    coef_ref,
    outer_ref,
    first_ref,
    second_ref,
    moment_ref,
    outer_sums_ref,
):
    planes = 4 * cases * depth
    lane, layer = lanes_of((8, 128)), rows_of((8, 128))
    post, arrived = Post(place_ref, first_ref, second_ref), Post(place_ref, first_in_ref, second_in_ref)

    def store(c, case, block, offset, tiles):
        for i, row in enumerate(OUTER):
            outer_ref[rows(PAD + i * planes + offset), :] = tiles[row]
        post.put_tiles(planes, offset, tiles)

    outer_rows(depth, cases, planes, range(4), loose_ref, arrived, coef_ref, store)

    line_sums(depth, cases, planes, next_moments, outer_ref, OUTER, outer_sums_ref, layer)
    for case in range(cases):

        def coef(i):
            return coef_ref[rows((case * N_COEF + i) * 8), :]

        moments = [joined_sums(middle_sums_ref, outer_sums_ref, case * 5 + i, layer) for i in range(5)]
        total, lifted, along, across, walls = moments
        for i in range(3):
            moment_ref[rows((case * 3 + i) * 8), :] = moments[i]

        def x_parts(plane):
            m1, m2 = jnp.where(layer >= 1, pltpu.roll(plane, 1, 0), 0.0), jnp.where(layer >= 2, pltpu.roll(plane, 2, 0), 0.0)
            p1, p2 = jnp.where(layer < 7, pltpu.roll(plane, 7, 0), 0.0), jnp.where(layer < 6, pltpu.roll(plane, 6, 0), 0.0)
            return 16.0 * (p1 + m1) - (p2 + m2), 8.0 * (p1 - m1) - (p2 - m2)

        def y_parts(plane):
            m1, m2 = jnp.where(lane >= 1, pltpu.roll(plane, 1, 1), 0.0), jnp.where(lane >= 2, pltpu.roll(plane, 2, 1), 0.0)
            p1, p2 = jnp.where(lane < 127, pltpu.roll(plane, 127, 1), 0.0), jnp.where(lane < 126, pltpu.roll(plane, 126, 1), 0.0)
            return 16.0 * (p1 + m1) - (p2 + m2), 8.0 * (p1 - m1) - (p2 - m2)

        value = coef(CENTER) * total + coef(SPREAD) * (x_parts(total)[0] + y_parts(total)[0])
        value += coef(ACROSS) * (2.0 * total - walls) + coef(CARRY) * x_parts(lifted)[1]
        value += coef(SOUND_STEP) * (x_parts(along)[1] + y_parts(across)[1]) + coef(STEP) * source_total_ref[rows(case * 8), :]
        sent = (value, coef(SPREAD), coef(CARRY), coef(SOUND_STEP), coef(FLUX))
        for i, plane in enumerate(sent):
            post.put(pl.ds(2 * planes + (case * 5 + i) * 2, 2), plane[6:8], plane[0:2])


def edge_sums(tile):
    for by in (4, 8, 16, 32, 64):
        tile = tile + pltpu.roll(tile, by, 1)
    return pltpu.roll(tile, 2, 1)


def final_kernel(
    depth,
    cases,
    place_ref,
    loose_ref,
    middle_sums_ref,
    corr_ref,
    first_in_ref,
    second_in_ref,
    coef_ref,
    moment_ref,
    outer_ref,
    grad_ref,
    line_ref,
    outer_sums_ref,
):
    planes = 4 * cases * depth
    lane, layer = lanes_of((8, 128)), rows_of((8, 128))
    arrived = Post(place_ref, first_in_ref, second_in_ref)

    def store(c, case, block, offset, tiles):
        for i, row in enumerate(OUTER):
            outer_ref[rows(PAD + i * planes + offset), :] = tiles[row]

    outer_rows(depth, cases, planes, range(2), loose_ref, arrived, coef_ref, store)
    line_sums(depth, cases, planes, wall_sums, outer_ref, OUTER, outer_sums_ref, layer)

    zero = jnp.zeros((8, 128), jnp.float32)
    grad, missing = zero, zero
    for case in range(cases):

        def coef(i):
            return coef_ref[rows((case * N_COEF + i) * 8), :]

        pairs = [arrived.get(pl.ds(2 * planes + (case * 5 + i) * 2, 2)) for i in range(5)]
        below, above = [pair[0] for pair in pairs], [pair[1] for pair in pairs]
        total, lifted, along = (moment_ref[rows((case * 3 + i) * 8), :] for i in range(3))

        def beyond(plane):
            first, second, last, before = plane[0:1], plane[1:2], plane[7:8], plane[6:7]
            down = (jnp.concatenate([-first, 16.0 * first - second], 0), jnp.concatenate([-first, 8.0 * first - second], 0))
            up = (jnp.concatenate([16.0 * last - before, -last], 0), jnp.concatenate([before - 8.0 * last, last], 0))
            return down, up

        down, up = zip(beyond(total), beyond(lifted), beyond(along), strict=True)
        mean_below = below[0] + below[1] * down[0][0] + below[2] * down[1][1] + below[3] * down[2][1]
        mean_above = above[0] + above[1] * up[0][0] + above[2] * up[1][1] + above[3] * up[2][1]
        mean, bend = (joined_sums(middle_sums_ref, outer_sums_ref, case * 2 + i, layer) for i in range(2))
        halo = jnp.concatenate([mean_above, zero[0:4], mean_below], axis=0)
        m1 = pltpu.roll(jnp.where(layer == 7, halo, mean), 1, 0)
        m2 = pltpu.roll(jnp.where(layer >= 6, halo, mean), 2, 0)
        p1 = pltpu.roll(jnp.where(layer == 0, halo, mean), 7, 0)
        p2 = pltpu.roll(jnp.where(layer < 2, halo, mean), 6, 0)
        grad += coef(FLUX) * (8.0 * (p1 - m1) - (p2 - m2)) + coef(BEND) * bend
        change = edge_sums(corr_ref[rows(case * 8), :])
        down_rows = jnp.concatenate([change[6:7] - 8.0 * change[7:8], change[7:8]], axis=0)
        up_rows = jnp.concatenate([-change[0:1], 8.0 * change[0:1] - change[1:2]], axis=0)
        missing += jnp.concatenate([above[4] * down_rows, zero[0:4], below[4] * up_rows], axis=0)
    corner = ((lane < 2) | (lane >= 126)) & ((layer < 2) | (layer >= 6))
    grad_ref[...] = grad
    inside = jnp.where(corner, 0.0, grad)
    rest = jnp.sum(inside * inside, axis=0, keepdims=True)
    corners = pltpu.roll(jnp.where(corner, grad, 0.0), 2, 1, stride=4, stride_axis=0)
    shares = pltpu.roll(jnp.where(corner, missing, 0.0), 34, 1, stride=4, stride_axis=0)
    line = jnp.sum(corners + shares, axis=0, keepdims=True)
    line = jnp.where(lanes_of((1, 128)) < 64, line, rest + pltpu.roll(rest, 64, 1))
    line_ref[...] = jnp.broadcast_to(line[None], line_ref.shape)


def rest_kernel(
    depth,
    cases,
    place_ref,
    loose_ref,
    middle_ref,
    early_ref,
    first_in_ref,
    second_in_ref,
    coef_ref,
    out_ref,
    state_ref,
    sems,
):
    planes = 4 * cases * depth
    half = planes * 4
    copies = [pltpu.make_async_copy(state_ref.at[rows(i * half, half), :], out_ref.at[rows(i * half, half), :], sems.at[i]) for i in range(2)]

    def place_tiles(c, refs):
        def one(case, _):
            for block in range(depth // 8):
                offset = pl.multiple_of((c * cases + case) * depth + 8 * block, 8)
                for row in range(8):
                    if refs[row] is not None:
                        ref, place = row_place(refs[row], row, planes)
                        state_ref[strided(offset * 8 + row), :] = ref[rows(place + offset), :]
            return 0

        lax.fori_loop(0, cases, one, 0)

    both = (middle_ref, early_ref)
    for c in range(2):
        place_tiles(c, [both] * 8)
    copies[0].start()
    for c in range(2, 4):
        place_tiles(c, [both if row in MIDDLE else None for row in range(8)])

    def store(c, case, block, offset, tiles):
        for row, tile in tiles.items():
            state_ref[strided(offset * 8 + row), :] = tile

    arrived = Post(place_ref, first_in_ref, second_in_ref)
    outer_rows(depth, cases, planes, (2, 3), loose_ref, arrived, coef_ref, store)
    copies[1].start()
    copies[0].wait()
    copies[1].wait()


def scale_kernel(cells, devices, trans, place_ref, grad_ref, sums_ref, out_ref, lines_ref, shares_ref):
    pad = -(-trans // 8) * 8
    lane, row = lanes_of((8, 128)), rows_of((8, 128))
    zero = jnp.zeros((pad, 128), jnp.float32)
    lines_ref[rows(0, pad), :] = zero
    lines_ref[rows(pad + devices, pad), :] = zero
    lines_ref[rows(pad, devices), :] = sums_ref[...]
    total = jnp.zeros((8, 128), jnp.float32)
    for block in range(devices // 8):
        here = lines_ref[rows(pad + 8 * block), :]
        below, above = lines_ref[rows(pad - trans + 8 * block), :], lines_ref[rows(pad + trans + 8 * block), :]
        share = pltpu.roll(jnp.where(lane < 48, below, above), 96, 1)
        shares_ref[rows(8 * block), :] = share
        corner = here + share
        total += jnp.where(lane < 32, corner * corner, jnp.where(lane >= 64, here, 0.0))
    total = jnp.sum(jnp.sum(total, axis=0, keepdims=True), axis=1, keepdims=True)
    own = jnp.broadcast_to(shares_ref[pl.ds(place_ref[DEVICE], 1), :], (8, 128))
    grad = grad_ref[...]
    edge = (lane < 2) | (lane >= 126)
    for i in (0, 1, 6, 7):
        grad += jnp.where((row == i) & edge, pltpu.roll(own, (126 - 4 * i) % 128, 1), 0.0)
    out_ref[...] = grad / jnp.sqrt(total / cells + 1e-06)


def f32(*shape):
    return jax.ShapeDtypeStruct(shape, jnp.float32)


def in_hbm(array):
    return pltpu.with_memory_space_constraint(array, pltpu.HBM)


def call(kernel, *args, outs, scratch=(), smem=0, hbm=0, hbm_at=None, out=VM):
    specs = [VM] * len(args)
    specs[:smem] = [SM] * smem
    at = smem if hbm_at is None else hbm_at
    specs[at : at + hbm] = [HB] * hbm
    return pl.pallas_call(
        kernel,
        out_shape=outs,
        in_specs=specs,
        out_specs=tuple([out] * len(outs)),
        scratch_shapes=[pltpu.VMEM(shape, jnp.float32) if isinstance(shape, tuple) else shape for shape in scratch],
        compiler_params=PARAMS,
    )(*args)


def neighbours(axis):
    size = lax.axis_size(axis)
    up = [(i, i + 1) for i in range(size - 1)]
    return up, [(j, i) for i, j in up]


def exchange_rows(first, second):
    size = lax.axis_size("roll")
    inner = [(i, i ^ 1) for i in range(size) if i ^ 1 < size]
    outer = [pair for i in range(1, size - 1, 2) for pair in ((i, i + 1), (i + 1, i))]
    return lax.ppermute(first, "roll", inner), lax.ppermute(second, "roll", outer)


def exchange_columns(cols):
    ahead, back = neighbours("trans")
    if lax.axis_size("trans") == 2:
        return lax.ppermute(cols, "trans", ahead + back)
    left, right = lax.ppermute(cols, "trans", ahead), lax.ppermute(cols, "trans", back)
    return jnp.where(lanes_of(cols.shape) % 4 < 2, left, right)


def on_device(adjoint, source, pressure, film, cavity, temp_index):
    components, cases, depth, width_x, width_y = adjoint.shape
    planes = components * cases * depth
    assert (components, width_x, width_y, 4 * depth) == (4, 8, 128, 128)
    state = adjoint.reshape(planes * 8, 128)
    forcing = source.reshape(planes * 8, 128)
    roll, trans, trans_size = lax.axis_index("roll"), lax.axis_index("trans"), lax.axis_size("trans")
    place = jnp.stack([trans, trans_size, roll % 2, roll * trans_size + trans]).astype(jnp.int32)
    devices = lax.axis_size("roll") * trans_size
    inner, part = f32(planes * 8, 128), f32(planes * 4 + 2 * PAD, 128)
    message, cols_shape = f32(planes * 2 + TAIL, 128), f32(components * cases * 8, 128)
    coef, packed, mask = call(
        functools.partial(coefficient_kernel, depth, cases),
        temp_index,
        place,
        pressure.reshape(cases * 8, 128),
        film,
        cavity.reshape(cases * 8, 128),
        outs=(f32(cases * N_COEF * 8, 128), f32(cases * N_PACKED * 8, 128), f32(8, 128)),
        smem=2,
    )
    state, first, second = call(
        functools.partial(send_kernel, depth, cases),
        place,
        in_hbm(state),
        outs=(inner, message, message),
        scratch=[pltpu.SemaphoreType.DMA((PIECES,))],
        smem=1,
        hbm=1,
    )
    middle, outer, cols, forcing = call(
        functools.partial(pack_kernel, depth, cases),
        state,
        in_hbm(forcing),
        outs=(part, part, cols_shape, inner),
        scratch=[pltpu.SemaphoreType.DMA],
        hbm=1,
        hbm_at=1,
    )
    for index in range(SECTIONS):
        more = index < SECTIONS - 1
        first, second = exchange_rows(first, second)
        side = exchange_columns(cols)
        whole, *total = call(
            functools.partial(inner_kernel, depth, cases),
            middle,
            outer,
            forcing,
            coef,
            outs=(inner, f32(cases * 8, 128)) if more else (inner,),
            scratch=[(planes * 8, 256)],
        )
        middle, loose, sums, corr = call(
            functools.partial(sides_kernel, depth, cases, next_moments if more else wall_sums),
            whole,
            side,
            mask,
            packed,
            outs=(part, part, f32(cases * (5 if more else 2) * 8, 128), cols_shape),
        )
        if more:
            outer, first, second, moments = call(
                functools.partial(joined_kernel, depth, cases),
                place,
                loose,
                sums,
                *total,
                first,
                second,
                coef,
                outs=(part, message, message, f32(cases * 3 * 8, 128)),
                scratch=[(cases * 5 * 8, 128)],
                smem=1,
            )
            (cols,) = call(functools.partial(columns_kernel, depth, cases), middle, outer, outs=(cols_shape,))
        else:
            early, grad, sums = call(
                functools.partial(final_kernel, depth, cases),
                place,
                loose,
                sums,
                corr,
                first,
                second,
                coef,
                moments,
                outs=(part, f32(8, 128), pltpu.VMEM((devices, 1, 128), jnp.float32)),
                scratch=[(cases * 2 * 8, 128)],
                smem=1,
            )
            (state,) = call(
                functools.partial(rest_kernel, depth, cases),
                place,
                loose,
                middle,
                early,
                first,
                second,
                coef,
                outs=(pltpu.HBM(inner.shape, jnp.float32),),
                scratch=[inner.shape, pltpu.SemaphoreType.DMA((2,))],
                smem=1,
                out=HB,
            )
    sums = lax.all_to_all(sums, ("roll", "trans"), 0, 0, tiled=True).reshape(devices, 128)
    pad = -(-trans_size // 8) * 8
    (wall_step,) = call(
        functools.partial(scale_kernel, devices * width_x * width_y, devices, trans_size),
        place,
        grad,
        sums,
        outs=(f32(8, 128),),
        scratch=[(devices + 2 * pad, 128), (devices, 128)],
        smem=1,
    )
    return (state.reshape(adjoint.shape), wall_step)


def solution(mesh):
    placed = (
        P(None, None, None, "roll", "trans"),
        P(None, None, None, "roll", "trans"),
        P(None, "roll", "trans"),
        P("roll", "trans"),
        P(None, "roll", "trans"),
        P(),
    )
    return jax.shard_map(
        on_device,
        mesh=mesh,
        in_specs=placed,
        out_specs=(P(None, None, None, "roll", "trans"), P("roll", "trans")),
        check_vma=False,
    )
```

time: 43.9 us -> 42 us (0.957)
  blocking collectives: 18.9 us -> 0 us
  starting transfers between devices: 10.4 us -> 18.7 us
  waiting for transfers between devices: 0.62 us -> 6.58 us
  Pallas kernels: 11.6 us -> 15 us
  local copies, waits for them, and re-layouts: 1.31 us -> 0.66 us
    all_to_all x1 -> x0, blocking collectives: 18.9 us -> none  [on_device(): sums = lax.all_to_all(sums, ('roll', 'trans'), 0, 0, tiled=True)]
    all_to_all x0 -> x1, starting transfers between devices: none -> 10.4 us  [on_device(): lax.all_to_all(sums, ('roll', 'trans'), 0, 0, tiled=True)]
    all_to_all x0 -> x1, waiting for transfers between devices: none -> 5.57 us  [on_device(): lax.all_to_all(sums, ('roll', 'trans'), 0, 0, tiled=True)]
    pallas_call x7 -> x12, Pallas kernels: 11.6 us -> 15 us  [call(): pl.pallas_call(kernel, out_shape=outs, in_specs=specs, out_specs=tuple([o...]
    ppermute x2, starting transfers between devices: 4.98 us -> 3.17 us  [exchange_rows(): lax.ppermute(first, 'roll', inner)]
    unnamed x12 -> x8, local copies, waits for them, and re-layouts: 1.31 us -> 0.66 us
  transfers between devices with their start and end apart: 6 -> 7, of which waited for: 1 -> 2; matrix products, arithmetic and copies ran while one was open for 0% -> 0% of each run, Pallas kernels for 11% -> 22%
where the time goes in v4:
time: 42 us; the launch traced here: 41.8 us
  starting transfers between devices  18.7 us (45%)
  Pallas kernels  15 us (36%)
  waiting for transfers between devices  6.58 us (16%)
  between operations  0.77 us (2%)
  local copies, waits for them, and re-layouts  0.66 us (2%)
    pallas_call x12, Pallas kernels, call(): pl.pallas_call(kernel, out_shape=outs, in_specs=specs, out_specs=tuple([o...  15 us
    all_to_all x1, starting transfers between devices, on_device(): lax.all_to_all(sums, ('roll', 'trans'), 0, 0, tiled=True)  10.4 us
    all_to_all x1, waiting for transfers between devices, on_device(): lax.all_to_all(sums, ('roll', 'trans'), 0, 0, tiled=True)  5.57 us
    ppermute x2, starting transfers between devices, exchange_columns(): return lax.ppermute(cols, 'trans', ahead + back)  3.76 us
    ppermute x2, starting transfers between devices, exchange_rows(): lax.ppermute(first, 'roll', inner)  3.17 us
    ppermute x2, starting transfers between devices, exchange_rows(): lax.ppermute(second, 'roll', outer)  1.33 us
    ppermute x2, waiting for transfers between devices, exchange_columns(): return lax.ppermute(cols, 'trans', ahead + back)  1 us
  transfers between devices with their start and end apart: 7, of which 2 were waited for; matrix products, arithmetic and copies ran while one was open for 0% of the time, Pallas kernels for 22%

profile of v4, /device:TPU:0, one launch (start us, length us, event | category | flops | bytes accessed | tf_op | source)
XLA Modules:
  0.0 41.8 jit_solution(828613813819997802)
XLA Ops:
  0.6 0.1 pad_add_fusion.place_ref
  0.7 1.8 %shard_map.77 = (f32[2048,128]{1,0:T(8,128)S(1)}, f32[536,128]{1,0:T(8,128)S(1)}, f32[536,128]{1,0:T(8,128)S(1)}) custom-call(s32[4]{0:T(128)S(1)} %pad_add_fusion.place_ref, f32[2048,128]{1,0:T(8,128)} %bitcast.12), custom_call_target="tpu_custom_call" | custom-call | tf_op jit(solution)/shard_map/pallas_call | solution.py:606
  2.5 0.5 %collective-permute-start.1 = (f32[536,128]{1,0:T(8,128)S(1)}, f32[536,128]{1,0:T(8,128)S(1)}, u32[]{:S(2)}, u32[]{:S(2)}) collective-permute-start(f32[536,128]{1,0:T(8,128)S(1)} %get-tuple-element.41), channel_id=1, source_target_pairs={{0,2},{2,0},{4,6},{6,4},{8,10},{10,8},{12,14},{14,12},{16,18},{18,... | collective-permute-start | bytes 823304 | tf_op jit(solution)/shard_map/ppermute | solution.py:626
  3.0 0.7 %collective-permute-start.2 = (f32[536,128]{1,0:T(8,128)S(1)}, f32[536,128]{1,0:T(8,128)S(1)}, u32[]{:S(2)}, u32[]{:S(2)}) collective-permute-start(f32[536,128]{1,0:T(8,128)S(1)} %get-tuple-element.42), channel_id=1, source_target_pairs={{2,4},{4,2},{6,8},{8,6},{10,12},{12,10},{14,16},{16,14},{18,20},{2... | collective-permute-start | bytes 823304 | tf_op jit(solution)/shard_map/ppermute | solution.py:626
  3.7 0.0 copy-start
  3.7 1.2 %shard_map.78 = (f32[1040,128]{1,0:T(8,128)S(1)}, f32[1040,128]{1,0:T(8,128)S(1)}, f32[64,128]{1,0:T(8,128)S(1)}, f32[2048,128]{1,0:T(8,128)S(1)}) custom-call(f32[2048,128]{1,0:T(8,128)S(1)} %get-tuple-element.28.state_ref, f32[2048,128]{1,0:T(8,128)} %bitcast.13), custom_call_target="tpu_custom_call" | custom-call | tf_op jit(solution)/shard_map/pallas_call | solution.py:606
  5.0 2.6 %collective-permute-start = (f32[64,128]{1,0:T(8,128)S(1)}, f32[64,128]{1,0:T(8,128)S(1)}, u32[]{:S(2)}, u32[]{:S(2)}) collective-permute-start(f32[64,128]{1,0:T(8,128)S(1)} %get-tuple-element.34), channel_id=1, source_target_pairs={{0,1},{1,0},{2,3},{3,2},{4,5},{5,4},{6,7},{7,6},{8,9},{9,8},{10,11... | collective-permute-start | bytes 98312 | tf_op jit(solution)/shard_map/ppermute | solution.py:632
  7.6 0.6 %copy-done.3 = s32[2]{0:T(128)S(1)} copy-done((s32[2]{0:T(128)S(1)}, s32[2]{0:T(128)}, u32[]{:S(2)}) %copy-start.3) | copy-done | bytes 32
  8.2 0.7 %shard_map.79 = (f32[240,128]{1,0:T(8,128)S(1)}, f32[64,128]{1,0:T(8,128)S(1)}, f32[8,128]{1,0:T(8,128)S(1)}) custom-call(s32[2]{0:T(128)S(1)} %copy-done.3, s32[4]{0:T(128)S(1)} %pad_add_fusion.place_ref, f32[16,128]{1,0:T(8,128)S(1)} %bitcast.10, f32[8,128]{1,0:T(8,128)S(1)} %copy-done.2, s32[16,128]{1,0:T(8,128)S(1)} %bitcast.11), custom_call_target="tpu_custom_call" | custom-call | tf_op jit(solution)/shard_map/pallas_call | solution.py:606
  8.9 1.9 %shard_map.80 = (f32[2048,128]{1,0:T(8,128)S(1)}, f32[16,128]{1,0:T(8,128)S(1)}) custom-call(f32[1040,128]{1,0:T(8,128)S(1)} %get-tuple-element.29.middle_ref, f32[1040,128]{1,0:T(8,128)S(1)} %get-tuple-element.30.outer_ref, f32[2048,128]{1,0:T(8,128)S(1)} %get-tuple-element.31.source_ref, f32[240,128]{1,0:T(8,128)S(1)} %get-tuple-element.32.coef_ref), custom_call_target="tpu_custom_call" | custom-call | tf_op jit(solution)/shard_map/pallas_call | solution.py:606
  10.8 0.9 %shard_map.81 = (f32[1040,128]{1,0:T(8,128)S(1)}, f32[1040,128]{1,0:T(8,128)S(1)}, f32[80,128]{1,0:T(8,128)S(1)}, f32[64,128]{1,0:T(8,128)}) custom-call(f32[2048,128]{1,0:T(8,128)S(1)} %get-tuple-element.33.inner_ref, f32[64,128]{1,0:T(8,128)S(1)} %collective-permute-done.side_ref, f32[8,128]{1,0:T(8,128)S(1)} %get-tuple-element.35.mask_ref, ...), custom_call_target="tpu_custom_call" | custom-call | tf_op jit(solution)/shard_map/pallas_call | solution.py:606
  11.7 0.9 %shard_map.82 = (f32[1040,128]{1,0:T(8,128)S(1)}, f32[536,128]{1,0:T(8,128)S(1)}, f32[536,128]{1,0:T(8,128)S(1)}, f32[48,128]{1,0:T(8,128)S(1)}) custom-call(s32[4]{0:T(128)S(1)} %pad_add_fusion.place_ref, f32[1040,128]{1,0:T(8,128)S(1)} %get-tuple-element.38.loose_ref, f32[80,128]{1,0:T(8,128)S(1)} %get-tuple-element.39.middle_sums_ref, ...), custom_call_target="tpu_custom_call" | custom-call | tf_op jit(solution)/shard_map/pallas_call | solution.py:606
  12.6 2.6 %collective-permute-start.4 = (f32[536,128]{1,0:T(8,128)S(1)}, f32[536,128]{1,0:T(8,128)S(1)}, u32[]{:S(2)}, u32[]{:S(2)}) collective-permute-start(f32[536,128]{1,0:T(8,128)S(1)} %get-tuple-element.48), channel_id=1, source_target_pairs={{0,2},{2,0},{4,6},{6,4},{8,10},{10,8},{12,14},{14,12},{16,18},{18,... | collective-permute-start | bytes 823304 | tf_op jit(solution)/shard_map/ppermute | solution.py:626
  15.3 0.7 %collective-permute-start.5 = (f32[536,128]{1,0:T(8,128)S(1)}, f32[536,128]{1,0:T(8,128)S(1)}, u32[]{:S(2)}, u32[]{:S(2)}) collective-permute-start(f32[536,128]{1,0:T(8,128)S(1)} %get-tuple-element.49), channel_id=1, source_target_pairs={{2,4},{4,2},{6,8},{8,6},{10,12},{12,10},{14,16},{16,14},{18,20},{2... | collective-permute-start | bytes 823304 | tf_op jit(solution)/shard_map/ppermute | solution.py:626
  15.9 0.6 %shard_map.84 = f32[64,128]{1,0:T(8,128)S(1)} custom-call(f32[1040,128]{1,0:T(8,128)S(1)} %get-tuple-element.37.middle_ref, f32[1040,128]{1,0:T(8,128)S(1)} %get-tuple-element.43.outer_ref), custom_call_target="tpu_custom_call" | custom-call | tf_op jit(solution)/shard_map/pallas_call | solution.py:606
  16.5 1.2 %collective-permute-start.3 = (f32[64,128]{1,0:T(8,128)S(1)}, f32[64,128]{1,0:T(8,128)S(1)}, u32[]{:S(2)}, u32[]{:S(2)}) collective-permute-start(f32[64,128]{1,0:T(8,128)S(1)} %shard_map.84), channel_id=1, source_target_pairs={{0,1},{1,0},{2,3},{3,2},{4,5},{5,4},{6,7},{7,6},{8,9},{9,8},{10,11... | collective-permute-start | bytes 98312 | tf_op jit(solution)/shard_map/ppermute | solution.py:632
  17.7 1.8 %shard_map.83.inner_ref = f32[2048,128]{1,0:T(8,128)S(1)} custom-call(f32[1040,128]{1,0:T(8,128)S(1)} %get-tuple-element.37.middle_ref, f32[1040,128]{1,0:T(8,128)S(1)} %get-tuple-element.43.outer_ref, f32[2048,128]{1,0:T(8,128)S(1)} %get-tuple-element.31.source_ref, f32[240,128]{1,0:T(8,128)S(1)} %get-tuple-element.32.coef_ref), custom_call_target="tpu_custom_call" | custom-call | tf_op jit(solution)/shard_map/pallas_call | solution.py:606
  19.5 1.0 %collective-permute-done.3.side_ref = f32[64,128]{1,0:T(8,128)S(1)} collective-permute-done((f32[64,128]{1,0:T(8,128)S(1)}, f32[64,128]{1,0:T(8,128)S(1)}, u32[]{:S(2)}, u32[]{:S(2)}) %collective-permute-start.3) | collective-permute-done | bytes 32800 | tf_op jit(solution)/shard_map/ppermute | solution.py:632
  20.5 0.5 %shard_map.85 = (f32[1040,128]{1,0:T(8,128)S(1)}, f32[1040,128]{1,0:T(8,128)S(1)}, f32[32,128]{1,0:T(8,128)S(1)}, f32[64,128]{1,0:T(8,128)S(1)}) custom-call(f32[2048,128]{1,0:T(8,128)S(1)} %shard_map.83.inner_ref, f32[64,128]{1,0:T(8,128)S(1)} %collective-permute-done.3.side_ref, f32[8,128]{1,0:T(8,128)S(1)} %get-tuple-element.35.mask_ref, ...), custom_call_target="tpu_custom_call" | custom-call | tf_op jit(solution)/shard_map/pallas_call | solution.py:606
  21.1 1.7 %shard_map.86 = (f32[1040,128]{1,0:T(8,128)S(1)}, f32[8,128]{1,0:T(8,128)S(1)}, f32[32,1,128]{2,1,0:T(1,128)}) custom-call(s32[4]{0:T(128)S(1)} %pad_add_fusion.place_ref, f32[1040,128]{1,0:T(8,128)S(1)} %get-tuple-element.44.loose_ref, f32[32,128]{1,0:T(8,128)S(1)} %get-tuple-element.46.middle_sums_ref, f32[64,128]{1,0:T(8,128)S(1)} %get-tuple-element.47.corr_ref, ...), custom_call_target="tpu_custom_call" | custom-call | tf_op jit(solution)/shard_map/pallas_call | solution.py:606
  22.8 10.4 %all-to-all-start = ((f32[32,1,128]{2,1,0:T(1,128)}), f32[32,1,128]{2,1,0:T(1,128)S(1)}, u32[]{:S(2)}, u32[]{:S(2)}) async-start(f32[32,1,128]{2,1,0:T(1,128)} %get-tuple-element.53), calls=%async_computation | async-start | bytes 32768 | tf_op jit(solution)/shard_map/all_to_all | solution.py:741
  33.2 1.6 %shard_map.87 = f32[2048,128]{1,0:T(8,128)} custom-call(s32[4]{0:T(128)S(1)} %pad_add_fusion.place_ref, f32[1040,128]{1,0:T(8,128)S(1)} %get-tuple-element.44.loose_ref, f32[1040,128]{1,0:T(8,128)S(1)} %get-tuple-element.45.middle_ref, f32[1040,128]{1,0:T(8,128)S(1)} %get-tuple-element.51.early_ref, f32[536,128]{1,0:T(8,128)S(1)} %collective-permute-done.4.first_in_ref, ...), custom_call_target="tpu_custom_call" | custom-call | tf_op jit(solution)/shard_map/pallas_call | solution.py:606
  34.9 5.6 %all-to-all-done = f32[32,1,128]{2,1,0:T(1,128)S(1)} async-done(((f32[32,1,128]{2,1,0:T(1,128)}), f32[32,1,128]{2,1,0:T(1,128)S(1)}, u32[]{:S(2)}, u32[]{:S(2)}) %all-to-all-start) | async-done | bytes 16416 | tf_op jit(solution)/shard_map/all_to_all | solution.py:741
  40.4 1.3 %shard_map.88 = f32[8,128]{1,0:T(8,128)} custom-call(s32[4]{0:T(128)S(1)} %pad_add_fusion.place_ref, f32[8,128]{1,0:T(8,128)S(1)} %get-tuple-element.52.grad_ref, f32[32,128]{1,0:T(8,128)S(1)} %bitcast.9), custom_call_target="tpu_custom_call" | custom-call | tf_op jit(solution)/shard_map/pallas_call | solution.py:606
  (11 shorter events, 0.0 us)
Async XLA Ops:
  2.5 9.2 %collective-permute-start.1 = (f32[536,128]{1,0:T(8,128)S(1)}, f32[536,128]{1,0:T(8,128)S(1)}, u32[]{:S(2)}, u32[]{:S(2)}) collective-permute-start(f32[536,128]{1,0:T(8,128)S(1)} %get-tuple-element.41), channel_id=1, source_target_pairs={{0,2},{2,0},{4,6},{6,4},{8,10},{10,8},{12,14},{14,12},{16,18},{18,... | collective-permute-start | bytes 823304 | tf_op jit(solution)/shard_map/ppermute | solution.py:626
  3.0 8.7 %collective-permute-start.2 = (f32[536,128]{1,0:T(8,128)S(1)}, f32[536,128]{1,0:T(8,128)S(1)}, u32[]{:S(2)}, u32[]{:S(2)}) collective-permute-start(f32[536,128]{1,0:T(8,128)S(1)} %get-tuple-element.42), channel_id=1, source_target_pairs={{2,4},{4,2},{6,8},{8,6},{10,12},{12,10},{14,16},{16,14},{18,20},{2... | collective-permute-start | bytes 823304 | tf_op jit(solution)/shard_map/ppermute | solution.py:626
  3.7 3.9 %copy-start = (f32[2,8,128]{2,1,0:T(8,128)S(1)}, f32[2,8,128]{2,1,0:T(8,128)}, u32[]{:S(2)}) copy-start(f32[2,8,128]{2,1,0:T(8,128)} %param.8) | copy-start | bytes 24580
  3.7 3.9 %copy-start.1 = (s32[2,8,128]{2,1,0:T(8,128)S(1)}, s32[2,8,128]{2,1,0:T(8,128)}, u32[]{:S(2)}) copy-start(s32[2,8,128]{2,1,0:T(8,128)} %param.10) | copy-start | bytes 24580
  5.0 2.6 %copy-start.2 = (f32[8,128]{1,0:T(8,128)S(1)}, f32[8,128]{1,0:T(8,128)}, u32[]{:S(2)}) copy-start(f32[8,128]{1,0:T(8,128)} %film_ref.1) | copy-start | bytes 12292
  5.0 5.8 %collective-permute-start = (f32[64,128]{1,0:T(8,128)S(1)}, f32[64,128]{1,0:T(8,128)S(1)}, u32[]{:S(2)}, u32[]{:S(2)}) collective-permute-start(f32[64,128]{1,0:T(8,128)S(1)} %get-tuple-element.34), channel_id=1, source_target_pairs={{0,1},{1,0},{2,3},{3,2},{4,5},{5,4},{6,7},{7,6},{8,9},{9,8},{10,11... | collective-permute-start | bytes 98312 | tf_op jit(solution)/shard_map/ppermute | solution.py:632
  7.6 0.7 %copy-start.3 = (s32[2]{0:T(128)S(1)}, s32[2]{0:T(128)}, u32[]{:S(2)}) copy-start(s32[2]{0:T(128)} %level_ref.1) | copy-start | bytes 28
  12.6 8.4 %collective-permute-start.4 = (f32[536,128]{1,0:T(8,128)S(1)}, f32[536,128]{1,0:T(8,128)S(1)}, u32[]{:S(2)}, u32[]{:S(2)}) collective-permute-start(f32[536,128]{1,0:T(8,128)S(1)} %get-tuple-element.48), channel_id=1, source_target_pairs={{0,2},{2,0},{4,6},{6,4},{8,10},{10,8},{12,14},{14,12},{16,18},{18,... | collective-permute-start | bytes 823304 | tf_op jit(solution)/shard_map/ppermute | solution.py:626
  15.3 5.8 %collective-permute-start.5 = (f32[536,128]{1,0:T(8,128)S(1)}, f32[536,128]{1,0:T(8,128)S(1)}, u32[]{:S(2)}, u32[]{:S(2)}) collective-permute-start(f32[536,128]{1,0:T(8,128)S(1)} %get-tuple-element.49), channel_id=1, source_target_pairs={{2,4},{4,2},{6,8},{8,6},{10,12},{12,10},{14,16},{16,14},{18,20},{2... | collective-permute-start | bytes 823304 | tf_op jit(solution)/shard_map/ppermute | solution.py:626
  16.5 4.0 %collective-permute-start.3 = (f32[64,128]{1,0:T(8,128)S(1)}, f32[64,128]{1,0:T(8,128)S(1)}, u32[]{:S(2)}, u32[]{:S(2)}) collective-permute-start(f32[64,128]{1,0:T(8,128)S(1)} %shard_map.84), channel_id=1, source_target_pairs={{0,1},{1,0},{2,3},{3,2},{4,5},{5,4},{6,7},{7,6},{8,9},{9,8},{10,11... | collective-permute-start | bytes 98312 | tf_op jit(solution)/shard_map/ppermute | solution.py:632
  22.8 17.6 %all-to-all-start = ((f32[32,1,128]{2,1,0:T(1,128)}), f32[32,1,128]{2,1,0:T(1,128)S(1)}, u32[]{:S(2)}, u32[]{:S(2)}) async-start(f32[32,1,128]{2,1,0:T(1,128)} %get-tuple-element.53), calls=%async_computation | async-start | bytes 32768 | tf_op jit(solution)/shard_map/all_to_all | solution.py:741

commit v5 on v4

--- a/solution.py
+++ b/solution.py
@@ -20,7 +20,6 @@
 COURANT = 0.8
 
 VM = pl.BlockSpec(memory_space=pltpu.VMEM)
-SM = pl.BlockSpec(memory_space=pltpu.SMEM)
 HB = pl.BlockSpec(memory_space=pltpu.HBM)
 PARAMS = pltpu.CompilerParams(vmem_limit_bytes=16 * 1024 * 1024)
 
@@ -56,7 +55,7 @@
     lane, row = lanes_of((8, 128)), rows_of((8, 128))
     film = film_ref[...]
     for case in range(cases):
-        theta = THETA_STEP * level_ref[case].astype(jnp.float32)
+        theta = THETA_STEP * level_ref[rows(case * 8), :].astype(jnp.float32)
         viscosity = jnp.exp(VISCOSITY_PRESS * pressure_ref[rows(case * 8), :] - VISCOSITY_TEMP * theta)
         film_coef = 4.0 * viscosity / (film * film)
         density = 1.0 - 0.6 * cavity_ref[rows(case * 8), :].astype(jnp.float32)
@@ -78,8 +77,9 @@
         packed = exact_dot(wanted, edge_columns())
         for i in range(N_PACKED):
             packed_ref[rows((case * N_PACKED + i) * 8), :] = packed[i * 8 : i * 8 + 8]
-    from_left = jnp.where(place_ref[TRANS] > 0, 1.0, 0.0)
-    from_right = jnp.where(place_ref[TRANS] < place_ref[TRANS_SIZE] - 1, 1.0, 0.0)
+    trans = place_ref[rows(TRANS * 8), :]
+    from_left = jnp.where(trans > 0, 1.0, 0.0)
+    from_right = jnp.where(trans < place_ref[rows(TRANS_SIZE * 8), :] - 1, 1.0, 0.0)
     mask_ref[...] = jnp.where(lane % 4 < 2, from_left, from_right)
 
 
@@ -104,17 +104,19 @@
 
 class Post:
     def __init__(self, place_ref, first_ref, second_ref):
-        self.odd = place_ref[ODD] == 1
+        self.odd = place_ref[rows(ODD * 8), :] == 1
         self.refs = first_ref, second_ref
 
     def put(self, where, up, down):
         first, second = self.refs
-        first[where, :] = jnp.where(self.odd, down, up)
-        second[where, :] = jnp.where(self.odd, up, down)
+        odd = self.odd[: where.size]
+        first[where, :] = jnp.where(odd, down, up)
+        second[where, :] = jnp.where(odd, up, down)
 
     def get(self, where):
         first, second = (ref[where, :] for ref in self.refs)
-        return jnp.where(self.odd, first, second), jnp.where(self.odd, second, first)
+        odd = self.odd[: where.size]
+        return jnp.where(odd, first, second), jnp.where(odd, second, first)
 
     def put_tiles(self, planes, first, tiles):
         for i in range(2):
@@ -566,23 +568,24 @@
     copies[1].wait()
 
 
-def scale_kernel(cells, devices, trans, place_ref, grad_ref, sums_ref, out_ref, lines_ref, shares_ref):
+def scale_kernel(cells, devices, trans, place_ref, grad_ref, sums_ref, out_ref, lines_ref):
     pad = -(-trans // 8) * 8
     lane, row = lanes_of((8, 128)), rows_of((8, 128))
     zero = jnp.zeros((pad, 128), jnp.float32)
     lines_ref[rows(0, pad), :] = zero
     lines_ref[rows(pad + devices, pad), :] = zero
     lines_ref[rows(pad, devices), :] = sums_ref[...]
-    total = jnp.zeros((8, 128), jnp.float32)
+    total, own = jnp.zeros((8, 128), jnp.float32), jnp.zeros((8, 128), jnp.float32)
+    device = place_ref[rows(DEVICE * 8), :]
     for block in range(devices // 8):
         here = lines_ref[rows(pad + 8 * block), :]
         below, above = lines_ref[rows(pad - trans + 8 * block), :], lines_ref[rows(pad + trans + 8 * block), :]
         share = pltpu.roll(jnp.where(lane < 48, below, above), 96, 1)
-        shares_ref[rows(8 * block), :] = share
+        own += jnp.where(row + 8 * block == device, share, 0.0)
         corner = here + share
         total += jnp.where(lane < 32, corner * corner, jnp.where(lane >= 64, here, 0.0))
     total = jnp.sum(jnp.sum(total, axis=0, keepdims=True), axis=1, keepdims=True)
-    own = jnp.broadcast_to(shares_ref[pl.ds(place_ref[DEVICE], 1), :], (8, 128))
+    own = jnp.broadcast_to(jnp.sum(own, axis=0, keepdims=True), (8, 128))
     grad = grad_ref[...]
     edge = (lane < 2) | (lane >= 126)
     for i in (0, 1, 6, 7):
@@ -594,15 +597,22 @@
     return jax.ShapeDtypeStruct(shape, jnp.float32)
 
 
+def over_tiles(numbers):
+    which = rows_of((8 * len(numbers), 128)) // 8
+    held = jnp.full(which.shape, numbers[0], jnp.int32)
+    for i, number in enumerate(numbers[1:], 1):
+        held = jnp.where(which == i, number, held)
+    return held
+
+
 def in_hbm(array):
     return pltpu.with_memory_space_constraint(array, pltpu.HBM)
 
 
-def call(kernel, *args, outs, scratch=(), smem=0, hbm=0, hbm_at=None, out=VM):
+def call(kernel, *args, outs, scratch=(), hbm=None, out=VM):
     specs = [VM] * len(args)
-    specs[:smem] = [SM] * smem
-    at = smem if hbm_at is None else hbm_at
-    specs[at : at + hbm] = [HB] * hbm
+    if hbm is not None:
+        specs[hbm] = HB
     return pl.pallas_call(
         kernel,
         out_shape=outs,
@@ -641,19 +651,19 @@
     state = adjoint.reshape(planes * 8, 128)
     forcing = source.reshape(planes * 8, 128)
     roll, trans, trans_size = lax.axis_index("roll"), lax.axis_index("trans"), lax.axis_size("trans")
-    place = jnp.stack([trans, trans_size, roll % 2, roll * trans_size + trans]).astype(jnp.int32)
+    place = over_tiles([trans, trans_size, roll % 2, roll * trans_size + trans])
+    level = jnp.broadcast_to(temp_index[:, None, None], (cases, 8, 128)).reshape(cases * 8, 128)
     devices = lax.axis_size("roll") * trans_size
     inner, part = f32(planes * 8, 128), f32(planes * 4 + 2 * PAD, 128)
     message, cols_shape = f32(planes * 2 + TAIL, 128), f32(components * cases * 8, 128)
     coef, packed, mask = call(
         functools.partial(coefficient_kernel, depth, cases),
-        temp_index,
+        level,
         place,
         pressure.reshape(cases * 8, 128),
         film,
         cavity.reshape(cases * 8, 128),
         outs=(f32(cases * N_COEF * 8, 128), f32(cases * N_PACKED * 8, 128), f32(8, 128)),
-        smem=2,
     )
     state, first, second = call(
         functools.partial(send_kernel, depth, cases),
@@ -661,7 +671,6 @@
         in_hbm(state),
         outs=(inner, message, message),
         scratch=[pltpu.SemaphoreType.DMA((PIECES,))],
-        smem=1,
         hbm=1,
     )
     middle, outer, cols, forcing = call(
@@ -671,7 +680,6 @@
         outs=(part, part, cols_shape, inner),
         scratch=[pltpu.SemaphoreType.DMA],
         hbm=1,
-        hbm_at=1,
     )
     for index in range(SECTIONS):
         more = index < SECTIONS - 1
@@ -706,7 +714,6 @@
                 coef,
                 outs=(part, message, message, f32(cases * 3 * 8, 128)),
                 scratch=[(cases * 5 * 8, 128)],
-                smem=1,
             )
             (cols,) = call(functools.partial(columns_kernel, depth, cases), middle, outer, outs=(cols_shape,))
         else:
@@ -722,7 +729,6 @@
                 moments,
                 outs=(part, f32(8, 128), pltpu.VMEM((devices, 1, 128), jnp.float32)),
                 scratch=[(cases * 2 * 8, 128)],
-                smem=1,
             )
             (state,) = call(
                 functools.partial(rest_kernel, depth, cases),
@@ -735,7 +741,6 @@
                 coef,
                 outs=(pltpu.HBM(inner.shape, jnp.float32),),
                 scratch=[inner.shape, pltpu.SemaphoreType.DMA((2,))],
-                smem=1,
                 out=HB,
             )
     sums = lax.all_to_all(sums, ("roll", "trans"), 0, 0, tiled=True).reshape(devices, 128)
@@ -746,8 +751,7 @@
         grad,
         sums,
         outs=(f32(8, 128),),
-        scratch=[(devices + 2 * pad, 128), (devices, 128)],
-        smem=1,
+        scratch=[(devices + 2 * pad, 128)],
     )
     return (state.reshape(adjoint.shape), wall_step)
 

time: 42 us -> 39.9 us (0.950)
  Pallas kernels: 15 us -> 11.7 us
  starting transfers between devices: 18.7 us -> 20 us
    pallas_call x12, Pallas kernels: 15 us -> 11.7 us  [call(): pl.pallas_call(kernel, out_shape=outs, in_specs=specs, out_specs=tuple([o...]
    unnamed x8, local copies, waits for them, and re-layouts: 0.66 us -> 0.03 us
    ppermute x2, starting transfers between devices: 3.17 us -> 3.74 us  [exchange_rows(): lax.ppermute(first, 'roll', inner)]
    all_to_all x1, waiting for transfers between devices: 5.57 us -> 6.1 us  [on_device(): lax.all_to_all(sums, ('roll', 'trans'), 0, 0, tiled=True)]
  transfers between devices with their start and end apart: 7 -> 7, of which waited for: 2 -> 2; matrix products, arithmetic and copies ran while one was open for 0% -> 1% of each run, Pallas kernels for 22% -> 21%
where the time goes in v5:
time: 39.9 us; the launch traced here: 39.6 us
  starting transfers between devices  20 us (50%)
  Pallas kernels  11.7 us (29%)
  waiting for transfers between devices  6.73 us (17%)
  between operations  0.81 us (2%)
    pallas_call x12, Pallas kernels, call(): pl.pallas_call(kernel, out_shape=outs, in_specs=specs, out_specs=tuple([o...  11.7 us
    all_to_all x1, starting transfers between devices, on_device(): lax.all_to_all(sums, ('roll', 'trans'), 0, 0, tiled=True)  10.8 us
    all_to_all x1, waiting for transfers between devices, on_device(): lax.all_to_all(sums, ('roll', 'trans'), 0, 0, tiled=True)  6.1 us
    ppermute x2, starting transfers between devices, exchange_columns(): return lax.ppermute(cols, 'trans', ahead + back)  4.13 us
    ppermute x2, starting transfers between devices, exchange_rows(): lax.ppermute(first, 'roll', inner)  3.74 us
    ppermute x2, starting transfers between devices, exchange_rows(): lax.ppermute(second, 'roll', outer)  1.33 us
  transfers between devices with their start and end apart: 7, of which 2 were waited for; matrix products, arithmetic and copies ran while one was open for 1% of the time, Pallas kernels for 21%

profile of v5, /device:TPU:0, one launch (start us, length us, event | category | flops | bytes accessed | tf_op | source)
XLA Modules:
  0.0 39.6 jit_solution(10611025231690718436)
XLA Ops:
  0.7 0.1 select_select_fusion.place_ref
  0.8 1.2 %shard_map.77 = (f32[2048,128]{1,0:T(8,128)S(1)}, f32[536,128]{1,0:T(8,128)S(1)}, f32[536,128]{1,0:T(8,128)S(1)}) custom-call(s32[32,128]{1,0:T(8,128)S(1)} %select_select_fusion.place_ref, f32[2048,128]{1,0:T(8,128)} %bitcast.10), custom_call_target="tpu_custom_call" | custom-call | tf_op jit(solution)/shard_map/pallas_call | solution.py:616
  2.0 0.5 %collective-permute-start.1 = (f32[536,128]{1,0:T(8,128)S(1)}, f32[536,128]{1,0:T(8,128)S(1)}, u32[]{:S(2)}, u32[]{:S(2)}) collective-permute-start(f32[536,128]{1,0:T(8,128)S(1)} %get-tuple-element.41), channel_id=1, source_target_pairs={{0,2},{2,0},{4,6},{6,4},{8,10},{10,8},{12,14},{14,12},{16,18},{18,... | collective-permute-start | bytes 823304 | tf_op jit(solution)/shard_map/ppermute | solution.py:636
  2.5 0.7 %collective-permute-start.2 = (f32[536,128]{1,0:T(8,128)S(1)}, f32[536,128]{1,0:T(8,128)S(1)}, u32[]{:S(2)}, u32[]{:S(2)}) collective-permute-start(f32[536,128]{1,0:T(8,128)S(1)} %get-tuple-element.42), channel_id=1, source_target_pairs={{2,4},{4,2},{6,8},{8,6},{10,12},{12,10},{14,16},{16,14},{18,20},{2... | collective-permute-start | bytes 823304 | tf_op jit(solution)/shard_map/ppermute | solution.py:636
  3.2 1.2 %shard_map.78 = (f32[1040,128]{1,0:T(8,128)S(1)}, f32[1040,128]{1,0:T(8,128)S(1)}, f32[64,128]{1,0:T(8,128)S(1)}, f32[2048,128]{1,0:T(8,128)S(1)}) custom-call(f32[2048,128]{1,0:T(8,128)S(1)} %get-tuple-element.28.state_ref, f32[2048,128]{1,0:T(8,128)} %bitcast.11), custom_call_target="tpu_custom_call" | custom-call | tf_op jit(solution)/shard_map/pallas_call | solution.py:616
  4.5 2.6 %collective-permute-start = (f32[64,128]{1,0:T(8,128)S(1)}, f32[64,128]{1,0:T(8,128)S(1)}, u32[]{:S(2)}, u32[]{:S(2)}) collective-permute-start(f32[64,128]{1,0:T(8,128)S(1)} %get-tuple-element.34), channel_id=1, source_target_pairs={{0,1},{1,0},{2,3},{3,2},{4,5},{5,4},{6,7},{7,6},{8,9},{9,8},{10,11... | collective-permute-start | bytes 98312 | tf_op jit(solution)/shard_map/ppermute | solution.py:642
  7.2 0.1 broadcast_in_dim.26
  7.2 0.1 broadcast_in_dim.27.level_ref
  7.3 0.2 shard_map.79
  7.5 1.9 %shard_map.80 = (f32[2048,128]{1,0:T(8,128)S(1)}, f32[16,128]{1,0:T(8,128)S(1)}) custom-call(f32[1040,128]{1,0:T(8,128)S(1)} %get-tuple-element.29.middle_ref, f32[1040,128]{1,0:T(8,128)S(1)} %get-tuple-element.30.outer_ref, f32[2048,128]{1,0:T(8,128)S(1)} %get-tuple-element.31.source_ref, f32[240,128]{1,0:T(8,128)S(1)} %get-tuple-element.32.coef_ref), custom_call_target="tpu_custom_call" | custom-call | tf_op jit(solution)/shard_map/pallas_call | solution.py:616
  9.4 0.9 %shard_map.81 = (f32[1040,128]{1,0:T(8,128)S(1)}, f32[1040,128]{1,0:T(8,128)S(1)}, f32[80,128]{1,0:T(8,128)S(1)}, f32[64,128]{1,0:T(8,128)}) custom-call(f32[2048,128]{1,0:T(8,128)S(1)} %get-tuple-element.33.inner_ref, f32[64,128]{1,0:T(8,128)S(1)} %collective-permute-done.side_ref, f32[8,128]{1,0:T(8,128)S(1)} %get-tuple-element.35.mask_ref, ...), custom_call_target="tpu_custom_call" | custom-call | tf_op jit(solution)/shard_map/pallas_call | solution.py:616
  10.3 0.3 shard_map.82
  10.6 3.2 %collective-permute-start.4 = (f32[536,128]{1,0:T(8,128)S(1)}, f32[536,128]{1,0:T(8,128)S(1)}, u32[]{:S(2)}, u32[]{:S(2)}) collective-permute-start(f32[536,128]{1,0:T(8,128)S(1)} %get-tuple-element.48), channel_id=1, source_target_pairs={{0,2},{2,0},{4,6},{6,4},{8,10},{10,8},{12,14},{14,12},{16,18},{18,... | collective-permute-start | bytes 823304 | tf_op jit(solution)/shard_map/ppermute | solution.py:636
  13.8 0.7 %collective-permute-start.5 = (f32[536,128]{1,0:T(8,128)S(1)}, f32[536,128]{1,0:T(8,128)S(1)}, u32[]{:S(2)}, u32[]{:S(2)}) collective-permute-start(f32[536,128]{1,0:T(8,128)S(1)} %get-tuple-element.49), channel_id=1, source_target_pairs={{2,4},{4,2},{6,8},{8,6},{10,12},{12,10},{14,16},{16,14},{18,20},{2... | collective-permute-start | bytes 823304 | tf_op jit(solution)/shard_map/ppermute | solution.py:636
  14.5 0.6 %shard_map.84 = f32[64,128]{1,0:T(8,128)S(1)} custom-call(f32[1040,128]{1,0:T(8,128)S(1)} %get-tuple-element.37.middle_ref, f32[1040,128]{1,0:T(8,128)S(1)} %get-tuple-element.43.outer_ref), custom_call_target="tpu_custom_call" | custom-call | tf_op jit(solution)/shard_map/pallas_call | solution.py:616
  15.1 1.6 %collective-permute-start.3 = (f32[64,128]{1,0:T(8,128)S(1)}, f32[64,128]{1,0:T(8,128)S(1)}, u32[]{:S(2)}, u32[]{:S(2)}) collective-permute-start(f32[64,128]{1,0:T(8,128)S(1)} %shard_map.84), channel_id=1, source_target_pairs={{0,1},{1,0},{2,3},{3,2},{4,5},{5,4},{6,7},{7,6},{8,9},{9,8},{10,11... | collective-permute-start | bytes 98312 | tf_op jit(solution)/shard_map/ppermute | solution.py:642
  16.7 1.8 %shard_map.83.inner_ref = f32[2048,128]{1,0:T(8,128)S(1)} custom-call(f32[1040,128]{1,0:T(8,128)S(1)} %get-tuple-element.37.middle_ref, f32[1040,128]{1,0:T(8,128)S(1)} %get-tuple-element.43.outer_ref, f32[2048,128]{1,0:T(8,128)S(1)} %get-tuple-element.31.source_ref, f32[240,128]{1,0:T(8,128)S(1)} %get-tuple-element.32.coef_ref), custom_call_target="tpu_custom_call" | custom-call | tf_op jit(solution)/shard_map/pallas_call | solution.py:616
  18.5 0.6 %collective-permute-done.3.side_ref = f32[64,128]{1,0:T(8,128)S(1)} collective-permute-done((f32[64,128]{1,0:T(8,128)S(1)}, f32[64,128]{1,0:T(8,128)S(1)}, u32[]{:S(2)}, u32[]{:S(2)}) %collective-permute-start.3) | collective-permute-done | bytes 32800 | tf_op jit(solution)/shard_map/ppermute | solution.py:642
  19.1 0.5 %shard_map.85 = (f32[1040,128]{1,0:T(8,128)S(1)}, f32[1040,128]{1,0:T(8,128)S(1)}, f32[32,128]{1,0:T(8,128)S(1)}, f32[64,128]{1,0:T(8,128)S(1)}) custom-call(f32[2048,128]{1,0:T(8,128)S(1)} %shard_map.83.inner_ref, f32[64,128]{1,0:T(8,128)S(1)} %collective-permute-done.3.side_ref, f32[8,128]{1,0:T(8,128)S(1)} %get-tuple-element.35.mask_ref, ...), custom_call_target="tpu_custom_call" | custom-call | tf_op jit(solution)/shard_map/pallas_call | solution.py:616
  19.7 1.2 %shard_map.86 = (f32[1040,128]{1,0:T(8,128)S(1)}, f32[8,128]{1,0:T(8,128)S(1)}, f32[32,1,128]{2,1,0:T(1,128)}) custom-call(s32[32,128]{1,0:T(8,128)S(1)} %select_select_fusion.place_ref, f32[1040,128]{1,0:T(8,128)S(1)} %get-tuple-element.44.loose_ref, f32[32,128]{1,0:T(8,128)S(1)} %get-tuple-element.46.middle_sums_ref, ...), custom_call_target="tpu_custom_call" | custom-call | tf_op jit(solution)/shard_map/pallas_call | solution.py:616
  20.9 10.8 %all-to-all-start = ((f32[32,1,128]{2,1,0:T(1,128)}), f32[32,1,128]{2,1,0:T(1,128)S(1)}, u32[]{:S(2)}, u32[]{:S(2)}) async-start(f32[32,1,128]{2,1,0:T(1,128)} %get-tuple-element.53), calls=%async_computation | async-start | bytes 32768 | tf_op jit(solution)/shard_map/all_to_all | solution.py:746
  31.7 1.1 %shard_map.87 = f32[2048,128]{1,0:T(8,128)} custom-call(s32[32,128]{1,0:T(8,128)S(1)} %select_select_fusion.place_ref, f32[1040,128]{1,0:T(8,128)S(1)} %get-tuple-element.44.loose_ref, f32[1040,128]{1,0:T(8,128)S(1)} %get-tuple-element.45.middle_ref, f32[1040,128]{1,0:T(8,128)S(1)} %get-tuple-element.51.early_ref, ...), custom_call_target="tpu_custom_call" | custom-call | tf_op jit(solution)/shard_map/pallas_call | solution.py:616
  32.7 6.1 %all-to-all-done = f32[32,1,128]{2,1,0:T(1,128)S(1)} async-done(((f32[32,1,128]{2,1,0:T(1,128)}), f32[32,1,128]{2,1,0:T(1,128)S(1)}, u32[]{:S(2)}, u32[]{:S(2)}) %all-to-all-start) | async-done | bytes 16416 | tf_op jit(solution)/shard_map/all_to_all | solution.py:746
  38.8 0.8 %shard_map.88 = f32[8,128]{1,0:T(8,128)} custom-call(s32[32,128]{1,0:T(8,128)S(1)} %select_select_fusion.place_ref, f32[8,128]{1,0:T(8,128)S(1)} %get-tuple-element.52.grad_ref, f32[32,128]{1,0:T(8,128)S(1)} %bitcast.6), custom_call_target="tpu_custom_call" | custom-call | tf_op jit(solution)/shard_map/pallas_call | solution.py:616
  (16 shorter events, 0.1 us)
Async XLA Ops:
  2.0 8.3 %collective-permute-start.1 = (f32[536,128]{1,0:T(8,128)S(1)}, f32[536,128]{1,0:T(8,128)S(1)}, u32[]{:S(2)}, u32[]{:S(2)}) collective-permute-start(f32[536,128]{1,0:T(8,128)S(1)} %get-tuple-element.41), channel_id=1, source_target_pairs={{0,2},{2,0},{4,6},{6,4},{8,10},{10,8},{12,14},{14,12},{16,18},{18,... | collective-permute-start | bytes 823304 | tf_op jit(solution)/shard_map/ppermute | solution.py:636
  2.5 7.8 %collective-permute-start.2 = (f32[536,128]{1,0:T(8,128)S(1)}, f32[536,128]{1,0:T(8,128)S(1)}, u32[]{:S(2)}, u32[]{:S(2)}) collective-permute-start(f32[536,128]{1,0:T(8,128)S(1)} %get-tuple-element.42), channel_id=1, source_target_pairs={{2,4},{4,2},{6,8},{8,6},{10,12},{12,10},{14,16},{16,14},{18,20},{2... | collective-permute-start | bytes 823304 | tf_op jit(solution)/shard_map/ppermute | solution.py:636
  3.2 4.1 %copy-start.2 = (f32[8,128]{1,0:T(8,128)S(1)}, f32[8,128]{1,0:T(8,128)}, u32[]{:S(2)}) copy-start(f32[8,128]{1,0:T(8,128)} %film_ref.1) | copy-start | bytes 12292
  4.5 2.6 %copy-start.3 = (s32[2]{0:T(128)S(1)}, s32[2]{0:T(128)}, u32[]{:S(2)}) copy-start(s32[2]{0:T(128)} %param.11) | copy-start | bytes 28
  4.5 2.8 %copy-start = (f32[2,8,128]{2,1,0:T(8,128)S(1)}, f32[2,8,128]{2,1,0:T(8,128)}, u32[]{:S(2)}) copy-start(f32[2,8,128]{2,1,0:T(8,128)} %param.8) | copy-start | bytes 24580
  4.5 2.8 %copy-start.1 = (s32[2,8,128]{2,1,0:T(8,128)S(1)}, s32[2,8,128]{2,1,0:T(8,128)}, u32[]{:S(2)}) copy-start(s32[2,8,128]{2,1,0:T(8,128)} %param.10) | copy-start | bytes 24580
  4.5 4.8 %collective-permute-start = (f32[64,128]{1,0:T(8,128)S(1)}, f32[64,128]{1,0:T(8,128)S(1)}, u32[]{:S(2)}, u32[]{:S(2)}) collective-permute-start(f32[64,128]{1,0:T(8,128)S(1)} %get-tuple-element.34), channel_id=1, source_target_pairs={{0,1},{1,0},{2,3},{3,2},{4,5},{5,4},{6,7},{7,6},{8,9},{9,8},{10,11... | collective-permute-start | bytes 98312 | tf_op jit(solution)/shard_map/ppermute | solution.py:642
  10.6 9.0 %collective-permute-start.4 = (f32[536,128]{1,0:T(8,128)S(1)}, f32[536,128]{1,0:T(8,128)S(1)}, u32[]{:S(2)}, u32[]{:S(2)}) collective-permute-start(f32[536,128]{1,0:T(8,128)S(1)} %get-tuple-element.48), channel_id=1, source_target_pairs={{0,2},{2,0},{4,6},{6,4},{8,10},{10,8},{12,14},{14,12},{16,18},{18,... | collective-permute-start | bytes 823304 | tf_op jit(solution)/shard_map/ppermute | solution.py:636
  13.8 5.8 %collective-permute-start.5 = (f32[536,128]{1,0:T(8,128)S(1)}, f32[536,128]{1,0:T(8,128)S(1)}, u32[]{:S(2)}, u32[]{:S(2)}) collective-permute-start(f32[536,128]{1,0:T(8,128)S(1)} %get-tuple-element.49), channel_id=1, source_target_pairs={{2,4},{4,2},{6,8},{8,6},{10,12},{12,10},{14,16},{16,14},{18,20},{2... | collective-permute-start | bytes 823304 | tf_op jit(solution)/shard_map/ppermute | solution.py:636
  15.1 4.0 %collective-permute-start.3 = (f32[64,128]{1,0:T(8,128)S(1)}, f32[64,128]{1,0:T(8,128)S(1)}, u32[]{:S(2)}, u32[]{:S(2)}) collective-permute-start(f32[64,128]{1,0:T(8,128)S(1)} %shard_map.84), channel_id=1, source_target_pairs={{0,1},{1,0},{2,3},{3,2},{4,5},{5,4},{6,7},{7,6},{8,9},{9,8},{10,11... | collective-permute-start | bytes 98312 | tf_op jit(solution)/shard_map/ppermute | solution.py:642
  20.9 18.0 %all-to-all-start = ((f32[32,1,128]{2,1,0:T(1,128)}), f32[32,1,128]{2,1,0:T(1,128)S(1)}, u32[]{:S(2)}, u32[]{:S(2)}) async-start(f32[32,1,128]{2,1,0:T(1,128)} %get-tuple-element.53), calls=%async_computation | async-start | bytes 32768 | tf_op jit(solution)/shard_map/all_to_all | solution.py:746

commit v6 on v5

--- a/solution.py
+++ b/solution.py
@@ -396,12 +396,12 @@
     loose_ref,
     middle_sums_ref,
     source_total_ref,
+    second_in_ref,
     first_in_ref,
-    second_in_ref,
     coef_ref,
     outer_ref,
+    second_ref,
     first_ref,
-    second_ref,
     moment_ref,
     outer_sums_ref,
 ):
@@ -458,8 +458,8 @@
     loose_ref,
     middle_sums_ref,
     corr_ref,
+    second_in_ref,
     first_in_ref,
-    second_in_ref,
     coef_ref,
     moment_ref,
     outer_ref,
@@ -527,8 +527,8 @@
     loose_ref,
     middle_ref,
     early_ref,
+    second_in_ref,
     first_in_ref,
-    second_in_ref,
     coef_ref,
     out_ref,
     state_ref,
@@ -633,7 +633,8 @@
     size = lax.axis_size("roll")
     inner = [(i, i ^ 1) for i in range(size) if i ^ 1 < size]
     outer = [pair for i in range(1, size - 1, 2) for pair in ((i, i + 1), (i + 1, i))]
-    return lax.ppermute(first, "roll", inner), lax.ppermute(second, "roll", outer)
+    second = lax.ppermute(second, "roll", outer)
+    return lax.ppermute(first, "roll", inner), second
 
 
 def exchange_columns(cols):
@@ -703,14 +704,14 @@
             outs=(part, part, f32(cases * (5 if more else 2) * 8, 128), cols_shape),
         )
         if more:
-            outer, first, second, moments = call(
+            outer, second, first, moments = call(
                 functools.partial(joined_kernel, depth, cases),
                 place,
                 loose,
                 sums,
                 *total,
+                second,
                 first,
-                second,
                 coef,
                 outs=(part, message, message, f32(cases * 3 * 8, 128)),
                 scratch=[(cases * 5 * 8, 128)],
@@ -723,8 +724,8 @@
                 loose,
                 sums,
                 corr,
+                second,
                 first,
-                second,
                 coef,
                 moments,
                 outs=(part, f32(8, 128), pltpu.VMEM((devices, 1, 128), jnp.float32)),
@@ -736,8 +737,8 @@
                 loose,
                 middle,
                 early,
+                second,
                 first,
-                second,
                 coef,
                 outs=(pltpu.HBM(inner.shape, jnp.float32),),
                 scratch=[inner.shape, pltpu.SemaphoreType.DMA((2,))],

time: 39.9 us -> 39 us (0.977)
  starting transfers between devices: 20 us -> 19 us
    ppermute x4, starting transfers between devices: 5.07 us -> 9.6 us  [the longest x2 8.25 us: exchange_rows(): return (lax.ppermute(first, 'roll', inner), second)]
    all_to_all x1, starting transfers between devices: 10.8 us -> 6.29 us  [on_device(): lax.all_to_all(sums, ('roll', 'trans'), 0, 0, tiled=True)]
    ppermute x2, starting transfers between devices: 4.13 us -> 3.11 us  [exchange_columns(): return lax.ppermute(cols, 'trans', ahead + back)]
  transfers between devices with their start and end apart: 7 -> 7, of which waited for: 2 -> 3; matrix products, arithmetic and copies ran while one was open for 1% -> 1% of each run, Pallas kernels for 21% -> 21%
where the time goes in v6:
time: 39 us; the launch traced here: 38.8 us
  starting transfers between devices  19 us (49%)
  Pallas kernels  11.7 us (30%)
  waiting for transfers between devices  6.89 us (18%)
  between operations  0.79 us (2%)
    pallas_call x12, Pallas kernels, call(): pl.pallas_call(kernel, out_shape=outs, in_specs=specs, out_specs=tuple([o...  11.7 us
    ppermute x2, starting transfers between devices, exchange_rows(): return (lax.ppermute(first, 'roll', inner), second)  8.25 us
    all_to_all x1, starting transfers between devices, on_device(): lax.all_to_all(sums, ('roll', 'trans'), 0, 0, tiled=True)  6.29 us
    all_to_all x1, waiting for transfers between devices, on_device(): lax.all_to_all(sums, ('roll', 'trans'), 0, 0, tiled=True)  6.1 us
    ppermute x2, starting transfers between devices, exchange_columns(): return lax.ppermute(cols, 'trans', ahead + back)  3.11 us
    ppermute x2, starting transfers between devices, exchange_rows(): second = lax.ppermute(second, 'roll', outer)  1.36 us
  transfers between devices with their start and end apart: 7, of which 3 were waited for; matrix products, arithmetic and copies ran while one was open for 1% of the time, Pallas kernels for 21%

profile of v6, /device:TPU:0, one launch (start us, length us, event | category | flops | bytes accessed | tf_op | source)
XLA Modules:
  0.0 38.8 jit_solution(11878842268690316303)
XLA Ops:
  0.7 0.1 select_select_fusion.place_ref
  0.8 1.2 %shard_map.77 = (f32[2048,128]{1,0:T(8,128)S(1)}, f32[536,128]{1,0:T(8,128)S(1)}, f32[536,128]{1,0:T(8,128)S(1)}) custom-call(s32[32,128]{1,0:T(8,128)S(1)} %select_select_fusion.place_ref, f32[2048,128]{1,0:T(8,128)} %bitcast.10), custom_call_target="tpu_custom_call" | custom-call | tf_op jit(solution)/shard_map/pallas_call | solution.py:616
  2.0 0.7 %collective-permute-start.1 = (f32[536,128]{1,0:T(8,128)S(1)}, f32[536,128]{1,0:T(8,128)S(1)}, u32[]{:S(2)}, u32[]{:S(2)}) collective-permute-start(f32[536,128]{1,0:T(8,128)S(1)} %get-tuple-element.41), channel_id=1, source_target_pairs={{2,4},{4,2},{6,8},{8,6},{10,12},{12,10},{14,16},{16,14},{18,20},{2... | collective-permute-start | bytes 823304 | tf_op jit(solution)/shard_map/ppermute | solution.py:636
  2.7 4.4 %collective-permute-start.2 = (f32[536,128]{1,0:T(8,128)S(1)}, f32[536,128]{1,0:T(8,128)S(1)}, u32[]{:S(2)}, u32[]{:S(2)}) collective-permute-start(f32[536,128]{1,0:T(8,128)S(1)} %get-tuple-element.42), channel_id=1, source_target_pairs={{0,2},{2,0},{4,6},{6,4},{8,10},{10,8},{12,14},{14,12},{16,18},{18,... | collective-permute-start | bytes 823304 | tf_op jit(solution)/shard_map/ppermute | solution.py:637
  7.1 1.2 %shard_map.78 = (f32[1040,128]{1,0:T(8,128)S(1)}, f32[1040,128]{1,0:T(8,128)S(1)}, f32[64,128]{1,0:T(8,128)S(1)}, f32[2048,128]{1,0:T(8,128)S(1)}) custom-call(f32[2048,128]{1,0:T(8,128)S(1)} %get-tuple-element.28.state_ref, f32[2048,128]{1,0:T(8,128)} %bitcast.11), custom_call_target="tpu_custom_call" | custom-call | tf_op jit(solution)/shard_map/pallas_call | solution.py:616
  8.4 1.6 %collective-permute-start = (f32[64,128]{1,0:T(8,128)S(1)}, f32[64,128]{1,0:T(8,128)S(1)}, u32[]{:S(2)}, u32[]{:S(2)}) collective-permute-start(f32[64,128]{1,0:T(8,128)S(1)} %get-tuple-element.34), channel_id=1, source_target_pairs={{0,1},{1,0},{2,3},{3,2},{4,5},{5,4},{6,7},{7,6},{8,9},{9,8},{10,11... | collective-permute-start | bytes 98312 | tf_op jit(solution)/shard_map/ppermute | solution.py:643
  10.0 0.1 broadcast_in_dim.26
  10.2 0.2 shard_map.79
  10.3 1.9 %shard_map.80 = (f32[2048,128]{1,0:T(8,128)S(1)}, f32[16,128]{1,0:T(8,128)S(1)}) custom-call(f32[1040,128]{1,0:T(8,128)S(1)} %get-tuple-element.29.middle_ref, f32[1040,128]{1,0:T(8,128)S(1)} %get-tuple-element.30.outer_ref, f32[2048,128]{1,0:T(8,128)S(1)} %get-tuple-element.31.source_ref, f32[240,128]{1,0:T(8,128)S(1)} %get-tuple-element.32.coef_ref), custom_call_target="tpu_custom_call" | custom-call | tf_op jit(solution)/shard_map/pallas_call | solution.py:616
  12.2 0.2 collective-permute-done.side_ref
  12.4 0.9 %shard_map.81 = (f32[1040,128]{1,0:T(8,128)S(1)}, f32[1040,128]{1,0:T(8,128)S(1)}, f32[80,128]{1,0:T(8,128)S(1)}, f32[64,128]{1,0:T(8,128)}) custom-call(f32[2048,128]{1,0:T(8,128)S(1)} %get-tuple-element.33.inner_ref, f32[64,128]{1,0:T(8,128)S(1)} %collective-permute-done.side_ref, f32[8,128]{1,0:T(8,128)S(1)} %get-tuple-element.35.mask_ref, ...), custom_call_target="tpu_custom_call" | custom-call | tf_op jit(solution)/shard_map/pallas_call | solution.py:616
  13.3 0.3 shard_map.82
  13.6 0.7 %collective-permute-start.4 = (f32[536,128]{1,0:T(8,128)S(1)}, f32[536,128]{1,0:T(8,128)S(1)}, u32[]{:S(2)}, u32[]{:S(2)}) collective-permute-start(f32[536,128]{1,0:T(8,128)S(1)} %get-tuple-element.48), channel_id=1, source_target_pairs={{2,4},{4,2},{6,8},{8,6},{10,12},{12,10},{14,16},{16,14},{18,20},{2... | collective-permute-start | bytes 823304 | tf_op jit(solution)/shard_map/ppermute | solution.py:636
  14.3 3.9 %collective-permute-start.5 = (f32[536,128]{1,0:T(8,128)S(1)}, f32[536,128]{1,0:T(8,128)S(1)}, u32[]{:S(2)}, u32[]{:S(2)}) collective-permute-start(f32[536,128]{1,0:T(8,128)S(1)} %get-tuple-element.49), channel_id=1, source_target_pairs={{0,2},{2,0},{4,6},{6,4},{8,10},{10,8},{12,14},{14,12},{16,18},{18,... | collective-permute-start | bytes 823304 | tf_op jit(solution)/shard_map/ppermute | solution.py:637
  18.2 0.6 %shard_map.84 = f32[64,128]{1,0:T(8,128)S(1)} custom-call(f32[1040,128]{1,0:T(8,128)S(1)} %get-tuple-element.37.middle_ref, f32[1040,128]{1,0:T(8,128)S(1)} %get-tuple-element.43.outer_ref), custom_call_target="tpu_custom_call" | custom-call | tf_op jit(solution)/shard_map/pallas_call | solution.py:616
  18.7 1.6 %collective-permute-start.3 = (f32[64,128]{1,0:T(8,128)S(1)}, f32[64,128]{1,0:T(8,128)S(1)}, u32[]{:S(2)}, u32[]{:S(2)}) collective-permute-start(f32[64,128]{1,0:T(8,128)S(1)} %shard_map.84), channel_id=1, source_target_pairs={{0,1},{1,0},{2,3},{3,2},{4,5},{5,4},{6,7},{7,6},{8,9},{9,8},{10,11... | collective-permute-start | bytes 98312 | tf_op jit(solution)/shard_map/ppermute | solution.py:643
  20.3 1.8 %shard_map.83.inner_ref = f32[2048,128]{1,0:T(8,128)S(1)} custom-call(f32[1040,128]{1,0:T(8,128)S(1)} %get-tuple-element.37.middle_ref, f32[1040,128]{1,0:T(8,128)S(1)} %get-tuple-element.43.outer_ref, f32[2048,128]{1,0:T(8,128)S(1)} %get-tuple-element.31.source_ref, f32[240,128]{1,0:T(8,128)S(1)} %get-tuple-element.32.coef_ref), custom_call_target="tpu_custom_call" | custom-call | tf_op jit(solution)/shard_map/pallas_call | solution.py:616
  22.1 0.6 %collective-permute-done.3.side_ref = f32[64,128]{1,0:T(8,128)S(1)} collective-permute-done((f32[64,128]{1,0:T(8,128)S(1)}, f32[64,128]{1,0:T(8,128)S(1)}, u32[]{:S(2)}, u32[]{:S(2)}) %collective-permute-start.3) | collective-permute-done | bytes 32800 | tf_op jit(solution)/shard_map/ppermute | solution.py:643
  22.7 0.5 %shard_map.85 = (f32[1040,128]{1,0:T(8,128)S(1)}, f32[1040,128]{1,0:T(8,128)S(1)}, f32[32,128]{1,0:T(8,128)S(1)}, f32[64,128]{1,0:T(8,128)S(1)}) custom-call(f32[2048,128]{1,0:T(8,128)S(1)} %shard_map.83.inner_ref, f32[64,128]{1,0:T(8,128)S(1)} %collective-permute-done.3.side_ref, f32[8,128]{1,0:T(8,128)S(1)} %get-tuple-element.35.mask_ref, ...), custom_call_target="tpu_custom_call" | custom-call | tf_op jit(solution)/shard_map/pallas_call | solution.py:616
  23.3 1.2 %shard_map.86 = (f32[1040,128]{1,0:T(8,128)S(1)}, f32[8,128]{1,0:T(8,128)S(1)}, f32[32,1,128]{2,1,0:T(1,128)}) custom-call(s32[32,128]{1,0:T(8,128)S(1)} %select_select_fusion.place_ref, f32[1040,128]{1,0:T(8,128)S(1)} %get-tuple-element.44.loose_ref, f32[32,128]{1,0:T(8,128)S(1)} %get-tuple-element.46.middle_sums_ref, ...), custom_call_target="tpu_custom_call" | custom-call | tf_op jit(solution)/shard_map/pallas_call | solution.py:616
  24.5 6.3 %all-to-all-start = ((f32[32,1,128]{2,1,0:T(1,128)}), f32[32,1,128]{2,1,0:T(1,128)S(1)}, u32[]{:S(2)}, u32[]{:S(2)}) async-start(f32[32,1,128]{2,1,0:T(1,128)} %get-tuple-element.53), calls=%async_computation | async-start | bytes 32768 | tf_op jit(solution)/shard_map/all_to_all | solution.py:747
  30.8 1.1 %shard_map.87 = f32[2048,128]{1,0:T(8,128)} custom-call(s32[32,128]{1,0:T(8,128)S(1)} %select_select_fusion.place_ref, f32[1040,128]{1,0:T(8,128)S(1)} %get-tuple-element.44.loose_ref, f32[1040,128]{1,0:T(8,128)S(1)} %get-tuple-element.45.middle_ref, f32[1040,128]{1,0:T(8,128)S(1)} %get-tuple-element.51.early_ref, ...), custom_call_target="tpu_custom_call" | custom-call | tf_op jit(solution)/shard_map/pallas_call | solution.py:616
  31.9 6.1 %all-to-all-done = f32[32,1,128]{2,1,0:T(1,128)S(1)} async-done(((f32[32,1,128]{2,1,0:T(1,128)}), f32[32,1,128]{2,1,0:T(1,128)S(1)}, u32[]{:S(2)}, u32[]{:S(2)}) %all-to-all-start) | async-done | bytes 16416 | tf_op jit(solution)/shard_map/all_to_all | solution.py:747
  38.0 0.8 %shard_map.88 = f32[8,128]{1,0:T(8,128)} custom-call(s32[32,128]{1,0:T(8,128)S(1)} %select_select_fusion.place_ref, f32[8,128]{1,0:T(8,128)S(1)} %get-tuple-element.52.grad_ref, f32[32,128]{1,0:T(8,128)S(1)} %bitcast.6), custom_call_target="tpu_custom_call" | custom-call | tf_op jit(solution)/shard_map/pallas_call | solution.py:616
  (16 shorter events, 0.2 us)
Async XLA Ops:
  2.0 11.3 %collective-permute-start.1 = (f32[536,128]{1,0:T(8,128)S(1)}, f32[536,128]{1,0:T(8,128)S(1)}, u32[]{:S(2)}, u32[]{:S(2)}) collective-permute-start(f32[536,128]{1,0:T(8,128)S(1)} %get-tuple-element.41), channel_id=1, source_target_pairs={{2,4},{4,2},{6,8},{8,6},{10,12},{12,10},{14,16},{16,14},{18,20},{2... | collective-permute-start | bytes 823304 | tf_op jit(solution)/shard_map/ppermute | solution.py:636
  2.7 10.6 %collective-permute-start.2 = (f32[536,128]{1,0:T(8,128)S(1)}, f32[536,128]{1,0:T(8,128)S(1)}, u32[]{:S(2)}, u32[]{:S(2)}) collective-permute-start(f32[536,128]{1,0:T(8,128)S(1)} %get-tuple-element.42), channel_id=1, source_target_pairs={{0,2},{2,0},{4,6},{6,4},{8,10},{10,8},{12,14},{14,12},{16,18},{18,... | collective-permute-start | bytes 823304 | tf_op jit(solution)/shard_map/ppermute | solution.py:637
  7.1 3.1 %copy-start.2 = (f32[8,128]{1,0:T(8,128)S(1)}, f32[8,128]{1,0:T(8,128)}, u32[]{:S(2)}) copy-start(f32[8,128]{1,0:T(8,128)} %film_ref.1) | copy-start | bytes 12292
  8.3 1.6 %copy-start.3 = (s32[2]{0:T(128)S(1)}, s32[2]{0:T(128)}, u32[]{:S(2)}) copy-start(s32[2]{0:T(128)} %param.11) | copy-start | bytes 28
  8.4 1.8 %copy-start = (f32[2,8,128]{2,1,0:T(8,128)S(1)}, f32[2,8,128]{2,1,0:T(8,128)}, u32[]{:S(2)}) copy-start(f32[2,8,128]{2,1,0:T(8,128)} %param.8) | copy-start | bytes 24580
  8.4 1.8 %copy-start.1 = (s32[2,8,128]{2,1,0:T(8,128)S(1)}, s32[2,8,128]{2,1,0:T(8,128)}, u32[]{:S(2)}) copy-start(s32[2,8,128]{2,1,0:T(8,128)} %param.10) | copy-start | bytes 24580
  8.4 4.0 %collective-permute-start = (f32[64,128]{1,0:T(8,128)S(1)}, f32[64,128]{1,0:T(8,128)S(1)}, u32[]{:S(2)}, u32[]{:S(2)}) collective-permute-start(f32[64,128]{1,0:T(8,128)S(1)} %get-tuple-element.34), channel_id=1, source_target_pairs={{0,1},{1,0},{2,3},{3,2},{4,5},{5,4},{6,7},{7,6},{8,9},{9,8},{10,11... | collective-permute-start | bytes 98312 | tf_op jit(solution)/shard_map/ppermute | solution.py:643
  13.6 9.7 %collective-permute-start.4 = (f32[536,128]{1,0:T(8,128)S(1)}, f32[536,128]{1,0:T(8,128)S(1)}, u32[]{:S(2)}, u32[]{:S(2)}) collective-permute-start(f32[536,128]{1,0:T(8,128)S(1)} %get-tuple-element.48), channel_id=1, source_target_pairs={{2,4},{4,2},{6,8},{8,6},{10,12},{12,10},{14,16},{16,14},{18,20},{2... | collective-permute-start | bytes 823304 | tf_op jit(solution)/shard_map/ppermute | solution.py:636
  14.3 9.0 %collective-permute-start.5 = (f32[536,128]{1,0:T(8,128)S(1)}, f32[536,128]{1,0:T(8,128)S(1)}, u32[]{:S(2)}, u32[]{:S(2)}) collective-permute-start(f32[536,128]{1,0:T(8,128)S(1)} %get-tuple-element.49), channel_id=1, source_target_pairs={{0,2},{2,0},{4,6},{6,4},{8,10},{10,8},{12,14},{14,12},{16,18},{18,... | collective-permute-start | bytes 823304 | tf_op jit(solution)/shard_map/ppermute | solution.py:637
  18.7 4.0 %collective-permute-start.3 = (f32[64,128]{1,0:T(8,128)S(1)}, f32[64,128]{1,0:T(8,128)S(1)}, u32[]{:S(2)}, u32[]{:S(2)}) collective-permute-start(f32[64,128]{1,0:T(8,128)S(1)} %shard_map.84), channel_id=1, source_target_pairs={{0,1},{1,0},{2,3},{3,2},{4,5},{5,4},{6,7},{7,6},{8,9},{9,8},{10,11... | collective-permute-start | bytes 98312 | tf_op jit(solution)/shard_map/ppermute | solution.py:643
  24.5 13.5 %all-to-all-start = ((f32[32,1,128]{2,1,0:T(1,128)}), f32[32,1,128]{2,1,0:T(1,128)S(1)}, u32[]{:S(2)}, u32[]{:S(2)}) async-start(f32[32,1,128]{2,1,0:T(1,128)} %get-tuple-element.53), calls=%async_computation | async-start | bytes 32768 | tf_op jit(solution)/shard_map/all_to_all | solution.py:747

commit v7 on v6

--- a/solution.py
+++ b/solution.py
@@ -51,11 +51,11 @@
     return pl.ds(start, 8, stride=8)
 
 
-def coefficient_kernel(depth, cases, level_ref, place_ref, pressure_ref, film_ref, cavity_ref, coef_ref, packed_ref, mask_ref):
+def coefficients(depth, cases, place_ref, level_ref, pressure_ref, film_ref, cavity_ref, coef_ref, packed_ref, mask_ref):
     lane, row = lanes_of((8, 128)), rows_of((8, 128))
     film = film_ref[...]
     for case in range(cases):
-        theta = THETA_STEP * level_ref[rows(case * 8), :].astype(jnp.float32)
+        theta = THETA_STEP * jnp.broadcast_to(level_ref[:, case : case + 1], (8, 128)).astype(jnp.float32)
         viscosity = jnp.exp(VISCOSITY_PRESS * pressure_ref[rows(case * 8), :] - VISCOSITY_TEMP * theta)
         film_coef = 4.0 * viscosity / (film * film)
         density = 1.0 - 0.6 * cavity_ref[rows(case * 8), :].astype(jnp.float32)
@@ -145,11 +145,13 @@
             post.put_tiles(planes, first, {row: copy_ref[strided(first * 8 + row), :] for row in (0, 1, 6, 7)})
 
 
-def pack_kernel(depth, cases, state_ref, source_ref, middle_ref, outer_ref, cols_ref, copy_ref, sem):
+def pack_kernel(depth, cases, state_ref, place_ref, *rest):
+    (middle_ref, outer_ref, cols_ref), outs, held, sems = rest[4:7], rest[7:10], rest[10:14], rest[14]
+    copies = [pltpu.make_async_copy(rest[i], held[i], sems.at[i]) for i in range(4)]
+    for copy in copies:
+        copy.start()
     planes = 4 * cases * depth
     lane = lanes_of((8, 128))
-    copy = pltpu.make_async_copy(source_ref, copy_ref, sem)
-    copy.start()
 
     def one(pair, _):
         held = jnp.zeros((8, 128), jnp.float32)
@@ -166,7 +168,9 @@
         return 0
 
     lax.fori_loop(0, 4 * cases, one, 0)
-    copy.wait()
+    for copy in copies:
+        copy.wait()
+    coefficients(depth, cases, place_ref, *held, *outs)
 
 
 def columns_kernel(depth, cases, middle_ref, outer_ref, cols_ref):
@@ -609,10 +613,10 @@
     return pltpu.with_memory_space_constraint(array, pltpu.HBM)
 
 
-def call(kernel, *args, outs, scratch=(), hbm=None, out=VM):
+def call(kernel, *args, outs, scratch=(), hbm=(), out=VM):
     specs = [VM] * len(args)
-    if hbm is not None:
-        specs[hbm] = HB
+    for i in hbm:
+        specs[i] = HB
     return pl.pallas_call(
         kernel,
         out_shape=outs,
@@ -653,34 +657,26 @@
     forcing = source.reshape(planes * 8, 128)
     roll, trans, trans_size = lax.axis_index("roll"), lax.axis_index("trans"), lax.axis_size("trans")
     place = over_tiles([trans, trans_size, roll % 2, roll * trans_size + trans])
-    level = jnp.broadcast_to(temp_index[:, None, None], (cases, 8, 128)).reshape(cases * 8, 128)
     devices = lax.axis_size("roll") * trans_size
     inner, part = f32(planes * 8, 128), f32(planes * 4 + 2 * PAD, 128)
-    message, cols_shape = f32(planes * 2 + TAIL, 128), f32(components * cases * 8, 128)
-    coef, packed, mask = call(
-        functools.partial(coefficient_kernel, depth, cases),
-        level,
-        place,
-        pressure.reshape(cases * 8, 128),
-        film,
-        cavity.reshape(cases * 8, 128),
-        outs=(f32(cases * N_COEF * 8, 128), f32(cases * N_PACKED * 8, 128), f32(8, 128)),
-    )
+    message, tailed, cols_shape = f32(planes * 2, 128), f32(planes * 2 + TAIL, 128), f32(components * cases * 8, 128)
     state, first, second = call(
         functools.partial(send_kernel, depth, cases),
         place,
         in_hbm(state),
         outs=(inner, message, message),
         scratch=[pltpu.SemaphoreType.DMA((PIECES,))],
-        hbm=1,
+        hbm=(1,),
     )
-    middle, outer, cols, forcing = call(
+    primal = (temp_index.reshape(1, cases), pressure.reshape(cases * 8, 128), film, cavity.reshape(cases * 8, 128))
+    middle, outer, cols, coef, packed, mask = call(
         functools.partial(pack_kernel, depth, cases),
         state,
-        in_hbm(forcing),
-        outs=(part, part, cols_shape, inner),
-        scratch=[pltpu.SemaphoreType.DMA],
-        hbm=1,
+        place,
+        *map(in_hbm, primal),
+        outs=(part, part, cols_shape, f32(cases * N_COEF * 8, 128), f32(cases * N_PACKED * 8, 128), f32(8, 128)),
+        scratch=[pltpu.VMEM(array.shape, array.dtype) for array in primal] + [pltpu.SemaphoreType.DMA((4,))],
+        hbm=range(2, 6),
     )
     for index in range(SECTIONS):
         more = index < SECTIONS - 1
@@ -695,13 +691,14 @@
             outs=(inner, f32(cases * 8, 128)) if more else (inner,),
             scratch=[(planes * 8, 256)],
         )
-        middle, loose, sums, corr = call(
+        middle, loose, sums, *corr = call(
             functools.partial(sides_kernel, depth, cases, next_moments if more else wall_sums),
             whole,
             side,
             mask,
             packed,
-            outs=(part, part, f32(cases * (5 if more else 2) * 8, 128), cols_shape),
+            outs=(part, part, f32(cases * (5 if more else 2) * 8, 128)) + (() if more else (cols_shape,)),
+            scratch=[cols_shape.shape] if more else [],
         )
         if more:
             outer, second, first, moments = call(
@@ -713,7 +710,7 @@
                 second,
                 first,
                 coef,
-                outs=(part, message, message, f32(cases * 3 * 8, 128)),
+                outs=(part, tailed, tailed, f32(cases * 3 * 8, 128)),
                 scratch=[(cases * 5 * 8, 128)],
             )
             (cols,) = call(functools.partial(columns_kernel, depth, cases), middle, outer, outs=(cols_shape,))
@@ -723,7 +720,7 @@
                 place,
                 loose,
                 sums,
-                corr,
+                *corr,
                 second,
                 first,
                 coef,

time: 39 us -> 38.7 us (level)
  waiting for transfers between devices: 6.89 us -> 7.3 us
  Pallas kernels: 11.7 us -> 11.3 us
    pallas_call x12 -> x11, Pallas kernels: 11.7 us -> 11.3 us  [call(): pl.pallas_call(kernel, out_shape=outs, in_specs=specs, out_specs=tuple([o...]
    ppermute x2, waiting for transfers between devices: 0.77 us -> 1.18 us  [exchange_columns(): return lax.ppermute(cols, 'trans', ahead + back)]
  transfers between devices with their start and end apart: 7 -> 7, of which waited for: 3 -> 3; matrix products, arithmetic and copies ran while one was open for 1% -> 0% of each run, Pallas kernels for 21% -> 20%
where the time goes in v7:
time: 38.7 us; the launch traced here: 38.5 us
  starting transfers between devices  19 us (49%)
  Pallas kernels  11.3 us (29%)
  waiting for transfers between devices  7.3 us (19%)
  between operations  0.79 us (2%)
    pallas_call x11, Pallas kernels, call(): pl.pallas_call(kernel, out_shape=outs, in_specs=specs, out_specs=tuple([o...  11.3 us
    ppermute x2, starting transfers between devices, exchange_rows(): return (lax.ppermute(first, 'roll', inner), second)  8.35 us
    all_to_all x1, starting transfers between devices, on_device(): lax.all_to_all(sums, ('roll', 'trans'), 0, 0, tiled=True)  6.18 us
    all_to_all x1, waiting for transfers between devices, on_device(): lax.all_to_all(sums, ('roll', 'trans'), 0, 0, tiled=True)  6.1 us
    ppermute x2, starting transfers between devices, exchange_columns(): return lax.ppermute(cols, 'trans', ahead + back)  3.11 us
    ppermute x2, starting transfers between devices, exchange_rows(): second = lax.ppermute(second, 'roll', outer)  1.35 us
    ppermute x2, waiting for transfers between devices, exchange_columns(): return lax.ppermute(cols, 'trans', ahead + back)  1.18 us
  transfers between devices with their start and end apart: 7, of which 3 were waited for; matrix products, arithmetic and copies ran while one was open for 0% of the time, Pallas kernels for 20%

profile of v7, /device:TPU:0, one launch (start us, length us, event | category | flops | bytes accessed | tf_op | source)
XLA Modules:
  0.0 38.5 jit_solution(16219931456629004205)
XLA Ops:
  0.7 0.1 select_select_fusion.place_ref
  0.8 0.0 copy-start
  0.8 1.3 %shard_map.77 = (f32[2048,128]{1,0:T(8,128)S(1)}, f32[512,128]{1,0:T(8,128)S(1)}, f32[512,128]{1,0:T(8,128)S(1)}) custom-call(s32[32,128]{1,0:T(8,128)S(1)} %select_select_fusion.place_ref, f32[2048,128]{1,0:T(8,128)} %bitcast.11), custom_call_target="tpu_custom_call" | custom-call | tf_op jit(solution)/shard_map/pallas_call | solution.py:620
  2.1 0.7 %collective-permute-start.1 = (f32[512,128]{1,0:T(8,128)S(1)}, f32[512,128]{1,0:T(8,128)S(1)}, u32[]{:S(2)}, u32[]{:S(2)}) collective-permute-start(f32[512,128]{1,0:T(8,128)S(1)} %get-tuple-element.39), channel_id=1, source_target_pairs={{2,4},{4,2},{6,8},{8,6},{10,12},{12,10},{14,16},{16,14},{18,20},{2... | collective-permute-start | bytes 786440 | tf_op jit(solution)/shard_map/ppermute | solution.py:640
  2.8 4.4 %collective-permute-start.2 = (f32[512,128]{1,0:T(8,128)S(1)}, f32[512,128]{1,0:T(8,128)S(1)}, u32[]{:S(2)}, u32[]{:S(2)}) collective-permute-start(f32[512,128]{1,0:T(8,128)S(1)} %get-tuple-element.40), channel_id=1, source_target_pairs={{0,2},{2,0},{4,6},{6,4},{8,10},{10,8},{12,14},{14,12},{16,18},{18,... | collective-permute-start | bytes 786440 | tf_op jit(solution)/shard_map/ppermute | solution.py:641
  7.2 1.3 %shard_map.78 = (f32[1040,128]{1,0:T(8,128)S(1)}, f32[1040,128]{1,0:T(8,128)S(1)}, f32[64,128]{1,0:T(8,128)S(1)}, f32[240,128]{1,0:T(8,128)S(1)}, f32[64,128]{1,0:T(8,128)S(1)}, /*index=5*/f32[8,128]{1,0:T(8,128)S(1)}) custom-call(f32[2048,128]{1,0:T(8,128)S(1)} %get-tuple-element.27.state_ref, s32[32,128]{1,0:T(8,128)S(1)} %select_select_fusion.place_ref, ...), custom_call_target="tpu_custom_call" | custom-call | tf_op jit(solution)/shard_map/pallas_call | solution.py:620
  8.5 1.6 %collective-permute-start = (f32[64,128]{1,0:T(8,128)S(1)}, f32[64,128]{1,0:T(8,128)S(1)}, u32[]{:S(2)}, u32[]{:S(2)}) collective-permute-start(f32[64,128]{1,0:T(8,128)S(1)} %get-tuple-element.32), channel_id=1, source_target_pairs={{0,1},{1,0},{2,3},{3,2},{4,5},{5,4},{6,7},{7,6},{8,9},{9,8},{10,11... | collective-permute-start | bytes 98312 | tf_op jit(solution)/shard_map/ppermute | solution.py:647
  10.0 1.9 %shard_map.79 = (f32[2048,128]{1,0:T(8,128)S(1)}, f32[16,128]{1,0:T(8,128)S(1)}) custom-call(f32[1040,128]{1,0:T(8,128)S(1)} %get-tuple-element.28.middle_ref, f32[1040,128]{1,0:T(8,128)S(1)} %get-tuple-element.29.outer_ref, f32[2048,128]{1,0:T(8,128)S(1)} %bitcast.7, f32[240,128]{1,0:T(8,128)S(1)} %get-tuple-element.30.coef_ref), custom_call_target="tpu_custom_call" | custom-call | tf_op jit(solution)/shard_map/pallas_call | solution.py:620
  11.9 0.6 %collective-permute-done.side_ref = f32[64,128]{1,0:T(8,128)S(1)} collective-permute-done((f32[64,128]{1,0:T(8,128)S(1)}, f32[64,128]{1,0:T(8,128)S(1)}, u32[]{:S(2)}, u32[]{:S(2)}) %collective-permute-start) | collective-permute-done | bytes 32800 | tf_op jit(solution)/shard_map/ppermute | solution.py:647
  12.4 0.6 %shard_map.80 = (f32[1040,128]{1,0:T(8,128)S(1)}, f32[1040,128]{1,0:T(8,128)S(1)}, f32[80,128]{1,0:T(8,128)S(1)}) custom-call(f32[2048,128]{1,0:T(8,128)S(1)} %get-tuple-element.31.inner_ref, f32[64,128]{1,0:T(8,128)S(1)} %collective-permute-done.side_ref, f32[8,128]{1,0:T(8,128)S(1)} %get-tuple-element.33.mask_ref, f32[64,128]{1,0:T(8,128)S(1)} %get-tuple-element.34.packed_ref), custom_call_target="tpu_custom_call" | custom-call | tf_op jit(solution)/shard_map/pallas_call | solution.py:620
  13.0 0.0 collective-permute-done.1.second_in_ref
  13.0 0.3 shard_map.81
  13.3 0.7 %collective-permute-start.4 = (f32[536,128]{1,0:T(8,128)S(1)}, f32[536,128]{1,0:T(8,128)S(1)}, u32[]{:S(2)}, u32[]{:S(2)}) collective-permute-start(f32[536,128]{1,0:T(8,128)S(1)} %get-tuple-element.46), channel_id=1, source_target_pairs={{2,4},{4,2},{6,8},{8,6},{10,12},{12,10},{14,16},{16,14},{18,20},{2... | collective-permute-start | bytes 823304 | tf_op jit(solution)/shard_map/ppermute | solution.py:640
  14.0 4.0 %collective-permute-start.5 = (f32[536,128]{1,0:T(8,128)S(1)}, f32[536,128]{1,0:T(8,128)S(1)}, u32[]{:S(2)}, u32[]{:S(2)}) collective-permute-start(f32[536,128]{1,0:T(8,128)S(1)} %get-tuple-element.47), channel_id=1, source_target_pairs={{0,2},{2,0},{4,6},{6,4},{8,10},{10,8},{12,14},{14,12},{16,18},{18,... | collective-permute-start | bytes 823304 | tf_op jit(solution)/shard_map/ppermute | solution.py:641
  18.0 0.6 %shard_map.83 = f32[64,128]{1,0:T(8,128)S(1)} custom-call(f32[1040,128]{1,0:T(8,128)S(1)} %get-tuple-element.35.middle_ref, f32[1040,128]{1,0:T(8,128)S(1)} %get-tuple-element.41.outer_ref), custom_call_target="tpu_custom_call" | custom-call | tf_op jit(solution)/shard_map/pallas_call | solution.py:620
  18.6 1.6 %collective-permute-start.3 = (f32[64,128]{1,0:T(8,128)S(1)}, f32[64,128]{1,0:T(8,128)S(1)}, u32[]{:S(2)}, u32[]{:S(2)}) collective-permute-start(f32[64,128]{1,0:T(8,128)S(1)} %shard_map.83), channel_id=1, source_target_pairs={{0,1},{1,0},{2,3},{3,2},{4,5},{5,4},{6,7},{7,6},{8,9},{9,8},{10,11... | collective-permute-start | bytes 98312 | tf_op jit(solution)/shard_map/ppermute | solution.py:647
  20.1 1.8 %shard_map.82.inner_ref = f32[2048,128]{1,0:T(8,128)S(1)} custom-call(f32[1040,128]{1,0:T(8,128)S(1)} %get-tuple-element.35.middle_ref, f32[1040,128]{1,0:T(8,128)S(1)} %get-tuple-element.41.outer_ref, f32[2048,128]{1,0:T(8,128)S(1)} %bitcast.8, f32[240,128]{1,0:T(8,128)S(1)} %get-tuple-element.30.coef_ref), custom_call_target="tpu_custom_call" | custom-call | tf_op jit(solution)/shard_map/pallas_call | solution.py:620
  21.9 0.6 %collective-permute-done.3.side_ref = f32[64,128]{1,0:T(8,128)S(1)} collective-permute-done((f32[64,128]{1,0:T(8,128)S(1)}, f32[64,128]{1,0:T(8,128)S(1)}, u32[]{:S(2)}, u32[]{:S(2)}) %collective-permute-start.3) | collective-permute-done | bytes 32800 | tf_op jit(solution)/shard_map/ppermute | solution.py:647
  22.6 0.5 %shard_map.84 = (f32[1040,128]{1,0:T(8,128)S(1)}, f32[1040,128]{1,0:T(8,128)S(1)}, f32[32,128]{1,0:T(8,128)S(1)}, f32[64,128]{1,0:T(8,128)S(1)}) custom-call(f32[2048,128]{1,0:T(8,128)S(1)} %shard_map.82.inner_ref, f32[64,128]{1,0:T(8,128)S(1)} %collective-permute-done.3.side_ref, f32[8,128]{1,0:T(8,128)S(1)} %get-tuple-element.33.mask_ref, ...), custom_call_target="tpu_custom_call" | custom-call | tf_op jit(solution)/shard_map/pallas_call | solution.py:620
  23.1 1.2 %shard_map.85 = (f32[1040,128]{1,0:T(8,128)S(1)}, f32[8,128]{1,0:T(8,128)S(1)}, f32[32,1,128]{2,1,0:T(1,128)}) custom-call(s32[32,128]{1,0:T(8,128)S(1)} %select_select_fusion.place_ref, f32[1040,128]{1,0:T(8,128)S(1)} %get-tuple-element.42.loose_ref, f32[32,128]{1,0:T(8,128)S(1)} %get-tuple-element.44.middle_sums_ref, ...), custom_call_target="tpu_custom_call" | custom-call | tf_op jit(solution)/shard_map/pallas_call | solution.py:620
  24.3 6.2 %all-to-all-start = ((f32[32,1,128]{2,1,0:T(1,128)}), f32[32,1,128]{2,1,0:T(1,128)S(1)}, u32[]{:S(2)}, u32[]{:S(2)}) async-start(f32[32,1,128]{2,1,0:T(1,128)} %get-tuple-element.51), calls=%async_computation | async-start | bytes 32768 | tf_op jit(solution)/shard_map/all_to_all | solution.py:744
  30.5 1.1 %shard_map.86 = f32[2048,128]{1,0:T(8,128)} custom-call(s32[32,128]{1,0:T(8,128)S(1)} %select_select_fusion.place_ref, f32[1040,128]{1,0:T(8,128)S(1)} %get-tuple-element.42.loose_ref, f32[1040,128]{1,0:T(8,128)S(1)} %get-tuple-element.43.middle_ref, f32[1040,128]{1,0:T(8,128)S(1)} %get-tuple-element.49.early_ref, ...), custom_call_target="tpu_custom_call" | custom-call | tf_op jit(solution)/shard_map/pallas_call | solution.py:620
  31.6 6.1 %all-to-all-done = f32[32,1,128]{2,1,0:T(1,128)S(1)} async-done(((f32[32,1,128]{2,1,0:T(1,128)}), f32[32,1,128]{2,1,0:T(1,128)S(1)}, u32[]{:S(2)}, u32[]{:S(2)}) %all-to-all-start) | async-done | bytes 16416 | tf_op jit(solution)/shard_map/all_to_all | solution.py:744
  37.7 0.8 %shard_map.87 = f32[8,128]{1,0:T(8,128)} custom-call(s32[32,128]{1,0:T(8,128)S(1)} %select_select_fusion.place_ref, f32[8,128]{1,0:T(8,128)S(1)} %get-tuple-element.50.grad_ref, f32[32,128]{1,0:T(8,128)S(1)} %bitcast.9), custom_call_target="tpu_custom_call" | custom-call | tf_op jit(solution)/shard_map/pallas_call | solution.py:620
  (6 shorter events, 0.0 us)
Async XLA Ops:
  0.8 9.3 %copy-start = (f32[4,2,32,8,128]{4,3,2,1,0:T(8,128)S(1)}, f32[4,2,32,8,128]{4,3,2,1,0:T(8,128)}, u32[]{:S(2)}) copy-start(f32[4,2,32,8,128]{4,3,2,1,0:T(8,128)} %param.7) | copy-start | bytes 3145732
  2.1 10.9 %collective-permute-start.1 = (f32[512,128]{1,0:T(8,128)S(1)}, f32[512,128]{1,0:T(8,128)S(1)}, u32[]{:S(2)}, u32[]{:S(2)}) collective-permute-start(f32[512,128]{1,0:T(8,128)S(1)} %get-tuple-element.39), channel_id=1, source_target_pairs={{2,4},{4,2},{6,8},{8,6},{10,12},{12,10},{14,16},{16,14},{18,20},{2... | collective-permute-start | bytes 786440 | tf_op jit(solution)/shard_map/ppermute | solution.py:640
  2.8 10.2 %collective-permute-start.2 = (f32[512,128]{1,0:T(8,128)S(1)}, f32[512,128]{1,0:T(8,128)S(1)}, u32[]{:S(2)}, u32[]{:S(2)}) collective-permute-start(f32[512,128]{1,0:T(8,128)S(1)} %get-tuple-element.40), channel_id=1, source_target_pairs={{0,2},{2,0},{4,6},{6,4},{8,10},{10,8},{12,14},{14,12},{16,18},{18,... | collective-permute-start | bytes 786440 | tf_op jit(solution)/shard_map/ppermute | solution.py:641
  8.5 4.0 %collective-permute-start = (f32[64,128]{1,0:T(8,128)S(1)}, f32[64,128]{1,0:T(8,128)S(1)}, u32[]{:S(2)}, u32[]{:S(2)}) collective-permute-start(f32[64,128]{1,0:T(8,128)S(1)} %get-tuple-element.32), channel_id=1, source_target_pairs={{0,1},{1,0},{2,3},{3,2},{4,5},{5,4},{6,7},{7,6},{8,9},{9,8},{10,11... | collective-permute-start | bytes 98312 | tf_op jit(solution)/shard_map/ppermute | solution.py:647
  13.3 9.8 %collective-permute-start.4 = (f32[536,128]{1,0:T(8,128)S(1)}, f32[536,128]{1,0:T(8,128)S(1)}, u32[]{:S(2)}, u32[]{:S(2)}) collective-permute-start(f32[536,128]{1,0:T(8,128)S(1)} %get-tuple-element.46), channel_id=1, source_target_pairs={{2,4},{4,2},{6,8},{8,6},{10,12},{12,10},{14,16},{16,14},{18,20},{2... | collective-permute-start | bytes 823304 | tf_op jit(solution)/shard_map/ppermute | solution.py:640
  14.0 9.1 %collective-permute-start.5 = (f32[536,128]{1,0:T(8,128)S(1)}, f32[536,128]{1,0:T(8,128)S(1)}, u32[]{:S(2)}, u32[]{:S(2)}) collective-permute-start(f32[536,128]{1,0:T(8,128)S(1)} %get-tuple-element.47), channel_id=1, source_target_pairs={{0,2},{2,0},{4,6},{6,4},{8,10},{10,8},{12,14},{14,12},{16,18},{18,... | collective-permute-start | bytes 823304 | tf_op jit(solution)/shard_map/ppermute | solution.py:641
  18.6 4.0 %collective-permute-start.3 = (f32[64,128]{1,0:T(8,128)S(1)}, f32[64,128]{1,0:T(8,128)S(1)}, u32[]{:S(2)}, u32[]{:S(2)}) collective-permute-start(f32[64,128]{1,0:T(8,128)S(1)} %shard_map.83), channel_id=1, source_target_pairs={{0,1},{1,0},{2,3},{3,2},{4,5},{5,4},{6,7},{7,6},{8,9},{9,8},{10,11... | collective-permute-start | bytes 98312 | tf_op jit(solution)/shard_map/ppermute | solution.py:647
  24.3 13.4 %all-to-all-start = ((f32[32,1,128]{2,1,0:T(1,128)}), f32[32,1,128]{2,1,0:T(1,128)S(1)}, u32[]{:S(2)}, u32[]{:S(2)}) async-start(f32[32,1,128]{2,1,0:T(1,128)} %get-tuple-element.51), calls=%async_computation | async-start | bytes 32768 | tf_op jit(solution)/shard_map/all_to_all | solution.py:744

commit v8 on v7

--- a/solution.py
+++ b/solution.py
@@ -145,12 +145,7 @@
             post.put_tiles(planes, first, {row: copy_ref[strided(first * 8 + row), :] for row in (0, 1, 6, 7)})
 
 
-def pack_kernel(depth, cases, state_ref, place_ref, *rest):
-    (middle_ref, outer_ref, cols_ref), outs, held, sems = rest[4:7], rest[7:10], rest[10:14], rest[14]
-    copies = [pltpu.make_async_copy(rest[i], held[i], sems.at[i]) for i in range(4)]
-    for copy in copies:
-        copy.start()
-    planes = 4 * cases * depth
+def pack_kernel(depth, cases, state_ref, cols_ref):
     lane = lanes_of((8, 128))
 
     def one(pair, _):
@@ -160,10 +155,23 @@
             plane = state_ref[rows(pl.multiple_of((pair * depth + layer) * 8, 8)), :]
             held = jnp.where(lane // 4 == group, pltpu.roll(plane, (4 * group + 2) % 128, 1), held)
         cols_ref[rows(pl.multiple_of(pair * 8, 8)), :] = held
+        return 0
+
+    lax.fori_loop(0, 4 * cases, one, 0, unroll=4)
+
+
+def tile_kernel(depth, cases, state_ref, place_ref, *rest):
+    planes = 4 * cases * depth
+    (middle_ref, outer_ref), outs, held, sems = rest[4:6], rest[6:9], rest[9:13], rest[13]
+    copies = [pltpu.make_async_copy(rest[i], held[i], sems.at[i]) for i in range(4)]
+    for copy in copies:
+        copy.start()
+
+    def one(pair, _):
         for row in range(8):
+            ref, place = row_place((middle_ref, outer_ref), row, planes)
             for block in range(depth // 8):
                 first = pl.multiple_of(pair * depth + 8 * block, 8)
-                ref, place = row_place((middle_ref, outer_ref), row, planes)
                 ref[rows(place + first), :] = state_ref[strided(first * 8 + row), :]
         return 0
 
@@ -669,12 +677,13 @@
         hbm=(1,),
     )
     primal = (temp_index.reshape(1, cases), pressure.reshape(cases * 8, 128), film, cavity.reshape(cases * 8, 128))
-    middle, outer, cols, coef, packed, mask = call(
-        functools.partial(pack_kernel, depth, cases),
+    (cols,) = call(functools.partial(pack_kernel, depth, cases), state, outs=(cols_shape,))
+    middle, outer, coef, packed, mask = call(
+        functools.partial(tile_kernel, depth, cases),
         state,
         place,
         *map(in_hbm, primal),
-        outs=(part, part, cols_shape, f32(cases * N_COEF * 8, 128), f32(cases * N_PACKED * 8, 128), f32(8, 128)),
+        outs=(part, part, f32(cases * N_COEF * 8, 128), f32(cases * N_PACKED * 8, 128), f32(8, 128)),
         scratch=[pltpu.VMEM(array.shape, array.dtype) for array in primal] + [pltpu.SemaphoreType.DMA((4,))],
         hbm=range(2, 6),
     )

time: 38.7 us -> 38.4 us (level)
  waiting for transfers between devices: 7.3 us -> 6.74 us
    ppermute x2, waiting for transfers between devices: 1.18 us -> 0.62 us  [exchange_columns(): return lax.ppermute(cols, 'trans', ahead + back)]
    ppermute x2, starting transfers between devices: 8.35 us -> 8.75 us  [exchange_rows(): return (lax.ppermute(first, 'roll', inner), second)]
    pallas_call x11 -> x12, Pallas kernels: 11.3 us -> 11.3 us  [call(): pl.pallas_call(kernel, out_shape=outs, in_specs=specs, out_specs=tuple([o...]
  transfers between devices with their start and end apart: 7 -> 7, of which waited for: 3 -> 2; matrix products, arithmetic and copies ran while one was open for 0% -> 0% of each run, Pallas kernels for 20% -> 20%
where the time goes in v8:
time: 38.4 us; the launch traced here: 38.2 us
  starting transfers between devices  19.2 us (50%)
  Pallas kernels  11.3 us (29%)
  waiting for transfers between devices  6.74 us (18%)
  between operations  0.8 us (2%)
    pallas_call x12, Pallas kernels, call(): pl.pallas_call(kernel, out_shape=outs, in_specs=specs, out_specs=tuple([o...  11.3 us
    ppermute x2, starting transfers between devices, exchange_rows(): return (lax.ppermute(first, 'roll', inner), second)  8.75 us
    all_to_all x1, waiting for transfers between devices, on_device(): lax.all_to_all(sums, ('roll', 'trans'), 0, 0, tiled=True)  6.1 us
    all_to_all x1, starting transfers between devices, on_device(): lax.all_to_all(sums, ('roll', 'trans'), 0, 0, tiled=True)  5.96 us
    ppermute x2, starting transfers between devices, exchange_columns(): return lax.ppermute(cols, 'trans', ahead + back)  3.11 us
    ppermute x2, starting transfers between devices, exchange_rows(): second = lax.ppermute(second, 'roll', outer)  1.35 us
  transfers between devices with their start and end apart: 7, of which 2 were waited for; matrix products, arithmetic and copies ran while one was open for 0% of the time, Pallas kernels for 20%

profile of v8, /device:TPU:0, one launch (start us, length us, event | category | flops | bytes accessed | tf_op | source)
XLA Modules:
  0.0 38.2 jit_solution(4493070737907584450)
XLA Ops:
  0.7 0.1 select_select_fusion.place_ref
  0.8 1.2 %shard_map.77 = (f32[2048,128]{1,0:T(8,128)S(1)}, f32[512,128]{1,0:T(8,128)S(1)}, f32[512,128]{1,0:T(8,128)S(1)}) custom-call(s32[32,128]{1,0:T(8,128)S(1)} %select_select_fusion.place_ref, f32[2048,128]{1,0:T(8,128)} %bitcast.11), custom_call_target="tpu_custom_call" | custom-call | tf_op jit(solution)/shard_map/pallas_call | solution.py:628
  2.0 0.7 %collective-permute-start.1 = (f32[512,128]{1,0:T(8,128)S(1)}, f32[512,128]{1,0:T(8,128)S(1)}, u32[]{:S(2)}, u32[]{:S(2)}) collective-permute-start(f32[512,128]{1,0:T(8,128)S(1)} %get-tuple-element.37), channel_id=1, source_target_pairs={{2,4},{4,2},{6,8},{8,6},{10,12},{12,10},{14,16},{16,14},{18,20},{2... | collective-permute-start | bytes 786440 | tf_op jit(solution)/shard_map/ppermute | solution.py:648
  2.7 4.4 %collective-permute-start.2 = (f32[512,128]{1,0:T(8,128)S(1)}, f32[512,128]{1,0:T(8,128)S(1)}, u32[]{:S(2)}, u32[]{:S(2)}) collective-permute-start(f32[512,128]{1,0:T(8,128)S(1)} %get-tuple-element.38), channel_id=1, source_target_pairs={{0,2},{2,0},{4,6},{6,4},{8,10},{10,8},{12,14},{14,12},{16,18},{18,... | collective-permute-start | bytes 786440 | tf_op jit(solution)/shard_map/ppermute | solution.py:649
  7.1 0.4 %shard_map.80 = f32[64,128]{1,0:T(8,128)S(1)} custom-call(f32[2048,128]{1,0:T(8,128)S(1)} %get-tuple-element.26.state_ref), custom_call_target="tpu_custom_call" | custom-call | tf_op jit(solution)/shard_map/pallas_call | solution.py:628
  7.5 1.6 %collective-permute-start = (f32[64,128]{1,0:T(8,128)S(1)}, f32[64,128]{1,0:T(8,128)S(1)}, u32[]{:S(2)}, u32[]{:S(2)}) collective-permute-start(f32[64,128]{1,0:T(8,128)S(1)} %shard_map.80), channel_id=1, source_target_pairs={{0,1},{1,0},{2,3},{3,2},{4,5},{5,4},{6,7},{7,6},{8,9},{9,8},{10,11... | collective-permute-start | bytes 98312 | tf_op jit(solution)/shard_map/ppermute | solution.py:655
  9.0 1.0 %shard_map.78 = (f32[1040,128]{1,0:T(8,128)S(1)}, f32[1040,128]{1,0:T(8,128)S(1)}, f32[240,128]{1,0:T(8,128)S(1)}, f32[64,128]{1,0:T(8,128)S(1)}, f32[8,128]{1,0:T(8,128)S(1)}) custom-call(f32[2048,128]{1,0:T(8,128)S(1)} %get-tuple-element.26.state_ref, s32[32,128]{1,0:T(8,128)S(1)} %select_select_fusion.place_ref, s32[1,2]{1,0:T(1,128)} %bitcast.14, ...), custom_call_target="tpu_custom_call" | custom-call | tf_op jit(solution)/shard_map/pallas_call | solution.py:628
  10.1 1.8 %shard_map.79 = (f32[2048,128]{1,0:T(8,128)S(1)}, f32[16,128]{1,0:T(8,128)S(1)}) custom-call(f32[1040,128]{1,0:T(8,128)S(1)} %get-tuple-element.27.middle_ref, f32[1040,128]{1,0:T(8,128)S(1)} %get-tuple-element.28.outer_ref, f32[2048,128]{1,0:T(8,128)S(1)} %bitcast.7, f32[240,128]{1,0:T(8,128)S(1)} %get-tuple-element.29.coef_ref), custom_call_target="tpu_custom_call" | custom-call | tf_op jit(solution)/shard_map/pallas_call | solution.py:628
  11.9 0.6 %shard_map.81 = (f32[1040,128]{1,0:T(8,128)S(1)}, f32[1040,128]{1,0:T(8,128)S(1)}, f32[80,128]{1,0:T(8,128)S(1)}) custom-call(f32[2048,128]{1,0:T(8,128)S(1)} %get-tuple-element.30.inner_ref, f32[64,128]{1,0:T(8,128)S(1)} %collective-permute-done.side_ref, f32[8,128]{1,0:T(8,128)S(1)} %get-tuple-element.31.mask_ref, f32[64,128]{1,0:T(8,128)S(1)} %get-tuple-element.32.packed_ref), custom_call_target="tpu_custom_call" | custom-call | tf_op jit(solution)/shard_map/pallas_call | solution.py:628
  12.5 0.0 collective-permute-done.1.second_in_ref
  12.5 0.0 collective-permute-done.2.first_in_ref
  12.5 0.3 shard_map.82
  12.8 0.7 %collective-permute-start.4 = (f32[536,128]{1,0:T(8,128)S(1)}, f32[536,128]{1,0:T(8,128)S(1)}, u32[]{:S(2)}, u32[]{:S(2)}) collective-permute-start(f32[536,128]{1,0:T(8,128)S(1)} %get-tuple-element.44), channel_id=1, source_target_pairs={{2,4},{4,2},{6,8},{8,6},{10,12},{12,10},{14,16},{16,14},{18,20},{2... | collective-permute-start | bytes 823304 | tf_op jit(solution)/shard_map/ppermute | solution.py:648
  13.5 4.4 %collective-permute-start.5 = (f32[536,128]{1,0:T(8,128)S(1)}, f32[536,128]{1,0:T(8,128)S(1)}, u32[]{:S(2)}, u32[]{:S(2)}) collective-permute-start(f32[536,128]{1,0:T(8,128)S(1)} %get-tuple-element.45), channel_id=1, source_target_pairs={{0,2},{2,0},{4,6},{6,4},{8,10},{10,8},{12,14},{14,12},{16,18},{18,... | collective-permute-start | bytes 823304 | tf_op jit(solution)/shard_map/ppermute | solution.py:649
  17.9 0.6 %shard_map.84 = f32[64,128]{1,0:T(8,128)S(1)} custom-call(f32[1040,128]{1,0:T(8,128)S(1)} %get-tuple-element.33.middle_ref, f32[1040,128]{1,0:T(8,128)S(1)} %get-tuple-element.39.outer_ref), custom_call_target="tpu_custom_call" | custom-call | tf_op jit(solution)/shard_map/pallas_call | solution.py:628
  18.5 1.6 %collective-permute-start.3 = (f32[64,128]{1,0:T(8,128)S(1)}, f32[64,128]{1,0:T(8,128)S(1)}, u32[]{:S(2)}, u32[]{:S(2)}) collective-permute-start(f32[64,128]{1,0:T(8,128)S(1)} %shard_map.84), channel_id=1, source_target_pairs={{0,1},{1,0},{2,3},{3,2},{4,5},{5,4},{6,7},{7,6},{8,9},{9,8},{10,11... | collective-permute-start | bytes 98312 | tf_op jit(solution)/shard_map/ppermute | solution.py:655
  20.0 1.8 %shard_map.83.inner_ref = f32[2048,128]{1,0:T(8,128)S(1)} custom-call(f32[1040,128]{1,0:T(8,128)S(1)} %get-tuple-element.33.middle_ref, f32[1040,128]{1,0:T(8,128)S(1)} %get-tuple-element.39.outer_ref, f32[2048,128]{1,0:T(8,128)S(1)} %bitcast.8, f32[240,128]{1,0:T(8,128)S(1)} %get-tuple-element.29.coef_ref), custom_call_target="tpu_custom_call" | custom-call | tf_op jit(solution)/shard_map/pallas_call | solution.py:628
  21.8 0.6 %collective-permute-done.3.side_ref = f32[64,128]{1,0:T(8,128)S(1)} collective-permute-done((f32[64,128]{1,0:T(8,128)S(1)}, f32[64,128]{1,0:T(8,128)S(1)}, u32[]{:S(2)}, u32[]{:S(2)}) %collective-permute-start.3) | collective-permute-done | bytes 32800 | tf_op jit(solution)/shard_map/ppermute | solution.py:655
  22.5 0.5 %shard_map.85 = (f32[1040,128]{1,0:T(8,128)S(1)}, f32[1040,128]{1,0:T(8,128)S(1)}, f32[32,128]{1,0:T(8,128)S(1)}, f32[64,128]{1,0:T(8,128)S(1)}) custom-call(f32[2048,128]{1,0:T(8,128)S(1)} %shard_map.83.inner_ref, f32[64,128]{1,0:T(8,128)S(1)} %collective-permute-done.3.side_ref, f32[8,128]{1,0:T(8,128)S(1)} %get-tuple-element.31.mask_ref, ...), custom_call_target="tpu_custom_call" | custom-call | tf_op jit(solution)/shard_map/pallas_call | solution.py:628
  23.0 1.2 %shard_map.86 = (f32[1040,128]{1,0:T(8,128)S(1)}, f32[8,128]{1,0:T(8,128)S(1)}, f32[32,1,128]{2,1,0:T(1,128)}) custom-call(s32[32,128]{1,0:T(8,128)S(1)} %select_select_fusion.place_ref, f32[1040,128]{1,0:T(8,128)S(1)} %get-tuple-element.40.loose_ref, f32[32,128]{1,0:T(8,128)S(1)} %get-tuple-element.42.middle_sums_ref, ...), custom_call_target="tpu_custom_call" | custom-call | tf_op jit(solution)/shard_map/pallas_call | solution.py:628
  24.2 6.0 %all-to-all-start = ((f32[32,1,128]{2,1,0:T(1,128)}), f32[32,1,128]{2,1,0:T(1,128)S(1)}, u32[]{:S(2)}, u32[]{:S(2)}) async-start(f32[32,1,128]{2,1,0:T(1,128)} %get-tuple-element.49), calls=%async_computation | async-start | bytes 32768 | tf_op jit(solution)/shard_map/all_to_all | solution.py:753
  30.2 1.1 %shard_map.87 = f32[2048,128]{1,0:T(8,128)} custom-call(s32[32,128]{1,0:T(8,128)S(1)} %select_select_fusion.place_ref, f32[1040,128]{1,0:T(8,128)S(1)} %get-tuple-element.40.loose_ref, f32[1040,128]{1,0:T(8,128)S(1)} %get-tuple-element.41.middle_ref, f32[1040,128]{1,0:T(8,128)S(1)} %get-tuple-element.47.early_ref, ...), custom_call_target="tpu_custom_call" | custom-call | tf_op jit(solution)/shard_map/pallas_call | solution.py:628
  31.3 6.1 %all-to-all-done = f32[32,1,128]{2,1,0:T(1,128)S(1)} async-done(((f32[32,1,128]{2,1,0:T(1,128)}), f32[32,1,128]{2,1,0:T(1,128)S(1)}, u32[]{:S(2)}, u32[]{:S(2)}) %all-to-all-start) | async-done | bytes 16416 | tf_op jit(solution)/shard_map/all_to_all | solution.py:753
  37.4 0.8 %shard_map.88 = f32[8,128]{1,0:T(8,128)} custom-call(s32[32,128]{1,0:T(8,128)S(1)} %select_select_fusion.place_ref, f32[8,128]{1,0:T(8,128)S(1)} %get-tuple-element.48.grad_ref, f32[32,128]{1,0:T(8,128)S(1)} %bitcast.9), custom_call_target="tpu_custom_call" | custom-call | tf_op jit(solution)/shard_map/pallas_call | solution.py:628
  (7 shorter events, 0.0 us)
Async XLA Ops:
  2.0 10.5 %collective-permute-start.1 = (f32[512,128]{1,0:T(8,128)S(1)}, f32[512,128]{1,0:T(8,128)S(1)}, u32[]{:S(2)}, u32[]{:S(2)}) collective-permute-start(f32[512,128]{1,0:T(8,128)S(1)} %get-tuple-element.37), channel_id=1, source_target_pairs={{2,4},{4,2},{6,8},{8,6},{10,12},{12,10},{14,16},{16,14},{18,20},{2... | collective-permute-start | bytes 786440 | tf_op jit(solution)/shard_map/ppermute | solution.py:648
  2.7 9.8 %collective-permute-start.2 = (f32[512,128]{1,0:T(8,128)S(1)}, f32[512,128]{1,0:T(8,128)S(1)}, u32[]{:S(2)}, u32[]{:S(2)}) collective-permute-start(f32[512,128]{1,0:T(8,128)S(1)} %get-tuple-element.38), channel_id=1, source_target_pairs={{0,2},{2,0},{4,6},{6,4},{8,10},{10,8},{12,14},{14,12},{16,18},{18,... | collective-permute-start | bytes 786440 | tf_op jit(solution)/shard_map/ppermute | solution.py:649
  7.1 3.0 %copy-start = (f32[4,2,32,8,128]{4,3,2,1,0:T(8,128)S(1)}, f32[4,2,32,8,128]{4,3,2,1,0:T(8,128)}, u32[]{:S(2)}) copy-start(f32[4,2,32,8,128]{4,3,2,1,0:T(8,128)} %param.7) | copy-start | bytes 3145732
  7.5 4.4 %collective-permute-start = (f32[64,128]{1,0:T(8,128)S(1)}, f32[64,128]{1,0:T(8,128)S(1)}, u32[]{:S(2)}, u32[]{:S(2)}) collective-permute-start(f32[64,128]{1,0:T(8,128)S(1)} %shard_map.80), channel_id=1, source_target_pairs={{0,1},{1,0},{2,3},{3,2},{4,5},{5,4},{6,7},{7,6},{8,9},{9,8},{10,11... | collective-permute-start | bytes 98312 | tf_op jit(solution)/shard_map/ppermute | solution.py:655
  12.8 10.2 %collective-permute-start.4 = (f32[536,128]{1,0:T(8,128)S(1)}, f32[536,128]{1,0:T(8,128)S(1)}, u32[]{:S(2)}, u32[]{:S(2)}) collective-permute-start(f32[536,128]{1,0:T(8,128)S(1)} %get-tuple-element.44), channel_id=1, source_target_pairs={{2,4},{4,2},{6,8},{8,6},{10,12},{12,10},{14,16},{16,14},{18,20},{2... | collective-permute-start | bytes 823304 | tf_op jit(solution)/shard_map/ppermute | solution.py:648
  13.5 9.5 %collective-permute-start.5 = (f32[536,128]{1,0:T(8,128)S(1)}, f32[536,128]{1,0:T(8,128)S(1)}, u32[]{:S(2)}, u32[]{:S(2)}) collective-permute-start(f32[536,128]{1,0:T(8,128)S(1)} %get-tuple-element.45), channel_id=1, source_target_pairs={{0,2},{2,0},{4,6},{6,4},{8,10},{10,8},{12,14},{14,12},{16,18},{18,... | collective-permute-start | bytes 823304 | tf_op jit(solution)/shard_map/ppermute | solution.py:649
  18.5 4.0 %collective-permute-start.3 = (f32[64,128]{1,0:T(8,128)S(1)}, f32[64,128]{1,0:T(8,128)S(1)}, u32[]{:S(2)}, u32[]{:S(2)}) collective-permute-start(f32[64,128]{1,0:T(8,128)S(1)} %shard_map.84), channel_id=1, source_target_pairs={{0,1},{1,0},{2,3},{3,2},{4,5},{5,4},{6,7},{7,6},{8,9},{9,8},{10,11... | collective-permute-start | bytes 98312 | tf_op jit(solution)/shard_map/ppermute | solution.py:655
  24.2 13.2 %all-to-all-start = ((f32[32,1,128]{2,1,0:T(1,128)}), f32[32,1,128]{2,1,0:T(1,128)S(1)}, u32[]{:S(2)}, u32[]{:S(2)}) async-start(f32[32,1,128]{2,1,0:T(1,128)} %get-tuple-element.49), calls=%async_computation | async-start | bytes 32768 | tf_op jit(solution)/shard_map/all_to_all | solution.py:753

commit v9 on v8

--- a/solution.py
+++ b/solution.py
@@ -532,55 +532,7 @@
     line_ref[...] = jnp.broadcast_to(line[None], line_ref.shape)
 
 
-def rest_kernel(
-    depth,
-    cases,
-    place_ref,
-    loose_ref,
-    middle_ref,
-    early_ref,
-    second_in_ref,
-    first_in_ref,
-    coef_ref,
-    out_ref,
-    state_ref,
-    sems,
-):
-    planes = 4 * cases * depth
-    half = planes * 4
-    copies = [pltpu.make_async_copy(state_ref.at[rows(i * half, half), :], out_ref.at[rows(i * half, half), :], sems.at[i]) for i in range(2)]
-
-    def place_tiles(c, refs):
-        def one(case, _):
-            for block in range(depth // 8):
-                offset = pl.multiple_of((c * cases + case) * depth + 8 * block, 8)
-                for row in range(8):
-                    if refs[row] is not None:
-                        ref, place = row_place(refs[row], row, planes)
-                        state_ref[strided(offset * 8 + row), :] = ref[rows(place + offset), :]
-            return 0
-
-        lax.fori_loop(0, cases, one, 0)
-
-    both = (middle_ref, early_ref)
-    for c in range(2):
-        place_tiles(c, [both] * 8)
-    copies[0].start()
-    for c in range(2, 4):
-        place_tiles(c, [both if row in MIDDLE else None for row in range(8)])
-
-    def store(c, case, block, offset, tiles):
-        for row, tile in tiles.items():
-            state_ref[strided(offset * 8 + row), :] = tile
-
-    arrived = Post(place_ref, first_in_ref, second_in_ref)
-    outer_rows(depth, cases, planes, (2, 3), loose_ref, arrived, coef_ref, store)
-    copies[1].start()
-    copies[0].wait()
-    copies[1].wait()
-
-
-def scale_kernel(cells, devices, trans, place_ref, grad_ref, sums_ref, out_ref, lines_ref):
+def scaled(cells, devices, trans, place_ref, grad_ref, sums_ref, lines_ref):
     pad = -(-trans // 8) * 8
     lane, row = lanes_of((8, 128)), rows_of((8, 128))
     zero = jnp.zeros((pad, 128), jnp.float32)
@@ -602,7 +554,67 @@
     edge = (lane < 2) | (lane >= 126)
     for i in (0, 1, 6, 7):
         grad += jnp.where((row == i) & edge, pltpu.roll(own, (126 - 4 * i) % 128, 1), 0.0)
-    out_ref[...] = grad / jnp.sqrt(total / cells + 1e-06)
+    return grad / jnp.sqrt(total / cells + 1e-06)
+
+
+def rest_kernel(
+    depth,
+    cases,
+    cells,
+    devices,
+    trans,
+    place_ref,
+    loose_ref,
+    middle_ref,
+    early_ref,
+    second_in_ref,
+    first_in_ref,
+    coef_ref,
+    grad_ref,
+    sums_ref,
+    out_ref,
+    wall_out_ref,
+    state_ref,
+    wall_ref,
+    lines_ref,
+    sems,
+):
+    wall_ref[...] = scaled(cells, devices, trans, place_ref, grad_ref, sums_ref, lines_ref)
+    wall_copy = pltpu.make_async_copy(wall_ref, wall_out_ref, sems.at[2])
+    wall_copy.start()
+    planes = 4 * cases * depth
+    half = planes * 4
+    copies = [pltpu.make_async_copy(state_ref.at[rows(i * half, half), :], out_ref.at[rows(i * half, half), :], sems.at[i]) for i in range(2)]
+
+    def place_tiles(c, refs):
+        def one(case, _):
+            for block in range(depth // 8):
+                offset = pl.multiple_of((c * cases + case) * depth + 8 * block, 8)
+                for row in range(8):
+                    if refs[row] is not None:
+                        ref, place = row_place(refs[row], row, planes)
+                        state_ref[strided(offset * 8 + row), :] = ref[rows(place + offset), :]
+            return 0
+
+        lax.fori_loop(0, cases, one, 0)
+
+    both = (middle_ref, early_ref)
+    for c in range(2):
+        place_tiles(c, [both] * 8)
+    copies[0].start()
+    for c in range(2, 4):
+        place_tiles(c, [both if row in MIDDLE else None for row in range(8)])
+
+    def store(c, case, block, offset, tiles):
+        for row, tile in tiles.items():
+            state_ref[strided(offset * 8 + row), :] = tile
+
+    arrived = Post(place_ref, first_in_ref, second_in_ref)
+    outer_rows(depth, cases, planes, (2, 3), loose_ref, arrived, coef_ref, store)
+    copies[1].start()
+    wall_copy.wait()
+    copies[0].wait()
+    copies[1].wait()
 
 
 def f32(*shape):
@@ -737,28 +749,22 @@
                 outs=(part, f32(8, 128), pltpu.VMEM((devices, 1, 128), jnp.float32)),
                 scratch=[(cases * 2 * 8, 128)],
             )
-            (state,) = call(
-                functools.partial(rest_kernel, depth, cases),
-                place,
-                loose,
-                middle,
-                early,
-                second,
-                first,
-                coef,
-                outs=(pltpu.HBM(inner.shape, jnp.float32),),
-                scratch=[inner.shape, pltpu.SemaphoreType.DMA((2,))],
-                out=HB,
-            )
     sums = lax.all_to_all(sums, ("roll", "trans"), 0, 0, tiled=True).reshape(devices, 128)
     pad = -(-trans_size // 8) * 8
-    (wall_step,) = call(
-        functools.partial(scale_kernel, devices * width_x * width_y, devices, trans_size),
+    state, wall_step = call(
+        functools.partial(rest_kernel, depth, cases, devices * width_x * width_y, devices, trans_size),
         place,
+        loose,
+        middle,
+        early,
+        second,
+        first,
+        coef,
         grad,
         sums,
-        outs=(f32(8, 128),),
-        scratch=[(devices + 2 * pad, 128)],
+        outs=(pltpu.HBM(inner.shape, jnp.float32), pltpu.HBM((8, 128), jnp.float32)),
+        scratch=[inner.shape, (8, 128), (devices + 2 * pad, 128), pltpu.SemaphoreType.DMA((3,))],
+        out=HB,
     )
     return (state.reshape(adjoint.shape), wall_step)
 

time: 38.4 us -> 38.1 us (level)
  blocking collectives: 0 us -> 13 us
  waiting for transfers between devices: 6.74 us -> 0.63 us
  starting transfers between devices: 19.2 us -> 13.2 us
  Pallas kernels: 11.3 us -> 10.2 us
    all_to_all x0 -> x1, blocking collectives: none -> 13 us  [on_device(): lax.all_to_all(sums, ('roll', 'trans'), 0, 0, tiled=True)]
    all_to_all x1 -> x0, waiting for transfers between devices: 6.1 us -> none  [on_device(): lax.all_to_all(sums, ('roll', 'trans'), 0, 0, tiled=True)]
    all_to_all x1 -> x0, starting transfers between devices: 5.96 us -> none  [on_device(): lax.all_to_all(sums, ('roll', 'trans'), 0, 0, tiled=True)]
    pallas_call x12 -> x11, Pallas kernels: 11.3 us -> 10.2 us  [call(): pl.pallas_call(kernel, out_shape=outs, in_specs=specs, out_specs=tuple([o...]
  transfers between devices with their start and end apart: 7 -> 6, of which waited for: 2 -> 1; matrix products, arithmetic and copies ran while one was open for 0% -> 0% of each run, Pallas kernels for 20% -> 18%
where the time goes in v9:
time: 38.1 us; the launch traced here: 37.9 us
  starting transfers between devices  13.2 us (35%)
  blocking collectives  13 us (34%)
  Pallas kernels  10.2 us (27%)
  between operations  0.79 us (2%)
  waiting for transfers between devices  0.63 us (2%)
    all_to_all x1, blocking collectives, on_device(): lax.all_to_all(sums, ('roll', 'trans'), 0, 0, tiled=True)  13 us
    pallas_call x11, Pallas kernels, call(): pl.pallas_call(kernel, out_shape=outs, in_specs=specs, out_specs=tuple([o...  10.2 us
    ppermute x2, starting transfers between devices, exchange_rows(): return (lax.ppermute(first, 'roll', inner), second)  8.75 us
    ppermute x2, starting transfers between devices, exchange_columns(): return lax.ppermute(cols, 'trans', ahead + back)  3.11 us
    ppermute x2, starting transfers between devices, exchange_rows(): second = lax.ppermute(second, 'roll', outer)  1.35 us
  transfers between devices with their start and end apart: 6, of which 1 were waited for; matrix products, arithmetic and copies ran while one was open for 0% of the time, Pallas kernels for 18%

profile of v9, /device:TPU:0, one launch (start us, length us, event | category | flops | bytes accessed | tf_op | source)
XLA Modules:
  0.0 37.9 jit_solution(7773332625132377855)
XLA Ops:
  0.7 0.1 select_select_fusion.place_ref
  0.8 1.2 %shard_map.77 = (f32[2048,128]{1,0:T(8,128)S(1)}, f32[512,128]{1,0:T(8,128)S(1)}, f32[512,128]{1,0:T(8,128)S(1)}) custom-call(s32[32,128]{1,0:T(8,128)S(1)} %select_select_fusion.place_ref, f32[2048,128]{1,0:T(8,128)} %bitcast.10), custom_call_target="tpu_custom_call" | custom-call | tf_op jit(solution)/shard_map/pallas_call | solution.py:640
  2.0 0.7 %collective-permute-start.1 = (f32[512,128]{1,0:T(8,128)S(1)}, f32[512,128]{1,0:T(8,128)S(1)}, u32[]{:S(2)}, u32[]{:S(2)}) collective-permute-start(f32[512,128]{1,0:T(8,128)S(1)} %get-tuple-element.39), channel_id=1, source_target_pairs={{2,4},{4,2},{6,8},{8,6},{10,12},{12,10},{14,16},{16,14},{18,20},{2... | collective-permute-start | bytes 786440 | tf_op jit(solution)/shard_map/ppermute | solution.py:660
  2.7 4.4 %collective-permute-start.2 = (f32[512,128]{1,0:T(8,128)S(1)}, f32[512,128]{1,0:T(8,128)S(1)}, u32[]{:S(2)}, u32[]{:S(2)}) collective-permute-start(f32[512,128]{1,0:T(8,128)S(1)} %get-tuple-element.40), channel_id=1, source_target_pairs={{0,2},{2,0},{4,6},{6,4},{8,10},{10,8},{12,14},{14,12},{16,18},{18,... | collective-permute-start | bytes 786440 | tf_op jit(solution)/shard_map/ppermute | solution.py:661
  7.1 0.4 %shard_map.80 = f32[64,128]{1,0:T(8,128)S(1)} custom-call(f32[2048,128]{1,0:T(8,128)S(1)} %get-tuple-element.28.state_ref), custom_call_target="tpu_custom_call" | custom-call | tf_op jit(solution)/shard_map/pallas_call | solution.py:640
  7.5 1.6 %collective-permute-start = (f32[64,128]{1,0:T(8,128)S(1)}, f32[64,128]{1,0:T(8,128)S(1)}, u32[]{:S(2)}, u32[]{:S(2)}) collective-permute-start(f32[64,128]{1,0:T(8,128)S(1)} %shard_map.80), channel_id=1, source_target_pairs={{0,1},{1,0},{2,3},{3,2},{4,5},{5,4},{6,7},{7,6},{8,9},{9,8},{10,11... | collective-permute-start | bytes 98312 | tf_op jit(solution)/shard_map/ppermute | solution.py:667
  9.0 1.0 %shard_map.78 = (f32[1040,128]{1,0:T(8,128)S(1)}, f32[1040,128]{1,0:T(8,128)S(1)}, f32[240,128]{1,0:T(8,128)S(1)}, f32[64,128]{1,0:T(8,128)S(1)}, f32[8,128]{1,0:T(8,128)S(1)}) custom-call(f32[2048,128]{1,0:T(8,128)S(1)} %get-tuple-element.28.state_ref, s32[32,128]{1,0:T(8,128)S(1)} %select_select_fusion.place_ref, s32[1,2]{1,0:T(1,128)} %bitcast.13, ...), custom_call_target="tpu_custom_call" | custom-call | tf_op jit(solution)/shard_map/pallas_call | solution.py:640
  10.1 1.8 %shard_map.79 = (f32[2048,128]{1,0:T(8,128)S(1)}, f32[16,128]{1,0:T(8,128)S(1)}) custom-call(f32[1040,128]{1,0:T(8,128)S(1)} %get-tuple-element.29.middle_ref, f32[1040,128]{1,0:T(8,128)S(1)} %get-tuple-element.30.outer_ref, f32[2048,128]{1,0:T(8,128)S(1)} %bitcast.7, f32[240,128]{1,0:T(8,128)S(1)} %get-tuple-element.31.coef_ref), custom_call_target="tpu_custom_call" | custom-call | tf_op jit(solution)/shard_map/pallas_call | solution.py:640
  11.9 0.0 collective-permute-done.side_ref
  11.9 0.6 %shard_map.81 = (f32[1040,128]{1,0:T(8,128)S(1)}, f32[1040,128]{1,0:T(8,128)S(1)}, f32[80,128]{1,0:T(8,128)S(1)}) custom-call(f32[2048,128]{1,0:T(8,128)S(1)} %get-tuple-element.32.inner_ref, f32[64,128]{1,0:T(8,128)S(1)} %collective-permute-done.side_ref, f32[8,128]{1,0:T(8,128)S(1)} %get-tuple-element.33.mask_ref, f32[64,128]{1,0:T(8,128)S(1)} %get-tuple-element.34.packed_ref), custom_call_target="tpu_custom_call" | custom-call | tf_op jit(solution)/shard_map/pallas_call | solution.py:640
  12.5 0.0 collective-permute-done.2.first_in_ref
  12.5 0.3 shard_map.82
  12.8 0.7 %collective-permute-start.4 = (f32[536,128]{1,0:T(8,128)S(1)}, f32[536,128]{1,0:T(8,128)S(1)}, u32[]{:S(2)}, u32[]{:S(2)}) collective-permute-start(f32[536,128]{1,0:T(8,128)S(1)} %get-tuple-element.46), channel_id=1, source_target_pairs={{2,4},{4,2},{6,8},{8,6},{10,12},{12,10},{14,16},{16,14},{18,20},{2... | collective-permute-start | bytes 823304 | tf_op jit(solution)/shard_map/ppermute | solution.py:660
  13.5 4.4 %collective-permute-start.5 = (f32[536,128]{1,0:T(8,128)S(1)}, f32[536,128]{1,0:T(8,128)S(1)}, u32[]{:S(2)}, u32[]{:S(2)}) collective-permute-start(f32[536,128]{1,0:T(8,128)S(1)} %get-tuple-element.47), channel_id=1, source_target_pairs={{0,2},{2,0},{4,6},{6,4},{8,10},{10,8},{12,14},{14,12},{16,18},{18,... | collective-permute-start | bytes 823304 | tf_op jit(solution)/shard_map/ppermute | solution.py:661
  17.9 0.6 %shard_map.84 = f32[64,128]{1,0:T(8,128)S(1)} custom-call(f32[1040,128]{1,0:T(8,128)S(1)} %get-tuple-element.35.middle_ref, f32[1040,128]{1,0:T(8,128)S(1)} %get-tuple-element.41.outer_ref), custom_call_target="tpu_custom_call" | custom-call | tf_op jit(solution)/shard_map/pallas_call | solution.py:640
  18.5 1.6 %collective-permute-start.3 = (f32[64,128]{1,0:T(8,128)S(1)}, f32[64,128]{1,0:T(8,128)S(1)}, u32[]{:S(2)}, u32[]{:S(2)}) collective-permute-start(f32[64,128]{1,0:T(8,128)S(1)} %shard_map.84), channel_id=1, source_target_pairs={{0,1},{1,0},{2,3},{3,2},{4,5},{5,4},{6,7},{7,6},{8,9},{9,8},{10,11... | collective-permute-start | bytes 98312 | tf_op jit(solution)/shard_map/ppermute | solution.py:667
  20.0 1.8 %shard_map.83.inner_ref = f32[2048,128]{1,0:T(8,128)S(1)} custom-call(f32[1040,128]{1,0:T(8,128)S(1)} %get-tuple-element.35.middle_ref, f32[1040,128]{1,0:T(8,128)S(1)} %get-tuple-element.41.outer_ref, f32[2048,128]{1,0:T(8,128)S(1)} %bitcast.8, f32[240,128]{1,0:T(8,128)S(1)} %get-tuple-element.31.coef_ref), custom_call_target="tpu_custom_call" | custom-call | tf_op jit(solution)/shard_map/pallas_call | solution.py:640
  21.8 0.6 %collective-permute-done.3.side_ref = f32[64,128]{1,0:T(8,128)S(1)} collective-permute-done((f32[64,128]{1,0:T(8,128)S(1)}, f32[64,128]{1,0:T(8,128)S(1)}, u32[]{:S(2)}, u32[]{:S(2)}) %collective-permute-start.3) | collective-permute-done | bytes 32800 | tf_op jit(solution)/shard_map/ppermute | solution.py:667
  22.5 0.5 %shard_map.85 = (f32[1040,128]{1,0:T(8,128)S(1)}, f32[1040,128]{1,0:T(8,128)S(1)}, f32[32,128]{1,0:T(8,128)S(1)}, f32[64,128]{1,0:T(8,128)S(1)}) custom-call(f32[2048,128]{1,0:T(8,128)S(1)} %shard_map.83.inner_ref, f32[64,128]{1,0:T(8,128)S(1)} %collective-permute-done.3.side_ref, f32[8,128]{1,0:T(8,128)S(1)} %get-tuple-element.33.mask_ref, ...), custom_call_target="tpu_custom_call" | custom-call | tf_op jit(solution)/shard_map/pallas_call | solution.py:640
  23.0 0.0 collective-permute-done.4.second_in_ref
  23.0 0.0 collective-permute-done.5.first_in_ref
  23.0 0.6 %shard_map.86 = (f32[1040,128]{1,0:T(8,128)S(1)}, f32[8,128]{1,0:T(8,128)S(1)}, f32[32,1,128]{2,1,0:T(1,128)S(1)}) custom-call(s32[32,128]{1,0:T(8,128)S(1)} %select_select_fusion.place_ref, f32[1040,128]{1,0:T(8,128)S(1)} %get-tuple-element.42.loose_ref, f32[32,128]{1,0:T(8,128)S(1)} %get-tuple-element.44.middle_sums_ref, ...), custom_call_target="tpu_custom_call" | custom-call | tf_op jit(solution)/shard_map/pallas_call | solution.py:640
  23.6 13.0 %all_to_all.5 = f32[32,1,128]{2,1,0:T(1,128)S(1)} all-to-all(f32[32,1,128]{2,1,0:T(1,128)S(1)} %get-tuple-element.51), channel_id=1, replica_groups=mesh['roll'=16,'trans'=2] {'roll','trans'}, dimensions={0} | all-to-all | bytes 32768 | tf_op jit(solution)/shard_map/all_to_all | solution.py:752
  36.6 1.3 %shard_map.87 = (f32[2048,128]{1,0:T(8,128)}, f32[8,128]{1,0:T(8,128)}) custom-call(s32[32,128]{1,0:T(8,128)S(1)} %select_select_fusion.place_ref, f32[1040,128]{1,0:T(8,128)S(1)} %get-tuple-element.42.loose_ref, f32[1040,128]{1,0:T(8,128)S(1)} %get-tuple-element.43.middle_ref, f32[1040,128]{1,0:T(8,128)S(1)} %get-tuple-element.49.early_ref, ...), custom_call_target="tpu_custom_call" | custom-call | tf_op jit(solution)/shard_map/pallas_call | solution.py:640
  (5 shorter events, 0.0 us)
Async XLA Ops:
  2.0 10.5 %collective-permute-start.1 = (f32[512,128]{1,0:T(8,128)S(1)}, f32[512,128]{1,0:T(8,128)S(1)}, u32[]{:S(2)}, u32[]{:S(2)}) collective-permute-start(f32[512,128]{1,0:T(8,128)S(1)} %get-tuple-element.39), channel_id=1, source_target_pairs={{2,4},{4,2},{6,8},{8,6},{10,12},{12,10},{14,16},{16,14},{18,20},{2... | collective-permute-start | bytes 786440 | tf_op jit(solution)/shard_map/ppermute | solution.py:660
  2.7 9.8 %collective-permute-start.2 = (f32[512,128]{1,0:T(8,128)S(1)}, f32[512,128]{1,0:T(8,128)S(1)}, u32[]{:S(2)}, u32[]{:S(2)}) collective-permute-start(f32[512,128]{1,0:T(8,128)S(1)} %get-tuple-element.40), channel_id=1, source_target_pairs={{0,2},{2,0},{4,6},{6,4},{8,10},{10,8},{12,14},{14,12},{16,18},{18,... | collective-permute-start | bytes 786440 | tf_op jit(solution)/shard_map/ppermute | solution.py:661
  7.1 3.0 %copy-start = (f32[4,2,32,8,128]{4,3,2,1,0:T(8,128)S(1)}, f32[4,2,32,8,128]{4,3,2,1,0:T(8,128)}, u32[]{:S(2)}) copy-start(f32[4,2,32,8,128]{4,3,2,1,0:T(8,128)} %param.7) | copy-start | bytes 3145732
  7.5 4.4 %collective-permute-start = (f32[64,128]{1,0:T(8,128)S(1)}, f32[64,128]{1,0:T(8,128)S(1)}, u32[]{:S(2)}, u32[]{:S(2)}) collective-permute-start(f32[64,128]{1,0:T(8,128)S(1)} %shard_map.80), channel_id=1, source_target_pairs={{0,1},{1,0},{2,3},{3,2},{4,5},{5,4},{6,7},{7,6},{8,9},{9,8},{10,11... | collective-permute-start | bytes 98312 | tf_op jit(solution)/shard_map/ppermute | solution.py:667
  12.8 10.2 %collective-permute-start.4 = (f32[536,128]{1,0:T(8,128)S(1)}, f32[536,128]{1,0:T(8,128)S(1)}, u32[]{:S(2)}, u32[]{:S(2)}) collective-permute-start(f32[536,128]{1,0:T(8,128)S(1)} %get-tuple-element.46), channel_id=1, source_target_pairs={{2,4},{4,2},{6,8},{8,6},{10,12},{12,10},{14,16},{16,14},{18,20},{2... | collective-permute-start | bytes 823304 | tf_op jit(solution)/shard_map/ppermute | solution.py:660
  13.5 9.5 %collective-permute-start.5 = (f32[536,128]{1,0:T(8,128)S(1)}, f32[536,128]{1,0:T(8,128)S(1)}, u32[]{:S(2)}, u32[]{:S(2)}) collective-permute-start(f32[536,128]{1,0:T(8,128)S(1)} %get-tuple-element.47), channel_id=1, source_target_pairs={{0,2},{2,0},{4,6},{6,4},{8,10},{10,8},{12,14},{14,12},{16,18},{18,... | collective-permute-start | bytes 823304 | tf_op jit(solution)/shard_map/ppermute | solution.py:661
  18.5 4.0 %collective-permute-start.3 = (f32[64,128]{1,0:T(8,128)S(1)}, f32[64,128]{1,0:T(8,128)S(1)}, u32[]{:S(2)}, u32[]{:S(2)}) collective-permute-start(f32[64,128]{1,0:T(8,128)S(1)} %shard_map.84), channel_id=1, source_target_pairs={{0,1},{1,0},{2,3},{3,2},{4,5},{5,4},{6,7},{7,6},{8,9},{9,8},{10,11... | collective-permute-start | bytes 98312 | tf_op jit(solution)/shard_map/ppermute | solution.py:667

commit v10 on v9

--- a/solution.py
+++ b/solution.py
@@ -579,12 +579,14 @@
     lines_ref,
     sems,
 ):
-    wall_ref[...] = scaled(cells, devices, trans, place_ref, grad_ref, sums_ref, lines_ref)
-    wall_copy = pltpu.make_async_copy(wall_ref, wall_out_ref, sems.at[2])
-    wall_copy.start()
     planes = 4 * cases * depth
-    half = planes * 4
-    copies = [pltpu.make_async_copy(state_ref.at[rows(i * half, half), :], out_ref.at[rows(i * half, half), :], sems.at[i]) for i in range(2)]
+    part = planes * 2
+
+    def copy(first, count, sem):
+        here = rows(first * part, count * part)
+        return pltpu.make_async_copy(state_ref.at[here, :], out_ref.at[here, :], sems.at[sem])
+
+    copies = [copy(2, 2, 0), copy(0, 1, 1), copy(1, 1, 2), pltpu.make_async_copy(wall_ref, wall_out_ref, sems.at[3])]
 
     def place_tiles(c, refs):
         def one(case, _):
@@ -599,9 +601,6 @@
         lax.fori_loop(0, cases, one, 0)
 
     both = (middle_ref, early_ref)
-    for c in range(2):
-        place_tiles(c, [both] * 8)
-    copies[0].start()
     for c in range(2, 4):
         place_tiles(c, [both if row in MIDDLE else None for row in range(8)])
 
@@ -611,10 +610,14 @@
 
     arrived = Post(place_ref, first_in_ref, second_in_ref)
     outer_rows(depth, cases, planes, (2, 3), loose_ref, arrived, coef_ref, store)
-    copies[1].start()
-    wall_copy.wait()
-    copies[0].wait()
-    copies[1].wait()
+    copies[0].start()
+    for c in range(2):
+        place_tiles(c, [both] * 8)
+        copies[1 + c].start()
+    wall_ref[...] = scaled(cells, devices, trans, place_ref, grad_ref, sums_ref, lines_ref)
+    copies[3].start()
+    for each in copies:
+        each.wait()
 
 
 def f32(*shape):
@@ -763,7 +766,7 @@
         grad,
         sums,
         outs=(pltpu.HBM(inner.shape, jnp.float32), pltpu.HBM((8, 128), jnp.float32)),
-        scratch=[inner.shape, (8, 128), (devices + 2 * pad, 128), pltpu.SemaphoreType.DMA((3,))],
+        scratch=[inner.shape, (8, 128), (devices + 2 * pad, 128), pltpu.SemaphoreType.DMA((4,))],
         out=HB,
     )
     return (state.reshape(adjoint.shape), wall_step)

time: 38.1 us -> 38 us (level)
  no operation moved by 1% of the time
where the time goes in v10:
time: 38 us; the launch traced here: 37.7 us
  starting transfers between devices  13.2 us (35%)
  blocking collectives  13 us (34%)
  Pallas kernels  10 us (26%)
  between operations  0.79 us (2%)
  waiting for transfers between devices  0.63 us (2%)
    all_to_all x1, blocking collectives, on_device(): lax.all_to_all(sums, ('roll', 'trans'), 0, 0, tiled=True)  13 us
    pallas_call x11, Pallas kernels, call(): pl.pallas_call(kernel, out_shape=outs, in_specs=specs, out_specs=tuple([o...  10 us
    ppermute x2, starting transfers between devices, exchange_rows(): return (lax.ppermute(first, 'roll', inner), second)  8.75 us
    ppermute x2, starting transfers between devices, exchange_columns(): return lax.ppermute(cols, 'trans', ahead + back)  3.11 us
    ppermute x2, starting transfers between devices, exchange_rows(): second = lax.ppermute(second, 'roll', outer)  1.35 us
  transfers between devices with their start and end apart: 6, of which 1 were waited for; matrix products, arithmetic and copies ran while one was open for 0% of the time, Pallas kernels for 18%

profile of v10, /device:TPU:0, one launch (start us, length us, event | category | flops | bytes accessed | tf_op | source)
XLA Modules:
  0.0 37.7 jit_solution(3631758013400421404)
XLA Ops:
  0.7 0.1 select_select_fusion.place_ref
  0.8 1.2 %shard_map.77 = (f32[2048,128]{1,0:T(8,128)S(1)}, f32[512,128]{1,0:T(8,128)S(1)}, f32[512,128]{1,0:T(8,128)S(1)}) custom-call(s32[32,128]{1,0:T(8,128)S(1)} %select_select_fusion.place_ref, f32[2048,128]{1,0:T(8,128)} %bitcast.10), custom_call_target="tpu_custom_call" | custom-call | tf_op jit(solution)/shard_map/pallas_call | solution.py:643
  2.0 0.7 %collective-permute-start.1 = (f32[512,128]{1,0:T(8,128)S(1)}, f32[512,128]{1,0:T(8,128)S(1)}, u32[]{:S(2)}, u32[]{:S(2)}) collective-permute-start(f32[512,128]{1,0:T(8,128)S(1)} %get-tuple-element.39), channel_id=1, source_target_pairs={{2,4},{4,2},{6,8},{8,6},{10,12},{12,10},{14,16},{16,14},{18,20},{2... | collective-permute-start | bytes 786440 | tf_op jit(solution)/shard_map/ppermute | solution.py:663
  2.7 4.4 %collective-permute-start.2 = (f32[512,128]{1,0:T(8,128)S(1)}, f32[512,128]{1,0:T(8,128)S(1)}, u32[]{:S(2)}, u32[]{:S(2)}) collective-permute-start(f32[512,128]{1,0:T(8,128)S(1)} %get-tuple-element.40), channel_id=1, source_target_pairs={{0,2},{2,0},{4,6},{6,4},{8,10},{10,8},{12,14},{14,12},{16,18},{18,... | collective-permute-start | bytes 786440 | tf_op jit(solution)/shard_map/ppermute | solution.py:664
  7.1 0.4 %shard_map.80 = f32[64,128]{1,0:T(8,128)S(1)} custom-call(f32[2048,128]{1,0:T(8,128)S(1)} %get-tuple-element.28.state_ref), custom_call_target="tpu_custom_call" | custom-call | tf_op jit(solution)/shard_map/pallas_call | solution.py:643
  7.5 1.6 %collective-permute-start = (f32[64,128]{1,0:T(8,128)S(1)}, f32[64,128]{1,0:T(8,128)S(1)}, u32[]{:S(2)}, u32[]{:S(2)}) collective-permute-start(f32[64,128]{1,0:T(8,128)S(1)} %shard_map.80), channel_id=1, source_target_pairs={{0,1},{1,0},{2,3},{3,2},{4,5},{5,4},{6,7},{7,6},{8,9},{9,8},{10,11... | collective-permute-start | bytes 98312 | tf_op jit(solution)/shard_map/ppermute | solution.py:670
  9.0 1.0 %shard_map.78 = (f32[1040,128]{1,0:T(8,128)S(1)}, f32[1040,128]{1,0:T(8,128)S(1)}, f32[240,128]{1,0:T(8,128)S(1)}, f32[64,128]{1,0:T(8,128)S(1)}, f32[8,128]{1,0:T(8,128)S(1)}) custom-call(f32[2048,128]{1,0:T(8,128)S(1)} %get-tuple-element.28.state_ref, s32[32,128]{1,0:T(8,128)S(1)} %select_select_fusion.place_ref, s32[1,2]{1,0:T(1,128)} %bitcast.13, ...), custom_call_target="tpu_custom_call" | custom-call | tf_op jit(solution)/shard_map/pallas_call | solution.py:643
  10.1 1.8 %shard_map.79 = (f32[2048,128]{1,0:T(8,128)S(1)}, f32[16,128]{1,0:T(8,128)S(1)}) custom-call(f32[1040,128]{1,0:T(8,128)S(1)} %get-tuple-element.29.middle_ref, f32[1040,128]{1,0:T(8,128)S(1)} %get-tuple-element.30.outer_ref, f32[2048,128]{1,0:T(8,128)S(1)} %bitcast.7, f32[240,128]{1,0:T(8,128)S(1)} %get-tuple-element.31.coef_ref), custom_call_target="tpu_custom_call" | custom-call | tf_op jit(solution)/shard_map/pallas_call | solution.py:643
  11.9 0.0 collective-permute-done.side_ref
  11.9 0.6 %shard_map.81 = (f32[1040,128]{1,0:T(8,128)S(1)}, f32[1040,128]{1,0:T(8,128)S(1)}, f32[80,128]{1,0:T(8,128)S(1)}) custom-call(f32[2048,128]{1,0:T(8,128)S(1)} %get-tuple-element.32.inner_ref, f32[64,128]{1,0:T(8,128)S(1)} %collective-permute-done.side_ref, f32[8,128]{1,0:T(8,128)S(1)} %get-tuple-element.33.mask_ref, f32[64,128]{1,0:T(8,128)S(1)} %get-tuple-element.34.packed_ref), custom_call_target="tpu_custom_call" | custom-call | tf_op jit(solution)/shard_map/pallas_call | solution.py:643
  12.5 0.0 collective-permute-done.2.first_in_ref
  12.5 0.3 shard_map.82
  12.8 0.7 %collective-permute-start.4 = (f32[536,128]{1,0:T(8,128)S(1)}, f32[536,128]{1,0:T(8,128)S(1)}, u32[]{:S(2)}, u32[]{:S(2)}) collective-permute-start(f32[536,128]{1,0:T(8,128)S(1)} %get-tuple-element.46), channel_id=1, source_target_pairs={{2,4},{4,2},{6,8},{8,6},{10,12},{12,10},{14,16},{16,14},{18,20},{2... | collective-permute-start | bytes 823304 | tf_op jit(solution)/shard_map/ppermute | solution.py:663
  13.5 4.4 %collective-permute-start.5 = (f32[536,128]{1,0:T(8,128)S(1)}, f32[536,128]{1,0:T(8,128)S(1)}, u32[]{:S(2)}, u32[]{:S(2)}) collective-permute-start(f32[536,128]{1,0:T(8,128)S(1)} %get-tuple-element.47), channel_id=1, source_target_pairs={{0,2},{2,0},{4,6},{6,4},{8,10},{10,8},{12,14},{14,12},{16,18},{18,... | collective-permute-start | bytes 823304 | tf_op jit(solution)/shard_map/ppermute | solution.py:664
  17.9 0.6 %shard_map.84 = f32[64,128]{1,0:T(8,128)S(1)} custom-call(f32[1040,128]{1,0:T(8,128)S(1)} %get-tuple-element.35.middle_ref, f32[1040,128]{1,0:T(8,128)S(1)} %get-tuple-element.41.outer_ref), custom_call_target="tpu_custom_call" | custom-call | tf_op jit(solution)/shard_map/pallas_call | solution.py:643
  18.5 1.6 %collective-permute-start.3 = (f32[64,128]{1,0:T(8,128)S(1)}, f32[64,128]{1,0:T(8,128)S(1)}, u32[]{:S(2)}, u32[]{:S(2)}) collective-permute-start(f32[64,128]{1,0:T(8,128)S(1)} %shard_map.84), channel_id=1, source_target_pairs={{0,1},{1,0},{2,3},{3,2},{4,5},{5,4},{6,7},{7,6},{8,9},{9,8},{10,11... | collective-permute-start | bytes 98312 | tf_op jit(solution)/shard_map/ppermute | solution.py:670
  20.0 1.8 %shard_map.83.inner_ref = f32[2048,128]{1,0:T(8,128)S(1)} custom-call(f32[1040,128]{1,0:T(8,128)S(1)} %get-tuple-element.35.middle_ref, f32[1040,128]{1,0:T(8,128)S(1)} %get-tuple-element.41.outer_ref, f32[2048,128]{1,0:T(8,128)S(1)} %bitcast.8, f32[240,128]{1,0:T(8,128)S(1)} %get-tuple-element.31.coef_ref), custom_call_target="tpu_custom_call" | custom-call | tf_op jit(solution)/shard_map/pallas_call | solution.py:643
  21.8 0.6 %collective-permute-done.3.side_ref = f32[64,128]{1,0:T(8,128)S(1)} collective-permute-done((f32[64,128]{1,0:T(8,128)S(1)}, f32[64,128]{1,0:T(8,128)S(1)}, u32[]{:S(2)}, u32[]{:S(2)}) %collective-permute-start.3) | collective-permute-done | bytes 32800 | tf_op jit(solution)/shard_map/ppermute | solution.py:670
  22.5 0.5 %shard_map.85 = (f32[1040,128]{1,0:T(8,128)S(1)}, f32[1040,128]{1,0:T(8,128)S(1)}, f32[32,128]{1,0:T(8,128)S(1)}, f32[64,128]{1,0:T(8,128)S(1)}) custom-call(f32[2048,128]{1,0:T(8,128)S(1)} %shard_map.83.inner_ref, f32[64,128]{1,0:T(8,128)S(1)} %collective-permute-done.3.side_ref, f32[8,128]{1,0:T(8,128)S(1)} %get-tuple-element.33.mask_ref, ...), custom_call_target="tpu_custom_call" | custom-call | tf_op jit(solution)/shard_map/pallas_call | solution.py:643
  23.0 0.0 collective-permute-done.4.second_in_ref
  23.0 0.0 collective-permute-done.5.first_in_ref
  23.0 0.6 %shard_map.86 = (f32[1040,128]{1,0:T(8,128)S(1)}, f32[8,128]{1,0:T(8,128)S(1)}, f32[32,1,128]{2,1,0:T(1,128)S(1)}) custom-call(s32[32,128]{1,0:T(8,128)S(1)} %select_select_fusion.place_ref, f32[1040,128]{1,0:T(8,128)S(1)} %get-tuple-element.42.loose_ref, f32[32,128]{1,0:T(8,128)S(1)} %get-tuple-element.44.middle_sums_ref, ...), custom_call_target="tpu_custom_call" | custom-call | tf_op jit(solution)/shard_map/pallas_call | solution.py:643
  23.6 13.0 %all_to_all.5 = f32[32,1,128]{2,1,0:T(1,128)S(1)} all-to-all(f32[32,1,128]{2,1,0:T(1,128)S(1)} %get-tuple-element.51), channel_id=1, replica_groups=mesh['roll'=16,'trans'=2] {'roll','trans'}, dimensions={0} | all-to-all | bytes 32768 | tf_op jit(solution)/shard_map/all_to_all | solution.py:755
  36.6 1.1 %shard_map.87 = (f32[2048,128]{1,0:T(8,128)}, f32[8,128]{1,0:T(8,128)}) custom-call(s32[32,128]{1,0:T(8,128)S(1)} %select_select_fusion.place_ref, f32[1040,128]{1,0:T(8,128)S(1)} %get-tuple-element.42.loose_ref, f32[1040,128]{1,0:T(8,128)S(1)} %get-tuple-element.43.middle_ref, f32[1040,128]{1,0:T(8,128)S(1)} %get-tuple-element.49.early_ref, ...), custom_call_target="tpu_custom_call" | custom-call | tf_op jit(solution)/shard_map/pallas_call | solution.py:643
  (5 shorter events, 0.0 us)
Async XLA Ops:
  2.0 10.5 %collective-permute-start.1 = (f32[512,128]{1,0:T(8,128)S(1)}, f32[512,128]{1,0:T(8,128)S(1)}, u32[]{:S(2)}, u32[]{:S(2)}) collective-permute-start(f32[512,128]{1,0:T(8,128)S(1)} %get-tuple-element.39), channel_id=1, source_target_pairs={{2,4},{4,2},{6,8},{8,6},{10,12},{12,10},{14,16},{16,14},{18,20},{2... | collective-permute-start | bytes 786440 | tf_op jit(solution)/shard_map/ppermute | solution.py:663
  2.7 9.8 %collective-permute-start.2 = (f32[512,128]{1,0:T(8,128)S(1)}, f32[512,128]{1,0:T(8,128)S(1)}, u32[]{:S(2)}, u32[]{:S(2)}) collective-permute-start(f32[512,128]{1,0:T(8,128)S(1)} %get-tuple-element.40), channel_id=1, source_target_pairs={{0,2},{2,0},{4,6},{6,4},{8,10},{10,8},{12,14},{14,12},{16,18},{18,... | collective-permute-start | bytes 786440 | tf_op jit(solution)/shard_map/ppermute | solution.py:664
  7.1 3.0 %copy-start = (f32[4,2,32,8,128]{4,3,2,1,0:T(8,128)S(1)}, f32[4,2,32,8,128]{4,3,2,1,0:T(8,128)}, u32[]{:S(2)}) copy-start(f32[4,2,32,8,128]{4,3,2,1,0:T(8,128)} %param.7) | copy-start | bytes 3145732
  7.5 4.4 %collective-permute-start = (f32[64,128]{1,0:T(8,128)S(1)}, f32[64,128]{1,0:T(8,128)S(1)}, u32[]{:S(2)}, u32[]{:S(2)}) collective-permute-start(f32[64,128]{1,0:T(8,128)S(1)} %shard_map.80), channel_id=1, source_target_pairs={{0,1},{1,0},{2,3},{3,2},{4,5},{5,4},{6,7},{7,6},{8,9},{9,8},{10,11... | collective-permute-start | bytes 98312 | tf_op jit(solution)/shard_map/ppermute | solution.py:670
  12.8 10.2 %collective-permute-start.4 = (f32[536,128]{1,0:T(8,128)S(1)}, f32[536,128]{1,0:T(8,128)S(1)}, u32[]{:S(2)}, u32[]{:S(2)}) collective-permute-start(f32[536,128]{1,0:T(8,128)S(1)} %get-tuple-element.46), channel_id=1, source_target_pairs={{2,4},{4,2},{6,8},{8,6},{10,12},{12,10},{14,16},{16,14},{18,20},{2... | collective-permute-start | bytes 823304 | tf_op jit(solution)/shard_map/ppermute | solution.py:663
  13.5 9.5 %collective-permute-start.5 = (f32[536,128]{1,0:T(8,128)S(1)}, f32[536,128]{1,0:T(8,128)S(1)}, u32[]{:S(2)}, u32[]{:S(2)}) collective-permute-start(f32[536,128]{1,0:T(8,128)S(1)} %get-tuple-element.47), channel_id=1, source_target_pairs={{0,2},{2,0},{4,6},{6,4},{8,10},{10,8},{12,14},{14,12},{16,18},{18,... | collective-permute-start | bytes 823304 | tf_op jit(solution)/shard_map/ppermute | solution.py:664
  18.5 4.0 %collective-permute-start.3 = (f32[64,128]{1,0:T(8,128)S(1)}, f32[64,128]{1,0:T(8,128)S(1)}, u32[]{:S(2)}, u32[]{:S(2)}) collective-permute-start(f32[64,128]{1,0:T(8,128)S(1)} %shard_map.84), channel_id=1, source_target_pairs={{0,1},{1,0},{2,3},{3,2},{4,5},{5,4},{6,7},{7,6},{8,9},{9,8},{10,11... | collective-permute-start | bytes 98312 | tf_op jit(solution)/shard_map/ppermute | solution.py:670

commit v11 on v10

--- a/solution.py
+++ b/solution.py
@@ -360,7 +360,7 @@
                     ref[rows(place + offset), :] = value
         return 0
 
-    lax.fori_loop(0, cases, one, 0)
+    lax.fori_loop(0, cases, one, 0, unroll=True)
     line_sums(depth, cases, planes, sums, middle_ref, MIDDLE, sums_ref, layer)
 
 
@@ -398,7 +398,7 @@
                 store(c, case, block, offsets[c], whole[c])
         return 0
 
-    lax.fori_loop(0, cases, one, 0)
+    lax.fori_loop(0, cases, one, 0, unroll=True)
 
 
 def joined_kernel(

time: 38 us -> 37.9 us (level)
  transfers between devices with their start and end apart: 6 -> 6, of which waited for: 1 -> 1; matrix products, arithmetic and copies ran while one was open for 0% -> 0% of each run, Pallas kernels for 18% -> 17%
where the time goes in v11:
time: 37.9 us; the launch traced here: 37.7 us
  starting transfers between devices  13.3 us (35%)
  blocking collectives  13.1 us (35%)
  Pallas kernels  9.75 us (26%)
  between operations  0.79 us (2%)
  waiting for transfers between devices  0.63 us (2%)
    all_to_all x1, blocking collectives, on_device(): lax.all_to_all(sums, ('roll', 'trans'), 0, 0, tiled=True)  13.1 us
    pallas_call x11, Pallas kernels, call(): pl.pallas_call(kernel, out_shape=outs, in_specs=specs, out_specs=tuple([o...  9.75 us
    ppermute x2, starting transfers between devices, exchange_rows(): return (lax.ppermute(first, 'roll', inner), second)  8.88 us
    ppermute x2, starting transfers between devices, exchange_columns(): return lax.ppermute(cols, 'trans', ahead + back)  3.11 us
    ppermute x2, starting transfers between devices, exchange_rows(): second = lax.ppermute(second, 'roll', outer)  1.36 us
  transfers between devices with their start and end apart: 6, of which 1 were waited for; matrix products, arithmetic and copies ran while one was open for 0% of the time, Pallas kernels for 17%

profile of v11, /device:TPU:0, one launch (start us, length us, event | category | flops | bytes accessed | tf_op | source)
XLA Modules:
  0.0 37.7 jit_solution(10122667259270679675)
XLA Ops:
  0.7 0.1 select_select_fusion.place_ref
  0.8 1.2 %shard_map.77 = (f32[2048,128]{1,0:T(8,128)S(1)}, f32[512,128]{1,0:T(8,128)S(1)}, f32[512,128]{1,0:T(8,128)S(1)}) custom-call(s32[32,128]{1,0:T(8,128)S(1)} %select_select_fusion.place_ref, f32[2048,128]{1,0:T(8,128)} %bitcast.10), custom_call_target="tpu_custom_call" | custom-call | tf_op jit(solution)/shard_map/pallas_call | solution.py:643
  2.0 0.7 %collective-permute-start.1 = (f32[512,128]{1,0:T(8,128)S(1)}, f32[512,128]{1,0:T(8,128)S(1)}, u32[]{:S(2)}, u32[]{:S(2)}) collective-permute-start(f32[512,128]{1,0:T(8,128)S(1)} %get-tuple-element.39), channel_id=1, source_target_pairs={{2,4},{4,2},{6,8},{8,6},{10,12},{12,10},{14,16},{16,14},{18,20},{2... | collective-permute-start | bytes 786440 | tf_op jit(solution)/shard_map/ppermute | solution.py:663
  2.7 4.4 %collective-permute-start.2 = (f32[512,128]{1,0:T(8,128)S(1)}, f32[512,128]{1,0:T(8,128)S(1)}, u32[]{:S(2)}, u32[]{:S(2)}) collective-permute-start(f32[512,128]{1,0:T(8,128)S(1)} %get-tuple-element.40), channel_id=1, source_target_pairs={{0,2},{2,0},{4,6},{6,4},{8,10},{10,8},{12,14},{14,12},{16,18},{18,... | collective-permute-start | bytes 786440 | tf_op jit(solution)/shard_map/ppermute | solution.py:664
  7.1 0.4 %shard_map.80 = f32[64,128]{1,0:T(8,128)S(1)} custom-call(f32[2048,128]{1,0:T(8,128)S(1)} %get-tuple-element.28.state_ref), custom_call_target="tpu_custom_call" | custom-call | tf_op jit(solution)/shard_map/pallas_call | solution.py:643
  7.5 1.6 %collective-permute-start = (f32[64,128]{1,0:T(8,128)S(1)}, f32[64,128]{1,0:T(8,128)S(1)}, u32[]{:S(2)}, u32[]{:S(2)}) collective-permute-start(f32[64,128]{1,0:T(8,128)S(1)} %shard_map.80), channel_id=1, source_target_pairs={{0,1},{1,0},{2,3},{3,2},{4,5},{5,4},{6,7},{7,6},{8,9},{9,8},{10,11... | collective-permute-start | bytes 98312 | tf_op jit(solution)/shard_map/ppermute | solution.py:670
  9.0 1.0 %shard_map.78 = (f32[1040,128]{1,0:T(8,128)S(1)}, f32[1040,128]{1,0:T(8,128)S(1)}, f32[240,128]{1,0:T(8,128)S(1)}, f32[64,128]{1,0:T(8,128)S(1)}, f32[8,128]{1,0:T(8,128)S(1)}) custom-call(f32[2048,128]{1,0:T(8,128)S(1)} %get-tuple-element.28.state_ref, s32[32,128]{1,0:T(8,128)S(1)} %select_select_fusion.place_ref, s32[1,2]{1,0:T(1,128)} %bitcast.13, ...), custom_call_target="tpu_custom_call" | custom-call | tf_op jit(solution)/shard_map/pallas_call | solution.py:643
  10.1 1.8 %shard_map.79 = (f32[2048,128]{1,0:T(8,128)S(1)}, f32[16,128]{1,0:T(8,128)S(1)}) custom-call(f32[1040,128]{1,0:T(8,128)S(1)} %get-tuple-element.29.middle_ref, f32[1040,128]{1,0:T(8,128)S(1)} %get-tuple-element.30.outer_ref, f32[2048,128]{1,0:T(8,128)S(1)} %bitcast.7, f32[240,128]{1,0:T(8,128)S(1)} %get-tuple-element.31.coef_ref), custom_call_target="tpu_custom_call" | custom-call | tf_op jit(solution)/shard_map/pallas_call | solution.py:643
  11.9 0.0 collective-permute-done.side_ref
  11.9 0.4 %shard_map.81 = (f32[1040,128]{1,0:T(8,128)S(1)}, f32[1040,128]{1,0:T(8,128)S(1)}, f32[80,128]{1,0:T(8,128)S(1)}) custom-call(f32[2048,128]{1,0:T(8,128)S(1)} %get-tuple-element.32.inner_ref, f32[64,128]{1,0:T(8,128)S(1)} %collective-permute-done.side_ref, f32[8,128]{1,0:T(8,128)S(1)} %get-tuple-element.33.mask_ref, f32[64,128]{1,0:T(8,128)S(1)} %get-tuple-element.34.packed_ref), custom_call_target="tpu_custom_call" | custom-call | tf_op jit(solution)/shard_map/pallas_call | solution.py:643
  12.4 0.0 collective-permute-done.1.second_in_ref
  12.4 0.0 collective-permute-done.2.first_in_ref
  12.4 0.3 shard_map.82
  12.7 0.7 %collective-permute-start.4 = (f32[536,128]{1,0:T(8,128)S(1)}, f32[536,128]{1,0:T(8,128)S(1)}, u32[]{:S(2)}, u32[]{:S(2)}) collective-permute-start(f32[536,128]{1,0:T(8,128)S(1)} %get-tuple-element.46), channel_id=1, source_target_pairs={{2,4},{4,2},{6,8},{8,6},{10,12},{12,10},{14,16},{16,14},{18,20},{2... | collective-permute-start | bytes 823304 | tf_op jit(solution)/shard_map/ppermute | solution.py:663
  13.4 4.5 %collective-permute-start.5 = (f32[536,128]{1,0:T(8,128)S(1)}, f32[536,128]{1,0:T(8,128)S(1)}, u32[]{:S(2)}, u32[]{:S(2)}) collective-permute-start(f32[536,128]{1,0:T(8,128)S(1)} %get-tuple-element.47), channel_id=1, source_target_pairs={{0,2},{2,0},{4,6},{6,4},{8,10},{10,8},{12,14},{14,12},{16,18},{18,... | collective-permute-start | bytes 823304 | tf_op jit(solution)/shard_map/ppermute | solution.py:664
  17.9 0.6 %shard_map.84 = f32[64,128]{1,0:T(8,128)S(1)} custom-call(f32[1040,128]{1,0:T(8,128)S(1)} %get-tuple-element.35.middle_ref, f32[1040,128]{1,0:T(8,128)S(1)} %get-tuple-element.41.outer_ref), custom_call_target="tpu_custom_call" | custom-call | tf_op jit(solution)/shard_map/pallas_call | solution.py:643
  18.5 1.6 %collective-permute-start.3 = (f32[64,128]{1,0:T(8,128)S(1)}, f32[64,128]{1,0:T(8,128)S(1)}, u32[]{:S(2)}, u32[]{:S(2)}) collective-permute-start(f32[64,128]{1,0:T(8,128)S(1)} %shard_map.84), channel_id=1, source_target_pairs={{0,1},{1,0},{2,3},{3,2},{4,5},{5,4},{6,7},{7,6},{8,9},{9,8},{10,11... | collective-permute-start | bytes 98312 | tf_op jit(solution)/shard_map/ppermute | solution.py:670
  20.0 1.8 %shard_map.83.inner_ref = f32[2048,128]{1,0:T(8,128)S(1)} custom-call(f32[1040,128]{1,0:T(8,128)S(1)} %get-tuple-element.35.middle_ref, f32[1040,128]{1,0:T(8,128)S(1)} %get-tuple-element.41.outer_ref, f32[2048,128]{1,0:T(8,128)S(1)} %bitcast.8, f32[240,128]{1,0:T(8,128)S(1)} %get-tuple-element.31.coef_ref), custom_call_target="tpu_custom_call" | custom-call | tf_op jit(solution)/shard_map/pallas_call | solution.py:643
  21.8 0.6 %collective-permute-done.3.side_ref = f32[64,128]{1,0:T(8,128)S(1)} collective-permute-done((f32[64,128]{1,0:T(8,128)S(1)}, f32[64,128]{1,0:T(8,128)S(1)}, u32[]{:S(2)}, u32[]{:S(2)}) %collective-permute-start.3) | collective-permute-done | bytes 32800 | tf_op jit(solution)/shard_map/ppermute | solution.py:670
  22.4 0.4 %shard_map.85 = (f32[1040,128]{1,0:T(8,128)S(1)}, f32[1040,128]{1,0:T(8,128)S(1)}, f32[32,128]{1,0:T(8,128)S(1)}, f32[64,128]{1,0:T(8,128)S(1)}) custom-call(f32[2048,128]{1,0:T(8,128)S(1)} %shard_map.83.inner_ref, f32[64,128]{1,0:T(8,128)S(1)} %collective-permute-done.3.side_ref, f32[8,128]{1,0:T(8,128)S(1)} %get-tuple-element.33.mask_ref, ...), custom_call_target="tpu_custom_call" | custom-call | tf_op jit(solution)/shard_map/pallas_call | solution.py:643
  22.9 0.0 collective-permute-done.4.second_in_ref
  22.9 0.6 %shard_map.86 = (f32[1040,128]{1,0:T(8,128)S(1)}, f32[8,128]{1,0:T(8,128)S(1)}, f32[32,1,128]{2,1,0:T(1,128)S(1)}) custom-call(s32[32,128]{1,0:T(8,128)S(1)} %select_select_fusion.place_ref, f32[1040,128]{1,0:T(8,128)S(1)} %get-tuple-element.42.loose_ref, f32[32,128]{1,0:T(8,128)S(1)} %get-tuple-element.44.middle_sums_ref, ...), custom_call_target="tpu_custom_call" | custom-call | tf_op jit(solution)/shard_map/pallas_call | solution.py:643
  23.5 13.1 %all_to_all.5 = f32[32,1,128]{2,1,0:T(1,128)S(1)} all-to-all(f32[32,1,128]{2,1,0:T(1,128)S(1)} %get-tuple-element.51), channel_id=1, replica_groups=mesh['roll'=16,'trans'=2] {'roll','trans'}, dimensions={0} | all-to-all | bytes 32768 | tf_op jit(solution)/shard_map/all_to_all | solution.py:755
  36.6 1.1 %shard_map.87 = (f32[2048,128]{1,0:T(8,128)}, f32[8,128]{1,0:T(8,128)}) custom-call(s32[32,128]{1,0:T(8,128)S(1)} %select_select_fusion.place_ref, f32[1040,128]{1,0:T(8,128)S(1)} %get-tuple-element.42.loose_ref, f32[1040,128]{1,0:T(8,128)S(1)} %get-tuple-element.43.middle_ref, f32[1040,128]{1,0:T(8,128)S(1)} %get-tuple-element.49.early_ref, ...), custom_call_target="tpu_custom_call" | custom-call | tf_op jit(solution)/shard_map/pallas_call | solution.py:643
  (5 shorter events, 0.0 us)
Async XLA Ops:
  2.0 10.4 %collective-permute-start.1 = (f32[512,128]{1,0:T(8,128)S(1)}, f32[512,128]{1,0:T(8,128)S(1)}, u32[]{:S(2)}, u32[]{:S(2)}) collective-permute-start(f32[512,128]{1,0:T(8,128)S(1)} %get-tuple-element.39), channel_id=1, source_target_pairs={{2,4},{4,2},{6,8},{8,6},{10,12},{12,10},{14,16},{16,14},{18,20},{2... | collective-permute-start | bytes 786440 | tf_op jit(solution)/shard_map/ppermute | solution.py:663
  2.7 9.7 %collective-permute-start.2 = (f32[512,128]{1,0:T(8,128)S(1)}, f32[512,128]{1,0:T(8,128)S(1)}, u32[]{:S(2)}, u32[]{:S(2)}) collective-permute-start(f32[512,128]{1,0:T(8,128)S(1)} %get-tuple-element.40), channel_id=1, source_target_pairs={{0,2},{2,0},{4,6},{6,4},{8,10},{10,8},{12,14},{14,12},{16,18},{18,... | collective-permute-start | bytes 786440 | tf_op jit(solution)/shard_map/ppermute | solution.py:664
  7.1 3.0 %copy-start = (f32[4,2,32,8,128]{4,3,2,1,0:T(8,128)S(1)}, f32[4,2,32,8,128]{4,3,2,1,0:T(8,128)}, u32[]{:S(2)}) copy-start(f32[4,2,32,8,128]{4,3,2,1,0:T(8,128)} %param.7) | copy-start | bytes 3145732
  7.5 4.4 %collective-permute-start = (f32[64,128]{1,0:T(8,128)S(1)}, f32[64,128]{1,0:T(8,128)S(1)}, u32[]{:S(2)}, u32[]{:S(2)}) collective-permute-start(f32[64,128]{1,0:T(8,128)S(1)} %shard_map.80), channel_id=1, source_target_pairs={{0,1},{1,0},{2,3},{3,2},{4,5},{5,4},{6,7},{7,6},{8,9},{9,8},{10,11... | collective-permute-start | bytes 98312 | tf_op jit(solution)/shard_map/ppermute | solution.py:670
  12.7 10.2 %collective-permute-start.4 = (f32[536,128]{1,0:T(8,128)S(1)}, f32[536,128]{1,0:T(8,128)S(1)}, u32[]{:S(2)}, u32[]{:S(2)}) collective-permute-start(f32[536,128]{1,0:T(8,128)S(1)} %get-tuple-element.46), channel_id=1, source_target_pairs={{2,4},{4,2},{6,8},{8,6},{10,12},{12,10},{14,16},{16,14},{18,20},{2... | collective-permute-start | bytes 823304 | tf_op jit(solution)/shard_map/ppermute | solution.py:663
  13.4 9.5 %collective-permute-start.5 = (f32[536,128]{1,0:T(8,128)S(1)}, f32[536,128]{1,0:T(8,128)S(1)}, u32[]{:S(2)}, u32[]{:S(2)}) collective-permute-start(f32[536,128]{1,0:T(8,128)S(1)} %get-tuple-element.47), channel_id=1, source_target_pairs={{0,2},{2,0},{4,6},{6,4},{8,10},{10,8},{12,14},{14,12},{16,18},{18,... | collective-permute-start | bytes 823304 | tf_op jit(solution)/shard_map/ppermute | solution.py:664
  18.5 4.0 %collective-permute-start.3 = (f32[64,128]{1,0:T(8,128)S(1)}, f32[64,128]{1,0:T(8,128)S(1)}, u32[]{:S(2)}, u32[]{:S(2)}) collective-permute-start(f32[64,128]{1,0:T(8,128)S(1)} %shard_map.84), channel_id=1, source_target_pairs={{0,1},{1,0},{2,3},{3,2},{4,5},{5,4},{6,7},{7,6},{8,9},{9,8},{10,11... | collective-permute-start | bytes 98312 | tf_op jit(solution)/shard_map/ppermute | solution.py:670

commit v12 on v11

--- a/solution.py
+++ b/solution.py
@@ -28,7 +28,7 @@
 CARRY, SOUND_STEP, STEP, HEAT, FLUX, BEND = range(9, 15)
 N_COEF = 15
 N_PACKED = 4
-PIECES = 4
+PIECES = 2
 TAIL = 24
 MIDDLE, OUTER = (2, 3, 4, 5), (0, 1, 6, 7)
 TRANS, TRANS_SIZE, ODD, DEVICE = range(4)
@@ -371,7 +371,7 @@
         for block in range(depth // 8):
             height = ((layer + 8 * block).astype(jnp.float32) + 0.5) / depth
             offsets = [pl.multiple_of((c * cases + case) * depth + 8 * block, 8) for c in range(4)]
-            near = {c: [post.get(rows(i * planes + offsets[c])) for i in range(2)] for c in {*parts, *range(2)}}
+            near = {c: [post.get(rows(i * planes + offsets[c])) for i in range(2)] for c in parts}
             whole = {c: {} for c in parts}
             for i, row in enumerate(OUTER):
 

time: 37.9 us -> 37.9 us (level)
  no operation moved by 1% of the time
where the time goes in v12:
time: 37.9 us; the launch traced here: 37.7 us
  starting transfers between devices  13.3 us (35%)
  blocking collectives  13.1 us (35%)
  Pallas kernels  9.77 us (26%)
  between operations  0.79 us (2%)
  waiting for transfers between devices  0.63 us (2%)
    all_to_all x1, blocking collectives, on_device(): lax.all_to_all(sums, ('roll', 'trans'), 0, 0, tiled=True)  13.1 us
    pallas_call x11, Pallas kernels, call(): pl.pallas_call(kernel, out_shape=outs, in_specs=specs, out_specs=tuple([o...  9.77 us
    ppermute x2, starting transfers between devices, exchange_rows(): return (lax.ppermute(first, 'roll', inner), second)  8.88 us
    ppermute x2, starting transfers between devices, exchange_columns(): return lax.ppermute(cols, 'trans', ahead + back)  3.11 us
    ppermute x2, starting transfers between devices, exchange_rows(): second = lax.ppermute(second, 'roll', outer)  1.36 us
  transfers between devices with their start and end apart: 6, of which 1 were waited for; matrix products, arithmetic and copies ran while one was open for 0% of the time, Pallas kernels for 17%

profile of v12, /device:TPU:0, one launch (start us, length us, event | category | flops | bytes accessed | tf_op | source)
XLA Modules:
  0.0 37.7 jit_solution(10267975182120594955)
XLA Ops:
  0.7 0.1 select_select_fusion.place_ref
  0.8 1.3 %shard_map.77 = (f32[2048,128]{1,0:T(8,128)S(1)}, f32[512,128]{1,0:T(8,128)S(1)}, f32[512,128]{1,0:T(8,128)S(1)}) custom-call(s32[32,128]{1,0:T(8,128)S(1)} %select_select_fusion.place_ref, f32[2048,128]{1,0:T(8,128)} %bitcast.10), custom_call_target="tpu_custom_call" | custom-call | tf_op jit(solution)/shard_map/pallas_call | solution.py:643
  2.0 0.7 %collective-permute-start.1 = (f32[512,128]{1,0:T(8,128)S(1)}, f32[512,128]{1,0:T(8,128)S(1)}, u32[]{:S(2)}, u32[]{:S(2)}) collective-permute-start(f32[512,128]{1,0:T(8,128)S(1)} %get-tuple-element.39), channel_id=1, source_target_pairs={{2,4},{4,2},{6,8},{8,6},{10,12},{12,10},{14,16},{16,14},{18,20},{2... | collective-permute-start | bytes 786440 | tf_op jit(solution)/shard_map/ppermute | solution.py:663
  2.7 4.4 %collective-permute-start.2 = (f32[512,128]{1,0:T(8,128)S(1)}, f32[512,128]{1,0:T(8,128)S(1)}, u32[]{:S(2)}, u32[]{:S(2)}) collective-permute-start(f32[512,128]{1,0:T(8,128)S(1)} %get-tuple-element.40), channel_id=1, source_target_pairs={{0,2},{2,0},{4,6},{6,4},{8,10},{10,8},{12,14},{14,12},{16,18},{18,... | collective-permute-start | bytes 786440 | tf_op jit(solution)/shard_map/ppermute | solution.py:664
  7.1 0.4 %shard_map.80 = f32[64,128]{1,0:T(8,128)S(1)} custom-call(f32[2048,128]{1,0:T(8,128)S(1)} %get-tuple-element.28.state_ref), custom_call_target="tpu_custom_call" | custom-call | tf_op jit(solution)/shard_map/pallas_call | solution.py:643
  7.5 1.6 %collective-permute-start = (f32[64,128]{1,0:T(8,128)S(1)}, f32[64,128]{1,0:T(8,128)S(1)}, u32[]{:S(2)}, u32[]{:S(2)}) collective-permute-start(f32[64,128]{1,0:T(8,128)S(1)} %shard_map.80), channel_id=1, source_target_pairs={{0,1},{1,0},{2,3},{3,2},{4,5},{5,4},{6,7},{7,6},{8,9},{9,8},{10,11... | collective-permute-start | bytes 98312 | tf_op jit(solution)/shard_map/ppermute | solution.py:670
  9.1 1.0 %shard_map.78 = (f32[1040,128]{1,0:T(8,128)S(1)}, f32[1040,128]{1,0:T(8,128)S(1)}, f32[240,128]{1,0:T(8,128)S(1)}, f32[64,128]{1,0:T(8,128)S(1)}, f32[8,128]{1,0:T(8,128)S(1)}) custom-call(f32[2048,128]{1,0:T(8,128)S(1)} %get-tuple-element.28.state_ref, s32[32,128]{1,0:T(8,128)S(1)} %select_select_fusion.place_ref, s32[1,2]{1,0:T(1,128)} %bitcast.13, ...), custom_call_target="tpu_custom_call" | custom-call | tf_op jit(solution)/shard_map/pallas_call | solution.py:643
  10.1 1.8 %shard_map.79 = (f32[2048,128]{1,0:T(8,128)S(1)}, f32[16,128]{1,0:T(8,128)S(1)}) custom-call(f32[1040,128]{1,0:T(8,128)S(1)} %get-tuple-element.29.middle_ref, f32[1040,128]{1,0:T(8,128)S(1)} %get-tuple-element.30.outer_ref, f32[2048,128]{1,0:T(8,128)S(1)} %bitcast.7, f32[240,128]{1,0:T(8,128)S(1)} %get-tuple-element.31.coef_ref), custom_call_target="tpu_custom_call" | custom-call | tf_op jit(solution)/shard_map/pallas_call | solution.py:643
  11.9 0.0 collective-permute-done.side_ref
  12.0 0.4 %shard_map.81 = (f32[1040,128]{1,0:T(8,128)S(1)}, f32[1040,128]{1,0:T(8,128)S(1)}, f32[80,128]{1,0:T(8,128)S(1)}) custom-call(f32[2048,128]{1,0:T(8,128)S(1)} %get-tuple-element.32.inner_ref, f32[64,128]{1,0:T(8,128)S(1)} %collective-permute-done.side_ref, f32[8,128]{1,0:T(8,128)S(1)} %get-tuple-element.33.mask_ref, f32[64,128]{1,0:T(8,128)S(1)} %get-tuple-element.34.packed_ref), custom_call_target="tpu_custom_call" | custom-call | tf_op jit(solution)/shard_map/pallas_call | solution.py:643
  12.4 0.0 collective-permute-done.1.second_in_ref
  12.4 0.0 collective-permute-done.2.first_in_ref
  12.4 0.3 shard_map.82
  12.7 0.7 %collective-permute-start.4 = (f32[536,128]{1,0:T(8,128)S(1)}, f32[536,128]{1,0:T(8,128)S(1)}, u32[]{:S(2)}, u32[]{:S(2)}) collective-permute-start(f32[536,128]{1,0:T(8,128)S(1)} %get-tuple-element.46), channel_id=1, source_target_pairs={{2,4},{4,2},{6,8},{8,6},{10,12},{12,10},{14,16},{16,14},{18,20},{2... | collective-permute-start | bytes 823304 | tf_op jit(solution)/shard_map/ppermute | solution.py:663
  13.4 4.5 %collective-permute-start.5 = (f32[536,128]{1,0:T(8,128)S(1)}, f32[536,128]{1,0:T(8,128)S(1)}, u32[]{:S(2)}, u32[]{:S(2)}) collective-permute-start(f32[536,128]{1,0:T(8,128)S(1)} %get-tuple-element.47), channel_id=1, source_target_pairs={{0,2},{2,0},{4,6},{6,4},{8,10},{10,8},{12,14},{14,12},{16,18},{18,... | collective-permute-start | bytes 823304 | tf_op jit(solution)/shard_map/ppermute | solution.py:664
  17.9 0.6 %shard_map.84 = f32[64,128]{1,0:T(8,128)S(1)} custom-call(f32[1040,128]{1,0:T(8,128)S(1)} %get-tuple-element.35.middle_ref, f32[1040,128]{1,0:T(8,128)S(1)} %get-tuple-element.41.outer_ref), custom_call_target="tpu_custom_call" | custom-call | tf_op jit(solution)/shard_map/pallas_call | solution.py:643
  18.5 1.6 %collective-permute-start.3 = (f32[64,128]{1,0:T(8,128)S(1)}, f32[64,128]{1,0:T(8,128)S(1)}, u32[]{:S(2)}, u32[]{:S(2)}) collective-permute-start(f32[64,128]{1,0:T(8,128)S(1)} %shard_map.84), channel_id=1, source_target_pairs={{0,1},{1,0},{2,3},{3,2},{4,5},{5,4},{6,7},{7,6},{8,9},{9,8},{10,11... | collective-permute-start | bytes 98312 | tf_op jit(solution)/shard_map/ppermute | solution.py:670
  20.0 1.8 %shard_map.83.inner_ref = f32[2048,128]{1,0:T(8,128)S(1)} custom-call(f32[1040,128]{1,0:T(8,128)S(1)} %get-tuple-element.35.middle_ref, f32[1040,128]{1,0:T(8,128)S(1)} %get-tuple-element.41.outer_ref, f32[2048,128]{1,0:T(8,128)S(1)} %bitcast.8, f32[240,128]{1,0:T(8,128)S(1)} %get-tuple-element.31.coef_ref), custom_call_target="tpu_custom_call" | custom-call | tf_op jit(solution)/shard_map/pallas_call | solution.py:643
  21.8 0.6 %collective-permute-done.3.side_ref = f32[64,128]{1,0:T(8,128)S(1)} collective-permute-done((f32[64,128]{1,0:T(8,128)S(1)}, f32[64,128]{1,0:T(8,128)S(1)}, u32[]{:S(2)}, u32[]{:S(2)}) %collective-permute-start.3) | collective-permute-done | bytes 32800 | tf_op jit(solution)/shard_map/ppermute | solution.py:670
  22.5 0.4 %shard_map.85 = (f32[1040,128]{1,0:T(8,128)S(1)}, f32[1040,128]{1,0:T(8,128)S(1)}, f32[32,128]{1,0:T(8,128)S(1)}, f32[64,128]{1,0:T(8,128)S(1)}) custom-call(f32[2048,128]{1,0:T(8,128)S(1)} %shard_map.83.inner_ref, f32[64,128]{1,0:T(8,128)S(1)} %collective-permute-done.3.side_ref, f32[8,128]{1,0:T(8,128)S(1)} %get-tuple-element.33.mask_ref, ...), custom_call_target="tpu_custom_call" | custom-call | tf_op jit(solution)/shard_map/pallas_call | solution.py:643
  22.9 0.0 collective-permute-done.4.second_in_ref
  22.9 0.6 %shard_map.86 = (f32[1040,128]{1,0:T(8,128)S(1)}, f32[8,128]{1,0:T(8,128)S(1)}, f32[32,1,128]{2,1,0:T(1,128)S(1)}) custom-call(s32[32,128]{1,0:T(8,128)S(1)} %select_select_fusion.place_ref, f32[1040,128]{1,0:T(8,128)S(1)} %get-tuple-element.42.loose_ref, f32[32,128]{1,0:T(8,128)S(1)} %get-tuple-element.44.middle_sums_ref, ...), custom_call_target="tpu_custom_call" | custom-call | tf_op jit(solution)/shard_map/pallas_call | solution.py:643
  23.5 13.1 %all_to_all.5 = f32[32,1,128]{2,1,0:T(1,128)S(1)} all-to-all(f32[32,1,128]{2,1,0:T(1,128)S(1)} %get-tuple-element.51), channel_id=1, replica_groups=mesh['roll'=16,'trans'=2] {'roll','trans'}, dimensions={0} | all-to-all | bytes 32768 | tf_op jit(solution)/shard_map/all_to_all | solution.py:755
  36.6 1.1 %shard_map.87 = (f32[2048,128]{1,0:T(8,128)}, f32[8,128]{1,0:T(8,128)}) custom-call(s32[32,128]{1,0:T(8,128)S(1)} %select_select_fusion.place_ref, f32[1040,128]{1,0:T(8,128)S(1)} %get-tuple-element.42.loose_ref, f32[1040,128]{1,0:T(8,128)S(1)} %get-tuple-element.43.middle_ref, f32[1040,128]{1,0:T(8,128)S(1)} %get-tuple-element.49.early_ref, ...), custom_call_target="tpu_custom_call" | custom-call | tf_op jit(solution)/shard_map/pallas_call | solution.py:643
  (5 shorter events, 0.0 us)
Async XLA Ops:
  2.0 10.4 %collective-permute-start.1 = (f32[512,128]{1,0:T(8,128)S(1)}, f32[512,128]{1,0:T(8,128)S(1)}, u32[]{:S(2)}, u32[]{:S(2)}) collective-permute-start(f32[512,128]{1,0:T(8,128)S(1)} %get-tuple-element.39), channel_id=1, source_target_pairs={{2,4},{4,2},{6,8},{8,6},{10,12},{12,10},{14,16},{16,14},{18,20},{2... | collective-permute-start | bytes 786440 | tf_op jit(solution)/shard_map/ppermute | solution.py:663
  2.7 9.7 %collective-permute-start.2 = (f32[512,128]{1,0:T(8,128)S(1)}, f32[512,128]{1,0:T(8,128)S(1)}, u32[]{:S(2)}, u32[]{:S(2)}) collective-permute-start(f32[512,128]{1,0:T(8,128)S(1)} %get-tuple-element.40), channel_id=1, source_target_pairs={{0,2},{2,0},{4,6},{6,4},{8,10},{10,8},{12,14},{14,12},{16,18},{18,... | collective-permute-start | bytes 786440 | tf_op jit(solution)/shard_map/ppermute | solution.py:664
  7.1 3.0 %copy-start = (f32[4,2,32,8,128]{4,3,2,1,0:T(8,128)S(1)}, f32[4,2,32,8,128]{4,3,2,1,0:T(8,128)}, u32[]{:S(2)}) copy-start(f32[4,2,32,8,128]{4,3,2,1,0:T(8,128)} %param.7) | copy-start | bytes 3145732
  7.5 4.4 %collective-permute-start = (f32[64,128]{1,0:T(8,128)S(1)}, f32[64,128]{1,0:T(8,128)S(1)}, u32[]{:S(2)}, u32[]{:S(2)}) collective-permute-start(f32[64,128]{1,0:T(8,128)S(1)} %shard_map.80), channel_id=1, source_target_pairs={{0,1},{1,0},{2,3},{3,2},{4,5},{5,4},{6,7},{7,6},{8,9},{9,8},{10,11... | collective-permute-start | bytes 98312 | tf_op jit(solution)/shard_map/ppermute | solution.py:670
  12.7 10.2 %collective-permute-start.4 = (f32[536,128]{1,0:T(8,128)S(1)}, f32[536,128]{1,0:T(8,128)S(1)}, u32[]{:S(2)}, u32[]{:S(2)}) collective-permute-start(f32[536,128]{1,0:T(8,128)S(1)} %get-tuple-element.46), channel_id=1, source_target_pairs={{2,4},{4,2},{6,8},{8,6},{10,12},{12,10},{14,16},{16,14},{18,20},{2... | collective-permute-start | bytes 823304 | tf_op jit(solution)/shard_map/ppermute | solution.py:663
  13.4 9.5 %collective-permute-start.5 = (f32[536,128]{1,0:T(8,128)S(1)}, f32[536,128]{1,0:T(8,128)S(1)}, u32[]{:S(2)}, u32[]{:S(2)}) collective-permute-start(f32[536,128]{1,0:T(8,128)S(1)} %get-tuple-element.47), channel_id=1, source_target_pairs={{0,2},{2,0},{4,6},{6,4},{8,10},{10,8},{12,14},{14,12},{16,18},{18,... | collective-permute-start | bytes 823304 | tf_op jit(solution)/shard_map/ppermute | solution.py:664
  18.5 4.0 %collective-permute-start.3 = (f32[64,128]{1,0:T(8,128)S(1)}, f32[64,128]{1,0:T(8,128)S(1)}, u32[]{:S(2)}, u32[]{:S(2)}) collective-permute-start(f32[64,128]{1,0:T(8,128)S(1)} %shard_map.84), channel_id=1, source_target_pairs={{0,1},{1,0},{2,3},{3,2},{4,5},{5,4},{6,7},{7,6},{8,9},{9,8},{10,11... | collective-permute-start | bytes 98312 | tf_op jit(solution)/shard_map/ppermute | solution.py:670
